TPU v7x, 32 devices: a whole 2x2x4 slice. The times are simulated.
32 devices in a mesh: row: 8 (over y, x, core), col: 4 (over z).
Axes of the slice: x: 2, y: 2, z: 4, core: 2. Of those that a mesh axis runs over, the one named last changes fastest.
Arguments:
- vis: float32 [2, 262144], P(None, ('row', 'col')), may hold values from -6 to 6
- vis_pos: int32 [2, 262144], P(None, ('row', 'col')), may hold values from 0 to 199
- vis_w: int32 [262144], P(('row', 'col')), may hold values from 0 to 1023
- subgrid_tile: int32 [1024, 1], P(('row', 'col')), may hold values from 0 to 3; in each aligned block of 32 rows (0 to 31, 32 to 63, ...) at most 16 rows name the same one
- subgrid_group: int32 [1024, 1], P(('row', 'col')), may hold values from 0 to 3; in each aligned block of 32 rows (0 to 31, 32 to 63, ...) at most 12 rows name the same one
- subgrid_col: int32 [1024], P(('row', 'col')), may hold values from 0 to 2016
- grid_kernel: float32 [8, 8], replicated, may hold values from 0.1 to 1
- scale_kernels: float32 [2, 33], replicated, may hold values from -1 to 1
Outputs:
- scale_images: float32 [2, 8192, 8192], P(None, ('row', 'col'))
Inputs may be any that keep to these rules, and one draw needn't show every extreme that they name: `vis_pos`: row 0 counts along grid rows, row 1 along grid columns, in steps of 1/8 cell from the corner of the visibility's subgrid. `subgrid_tile`: among the subgrids of one device (aligned blocks of 32), at most 16 name the same column tile; in some blocks one tile is named exactly that often. `subgrid_group`: among the subgrids of one device (aligned blocks of 32), at most 12 name the same row group; in some blocks one group is named exactly that often.
All inputs are finite; a program needn't handle non-finite values.
Results may differ from a plain program's by a relative error of at most 0.0003.
Values sent between devices are 32-bit elements; how exact they have to be, the bound alone decides.
No kernel may reach another device: no remote copies, remote signals or barrier semaphores. Data moves between devices by JAX's collectives and lax.ppermute only.
A program may use at most 128 MiB of HBM per device.

v0:
```python
import math

import jax
import jax.numpy as jnp
from jax import lax
from jax.sharding import PartitionSpec as P

G = 8192
SUB = 32
SUP = 8
OVER = 8
VPS = 256
WSTEPS = 1024
KW = 33
NSCALE = 2


HIGHEST = lax.Precision.HIGHEST


def with_halo(array, sides, width):
    for axis, dim in sides:
        count, length = (lax.axis_size(axis), array.shape[dim])
        up = [(i, (i + 1) % count) for i in range(count - 1)]
        down = [(j, i) for i, j in up]
        last = lax.slice_in_dim(array, length - width, length, axis=dim)
        initial = lax.slice_in_dim(array, 0, width, axis=dim)
        before = lax.ppermute(last, axis, up)
        after = lax.ppermute(initial, axis, down)
        array = jnp.concatenate([before, array, after], axis=dim)
    return array


def kernel_taps(positions, grid_kernel):
    cell_index = positions // OVER
    fraction = positions % OVER
    onehot = (fraction[:, None] == jnp.arange(OVER, dtype=jnp.int32)[None, :]).astype(
        grid_kernel.dtype
    )
    values = jnp.dot(onehot, grid_kernel, precision=HIGHEST)
    offset = jnp.arange(SUB, dtype=jnp.int32)[None, :] - cell_index[:, None]
    result = jnp.zeros(offset.shape, grid_kernel.dtype)
    for tap_index in range(SUP):
        result = result + jnp.where(offset == tap_index, values[:, tap_index : tap_index + 1], 0.0)
    return result


def make_subgrids(vis_block, pos_block, phase_steps, grid_kernel, number):
    along_rows = kernel_taps(pos_block[0], grid_kernel).reshape(number, VPS, SUB)
    along_cols = kernel_taps(pos_block[1], grid_kernel).reshape(number, VPS, SUB)
    angles = phase_steps.astype(grid_kernel.dtype) * (2.0 * math.pi / WSTEPS)
    cosine = jnp.cos(angles)
    sine_part = jnp.sin(angles)
    rotated_real = vis_block[0] * cosine + vis_block[1] * sine_part
    rotated_imag = vis_block[1] * cosine - vis_block[0] * sine_part
    weighted_real = along_rows * rotated_real.reshape(number, VPS, 1)
    weighted_imag = along_rows * rotated_imag.reshape(number, VPS, 1)
    sub_real = jnp.einsum("sja,sjb->sab", weighted_real, along_cols, precision=HIGHEST)
    sub_imag = jnp.einsum("sja,sjb->sab", weighted_imag, along_cols, precision=HIGHEST)
    return (sub_real, sub_imag)


def dft_table(length):
    positions = jnp.arange(length, dtype=jnp.int32)
    product = positions[:, None] * positions[None, :] % length
    angles = product.astype(jnp.float32) * (2.0 * math.pi / length)
    return (jnp.cos(angles), jnp.sin(angles))


def transform_last(real_part, imag_part, real_only):
    length = real_part.shape[-1]
    factor_one = 2 ** ((length.bit_length() - 1) // 2)
    factor_two = length // factor_one
    leading = real_part.shape[:-1]
    real_part = real_part.reshape(leading + (factor_one, factor_two))
    imag_part = imag_part.reshape(leading + (factor_one, factor_two))
    cos_one, sin_one = dft_table(factor_one)
    section_real = jnp.einsum(
        "...ab,ak->...kb", real_part, cos_one, precision=HIGHEST
    ) - jnp.einsum("...ab,ak->...kb", imag_part, sin_one, precision=HIGHEST)
    section_imag = jnp.einsum(
        "...ab,ak->...kb", real_part, sin_one, precision=HIGHEST
    ) + jnp.einsum("...ab,ak->...kb", imag_part, cos_one, precision=HIGHEST)
    outer_index = (
        jnp.arange(factor_one, dtype=jnp.int32)[:, None]
        * jnp.arange(factor_two, dtype=jnp.int32)[None, :]
        % length
    )
    twiddle = outer_index.astype(jnp.float32) * (2.0 * math.pi / length)
    twiddle_cos = jnp.cos(twiddle)
    twiddle_sin = jnp.sin(twiddle)
    turned_real = section_real * twiddle_cos - section_imag * twiddle_sin
    turned_imag = section_real * twiddle_sin + section_imag * twiddle_cos
    cos_two, sin_two = dft_table(factor_two)
    result_real = jnp.einsum(
        "...kb,bq->...qk", turned_real, cos_two, precision=HIGHEST
    ) - jnp.einsum("...kb,bq->...qk", turned_imag, sin_two, precision=HIGHEST)
    result_real = result_real.reshape(leading + (length,))
    if real_only:
        return result_real
    result_imag = jnp.einsum(
        "...kb,bq->...qk", turned_real, sin_two, precision=HIGHEST
    ) + jnp.einsum("...kb,bq->...qk", turned_imag, cos_two, precision=HIGHEST)
    return (result_real, result_imag.reshape(leading + (length,)))


def band_matrix(kernel_row, height, columns):
    distance = (
        jnp.arange(height, dtype=jnp.int32)[:, None] - jnp.arange(columns, dtype=jnp.int32)[None, :]
    )
    matrix = jnp.zeros((height, columns), jnp.float32)
    for tap_index in range(KW):
        matrix = matrix + jnp.where(distance == tap_index, kernel_row[tap_index], 0.0)
    return matrix


def smooth_along_rows(field, kernel_row):
    height = field.shape[0]
    length = field.shape[1]
    halo_width = (KW - 1) // 2
    block_size = min(128, length)
    blocks = length // block_size
    padded = jnp.pad(field, ((0, 0), (halo_width, block_size - halo_width)))
    framed = padded.reshape(height, blocks + 1, block_size)
    windows = jnp.concatenate([framed[:, :-1, :], framed[:, 1:, : 2 * halo_width]], axis=2)
    matrix = band_matrix(kernel_row, block_size + 2 * halo_width, block_size)
    return jnp.einsum("rni,io->rno", windows, matrix, precision=HIGHEST).reshape(height, length)


def smooth_across(field, kernel_row):
    height = field.shape[0]
    inner_rows = height - (KW - 1)
    matrix = band_matrix(kernel_row, height, inner_rows)
    return jnp.einsum("ry,rx->xy", field, matrix, precision=HIGHEST)


def slot_numbers(bucket_keys, buckets, capacity):
    onehot = (bucket_keys[:, None] == jnp.arange(buckets, dtype=jnp.int32)[None, :]).astype(
        jnp.int32
    )
    before = jnp.cumsum(onehot, axis=0) - onehot
    rank_within = jnp.sum(before * onehot, axis=1)
    return bucket_keys * capacity + rank_within


def place_blocks(piece_real, piece_imag, owner, start, buckets, width):
    count = piece_real.shape[0]
    piece_rows = piece_real.shape[1] // SUB
    step = math.gcd(count, 32)
    turns = count // step
    piece_real = piece_real.reshape(turns, step, piece_rows, SUB)
    piece_imag = piece_imag.reshape(turns, step, piece_rows, SUB)
    owner = owner.reshape(turns, step)
    start = start.reshape(turns, step)
    column_index = jnp.arange(width, dtype=jnp.int32)
    sub_index = jnp.arange(SUB, dtype=jnp.int32)
    bucket_index = jnp.arange(buckets, dtype=jnp.int32)

    def add_block(carry, block):
        block_real, block_imag, block_owner, block_start = block
        shift = (
            column_index[None, None, :] == block_start[:, None, None] + sub_index[None, :, None]
        ).astype(jnp.float32)
        pick = (block_owner[:, None] == bucket_index[None, :]).astype(jnp.float32)
        moved_real = jnp.einsum("sab,sbc->sac", block_real, shift, precision=HIGHEST)
        moved_imag = jnp.einsum("sab,sbc->sac", block_imag, shift, precision=HIGHEST)
        total_real = carry[0] + jnp.einsum("sg,sac->gac", pick, moved_real, precision=HIGHEST)
        total_imag = carry[1] + jnp.einsum("sg,sac->gac", pick, moved_imag, precision=HIGHEST)
        return ((total_real, total_imag), None)

    empty = jnp.zeros((buckets, piece_rows, width), jnp.float32)
    (placed_real, placed_imag), unused = lax.scan(
        add_block, (empty, empty), (piece_real, piece_imag, owner, start)
    )
    return (placed_real, placed_imag)


def per_device(
    vis, vis_pos, vis_w, subgrid_tile, subgrid_group, subgrid_col, grid_kernel, scale_kernels
):
    row_devices = lax.axis_size("row")
    col_devices = lax.axis_size("col")
    band_rows = G // row_devices
    tile_width = G // col_devices
    group_rows = band_rows // col_devices
    pencil_cols = G // (row_devices * col_devices)
    piece_rows = min(group_rows, SUB)
    pieces = SUB // piece_rows
    subgrids_here = subgrid_col.shape[0]
    batch_size = min(16, subgrids_here)
    batches = subgrids_here // batch_size
    batch_vis = batch_size * VPS

    def grid_batch(step_index):
        start = step_index * batch_vis
        vis_block = lax.dynamic_slice_in_dim(vis, start, batch_vis, 1)
        pos_block = lax.dynamic_slice_in_dim(vis_pos, start, batch_vis, 1)
        phase_block = lax.dynamic_slice_in_dim(vis_w, start, batch_vis, 0)
        sub_real, sub_imag = make_subgrids(
            vis_block, pos_block, phase_block, grid_kernel, batch_size
        )
        return (sub_real.reshape(batch_size, SUB * SUB), sub_imag.reshape(batch_size, SUB * SUB))

    sub_real, sub_imag = lax.map(grid_batch, jnp.arange(batches, dtype=jnp.int32))
    sub_real = sub_real.reshape(subgrids_here, SUB * SUB)
    sub_imag = sub_imag.reshape(subgrids_here, SUB * SUB)
    tile_index = subgrid_tile[:, 0]
    groups = subgrid_group[:, 0]
    groups_used = col_devices - pieces + 1
    most_group = min(subgrids_here, 3 * ((subgrids_here + groups_used - 1) // groups_used) // 2)
    capacity = pieces * most_group
    owners = (groups[:, None] + jnp.arange(pieces, dtype=jnp.int32)[None, :]).reshape(-1)
    starts = jnp.broadcast_to(
        (tile_index * tile_width + subgrid_col)[:, None], (subgrids_here, pieces)
    ).reshape(-1)
    slot_index = slot_numbers(owners, col_devices, capacity)
    piece_real = sub_real.reshape(subgrids_here * pieces, piece_rows * SUB)
    piece_imag = sub_imag.reshape(subgrids_here * pieces, piece_rows * SUB)
    send_real = (
        jnp.zeros((col_devices * capacity, piece_rows * SUB), jnp.float32)
        .at[slot_index]
        .set(piece_real)
    )
    send_imag = (
        jnp.zeros((col_devices * capacity, piece_rows * SUB), jnp.float32)
        .at[slot_index]
        .set(piece_imag)
    )
    send_start = jnp.zeros((col_devices * capacity,), jnp.int32).at[slot_index].set(starts)
    recv_real, recv_imag, recv_start = (
        lax.all_to_all(send_real, "col", split_axis=0, concat_axis=0, tiled=True),
        lax.all_to_all(send_imag, "col", split_axis=0, concat_axis=0, tiled=True),
        lax.all_to_all(send_start, "col", split_axis=0, concat_axis=0, tiled=True),
    )
    placed_real, placed_imag = place_blocks(
        recv_real,
        recv_imag,
        recv_start // tile_width,
        recv_start % tile_width,
        col_devices,
        tile_width,
    )
    widen = ((0, group_rows - piece_rows), (0, 0))
    slab_real = jnp.pad(placed_real.transpose(1, 0, 2).reshape(piece_rows, G), widen)
    slab_imag = jnp.pad(placed_imag.transpose(1, 0, 2).reshape(piece_rows, G), widen)
    rows_real, rows_imag = transform_last(slab_real, slab_imag, False)
    cols_real, cols_imag = (
        lax.all_to_all(
            lax.all_to_all(rows_real, "row", split_axis=1, concat_axis=0, tiled=True),
            "col",
            split_axis=1,
            concat_axis=0,
            tiled=True,
        ),
        lax.all_to_all(
            lax.all_to_all(rows_imag, "row", split_axis=1, concat_axis=0, tiled=True),
            "col",
            split_axis=1,
            concat_axis=0,
            tiled=True,
        ),
    )

    def reorder(field):
        return (
            field.reshape(col_devices, row_devices, group_rows, pencil_cols)
            .transpose(3, 1, 0, 2)
            .reshape(pencil_cols, G)
        )

    image = transform_last(reorder(cols_real), reorder(cols_imag), True) * (1.0 / G)
    halo_width = (KW - 1) // 2
    results = []
    padded = with_halo(image, ((("row", "col"), 0),), halo_width)
    for scale_index in range(NSCALE):
        vertical = smooth_along_rows(padded, scale_kernels[scale_index])
        results.append(smooth_across(vertical, scale_kernels[scale_index]))
    return jnp.stack(results)


def solution(mesh):
    return jax.shard_map(
        per_device,
        mesh=mesh,
        in_specs=(
            P(None, ("row", "col")),
            P(None, ("row", "col")),
            P(("row", "col")),
            P(("row", "col"), None),
            P(("row", "col"), None),
            P(("row", "col")),
            P(),
            P(),
        ),
        out_specs=P(None, ("row", "col"), None),
        check_vma=False,
    )
```

profile of v0, /device:TPU:0, one launch (start us, length us, event | category | flops | bytes accessed | tf_op | source)
XLA Modules:
  0.0 1133.9 jit_solution(3298642147351475299)
XLA Ops:
  4.3 6.3 all-to-all-start
  10.6 22.4 %while.28 = (s32[]{:T(128)}, f32[2,16,1024]{2,1,0:T(8,128)S(1)}, f32[2,16,1024]{2,1,0:T(8,128)S(1)}, s32[2]{0:T(128)S(1)}, s32[2,8192]{1,0:T(2,128)}, /*index=5*...) while((s32[]{:T(128)}, f32[2,16,1024]{2,1,0:T(8,128)S(1)}, ...), condition=%wide.region_3.4_spmd, body=%wide.region_2.3_spmd.sunk | while | flops 120111112 | bytes 3130095 | solution.py:204
  41.1 6.8 all-to-all-done.1
  59.4 46.1 %while.29 = (s32[]{:T(128)}, f32[4,32,2048]{2,0,1:T(4,128)S(1)}, f32[4,32,2048]{2,0,1:T(4,128)S(1)}, s32[3,16]{1,0:T(4,128)S(1)}, f32[3,16,32,32]{3,2,1,0:T(8,12...) while((s32[]{:T(128)}, f32[4,32,2048]{2,0,1:T(4,128)S(1)}, ...), condition=%wide.region_8.9_spmd.clone, body=%wide.region_7.8_spmd.clone.sunk | while | flops 909116032 | bytes 21508668 | solution.py:172
  108.7 9.8 fusion.872
  118.5 9.9 fusion.866
  131.6 9.9 fusion.864
  141.4 19.5 %subtract_bitcast_fusion.2 = (f32[256,64,128]{2,1,0:T(8,128)}, f32[256,64,128]{2,1,0:T(8,128)}) fusion(f32[64,128]{1,0:T(8,128)S(1)} %get-tuple-element.359, f32[64,128]{1,0:T(8,128)S(1)} %get-tuple-element.360, f32[64,256,128]{2,0,1:T(8,128)} %fusion.864, f32[64,256,128]{2,0,1:T(8,128)} %fusion.872, f32[64,256,128]{2,0,1:T(8,128)} %fusion.866, ...), kind=kOutput, calls=%fused_computation.154 | convolution fusion | flops 1627447296 | bytes 50397184 | tf_op jit(solution)/shard_map/...ab,ak->...kb/dot_general | solution.py:78
  161.0 16.4 %fusion.96 = f32[128,256,64]{1,0,2:T(8,128)S(1)} fusion(f32[256,64,128]{2,1,0:T(8,128)} %get-tuple-element.288), kind=kOutput, calls=%fused_computation.157 | convolution fusion | flops 3221454848 | bytes 16777216 | tf_op jit(solution)/shard_map/...kb,bq->...qk/dot_general | solution.py:103
  177.4 17.9 %add_bitcast_fusion.1 = f32[256,128,64]{0,1,2:T(8,128)} fusion(f32[128,256,64]{1,0,2:T(8,128)S(1)} %fusion.96, f32[256,64,128]{2,1,0:T(8,128)S(1)} %copy-done.1), kind=kOutput, calls=%fused_computation.151 | convolution fusion | flops 3223552000 | bytes 25165824 | tf_op jit(solution)/shard_map/...kb,bq->...qk/dot_general | solution.py:101
  195.3 11.5 %copy.92 = f32[256,128,64]{0,2,1:T(8,128)} copy(f32[256,128,64]{0,1,2:T(8,128)} %add_bitcast_fusion.1) | data formatting | bytes 16777216 | tf_op jit(solution)/shard_map/add | solution.py:101
  211.8 16.0 %fusion.98 = f32[128,256,64]{1,0,2:T(8,128)S(1)} fusion(f32[256,64,128]{2,1,0:T(8,128)} %get-tuple-element.288), kind=kOutput, calls=%fused_computation.159 | convolution fusion | flops 3221454848 | bytes 16777216 | tf_op jit(solution)/shard_map/...kb,bq->...qk/dot_general | solution.py:97
  227.8 16.3 %subtract_bitcast_fusion.1 = f32[256,128,64]{0,1,2:T(8,128)S(1)} fusion(f32[128,256,64]{1,0,2:T(8,128)S(1)} %fusion.98, f32[256,64,128]{2,1,0:T(8,128)} %get-tuple-element.287), kind=kOutput, calls=%fused_computation.152 | convolution fusion | flops 3223552000 | bytes 25165824 | tf_op jit(solution)/shard_map/...kb,bq->...qk/dot_general | solution.py:95
  244.0 8.3 copy.86
  252.3 53.6 %all-to-all-done.5 = f32[256,8,1024]{0,2,1:T(8,128)} async-done(((f32[256,8,1024]{0,2,1:T(8,128)}), f32[256,8,1024]{0,2,1:T(8,128)}, u32[]{:S(2)}, u32[]{:S(2)}) %all-to-all-start.5) | async-done | bytes 8388640 | tf_op jit(solution)/shard_map/all_to_all | solution.py:256
  305.9 5.4 all-to-all-start.3
  311.2 11.5 %copy.93 = f32[8,256,1024]{1,0,2:T(8,128)} copy(f32[8,256,1024]{1,2,0:T(8,128)} %bitcast.61) | data formatting | bytes 16777216 | tf_op jit(solution)/shard_map/all_to_all | solution.py:256
  322.7 9.3 all_to_all.84
  332.0 73.3 %all-to-all-done.3 = f32[256,8,1024]{0,2,1:T(8,128)} async-done(((f32[256,8,1024]{0,2,1:T(8,128)}), f32[256,8,1024]{0,2,1:T(8,128)}, u32[]{:S(2)}, u32[]{:S(2)}) %all-to-all-start.3) | async-done | bytes 8388640 | tf_op jit(solution)/shard_map/all_to_all | solution.py:249
  405.3 5.7 all-to-all-start.6
  411.0 11.6 %copy.87 = f32[8,256,1024]{1,0,2:T(8,128)} copy(f32[8,256,1024]{1,2,0:T(8,128)} %bitcast.55) | data formatting | bytes 16777216 | tf_op jit(solution)/shard_map/all_to_all | solution.py:249
  422.6 9.3 all_to_all.78
  431.9 159.5 %all-to-all-done.6 = f32[2048,4,256]{0,2,1:T(8,128)} async-done(((f32[2048,4,256]{0,2,1:T(8,128)}), f32[2048,4,256]{0,2,1:T(8,128)}, u32[]{:S(2)}, u32[]{:S(2)}) %all-to-all-start.6) | async-done | bytes 8388640 | tf_op jit(solution)/shard_map/all_to_all | solution.py:255
  591.4 5.9 all-to-all-start.4
  597.3 8.7 copy.94
  606.0 10.5 copy.95
  616.4 10.3 reshape_reshape.7
  626.7 12.8 %fusion.868 = f32[64,256,128]{2,0,1:T(8,128)} fusion(f32[256,64,128]{2,1,0:T(8,128)} %reshape_reshape.7), kind=kOutput, calls=%fused_computation.802 | convolution fusion | flops 1610670080 | bytes 16777216 | tf_op jit(solution)/shard_map/...ab,ak->...kb/dot_general | solution.py:83
  639.5 9.8 fusion.862
  649.3 130.6 %all-to-all-done.4 = f32[2048,4,256]{0,2,1:T(8,128)} async-done(((f32[2048,4,256]{0,2,1:T(8,128)}), f32[2048,4,256]{0,2,1:T(8,128)}, u32[]{:S(2)}, u32[]{:S(2)}) %all-to-all-start.4) | async-done | bytes 8388640 | tf_op jit(solution)/shard_map/all_to_all | solution.py:248
  779.9 8.7 copy.88
  788.5 10.4 copy.89
  799.0 10.3 reshape_reshape.6
  809.2 12.3 %fusion.860 = f32[64,256,128]{2,0,1:T(8,128)} fusion(f32[256,64,128]{2,1,0:T(8,128)} %reshape_reshape.6), kind=kOutput, calls=%fused_computation.794 | convolution fusion | flops 1610670080 | bytes 16777216 | tf_op jit(solution)/shard_map/...ab,ak->...kb/dot_general | solution.py:81
  821.5 19.4 %subtract_bitcast_fusion = (f32[256,64,128]{2,1,0:T(8,128)}, f32[256,64,128]{2,1,0:T(8,128)}) fusion(f32[64,128]{1,0:T(8,128)S(1)} %get-tuple-element.359, f32[64,128]{1,0:T(8,128)S(1)} %get-tuple-element.360, f32[64,256,128]{2,0,1:T(8,128)} %fusion.860, f32[64,256,128]{2,0,1:T(8,128)} %fusion.868, f32[64,256,128]{2,0,1:T(8,128)} %fusion.862, ...), kind=kOutput, calls=%fused_computation.150 | convolution fusion | flops 1627447296 | bytes 50397184 | tf_op jit(solution)/shard_map/...ab,ak->...kb/dot_general | solution.py:78
  840.9 15.9 %fusion.92 = f32[128,256,64]{1,0,2:T(8,128)S(1)} fusion(f32[256,64,128]{2,1,0:T(8,128)} %get-tuple-element.286), kind=kOutput, calls=%fused_computation.144 | convolution fusion | flops 3221454848 | bytes 16777216 | tf_op jit(solution)/shard_map/...kb,bq->...qk/dot_general | solution.py:97
  856.9 16.9 %multiply_bitcast_fusion = f32[256,128,64]{0,1,2:T(8,128)S(1)} fusion(f32[128,256,64]{1,0,2:T(8,128)S(1)} %fusion.92, f32[256,64,128]{2,1,0:T(8,128)} %get-tuple-element.285), kind=kOutput, calls=%fused_computation.148 | convolution fusion | flops 3225649152 | bytes 25165824 | tf_op jit(solution)/shard_map/...kb,bq->...qk/dot_general | solution.py:95
  873.8 5.3 fusion.1103
  897.7 11.5 %copy.99 = f32[256,128,64]{0,2,1:T(8,128)} copy(f32[256,128,64]{0,1,2:T(8,128)} %copy-done) | data formatting | bytes 16777216 | tf_op jit(solution)/shard_map/mul | solution.py:271
  919.4 9.6 select_maximum_fusion
  934.1 10.6 slice.652
  944.7 11.7 %copy.105 = f32[288,64,128]{2,1,0:T(8,128)} copy(f32[288,64,128]{0,2,1:T(8,128)} %slice.652) | data formatting | bytes 18874368
  956.5 6.7 copy.106
  963.2 41.8 %fusion.86 = f32[288,64,128]{2,1,0:T(8,128)S(1)} fusion(f32[288,64,32]{2,1,0:T(8,128)} %copy.106, f32[288,64,128]{2,1,0:T(8,128)} %copy.105, f32[]{:T(128)} %bitcast.37, f32[]{:T(128)} %bitcast.36, f32[]{:T(128)} %bitcast.35, f32[]{:T(128)} %bitcast.34, f32[]{:T(128)} %bitcast.33, f32[]{:T(128)} %bitcast.32, f32[]{:T(128)} %bitcast.31, f32[]{:T(128)} %bitcast.30, ...), kind=kOutput, calls=%fused_computation.134 | convolution fusion | flops 4534824960 | bytes 21233796 | tf_op jit(solution)/shard_map/rni,io->rno/dot_general | solution.py:127
  1005.0 45.8 %convolution_bitcast_fusion.1 = f32[1,256,8192]{2,1,0:T(8,128)} fusion(f32[36,8,64,128]{3,2,1,0:T(8,128)S(1)} %bitcast.246, f32[]{:T(128)} %bitcast.37, f32[]{:T(128)} %bitcast.36, f32[]{:T(128)} %bitcast.35, f32[]{:T(128)} %bitcast.34, f32[]{:T(128)} %bitcast.33, f32[]{:T(128)} %bitcast.32, f32[]{:T(128)} %bitcast.31, f32[]{:T(128)} %bitcast.30, ...), kind=kOutput, calls=%fused_computation.139 | convolution fusion | flops 7255056384 | bytes 17825924 | tf_op jit(solution)/shard_map/ry,rx->xy/dot_general | solution.py:134
  1050.9 36.8 %fusion.85 = f32[288,64,128]{2,1,0:T(8,128)S(1)} fusion(f32[288,64,32]{2,1,0:T(8,128)S(1)} %bitcast.234, f32[288,64,128]{2,1,0:T(8,128)S(1)} %bitcast.236, f32[]{:T(128)} %bitcast.104, f32[]{:T(128)} %bitcast.103, f32[]{:T(128)} %bitcast.102, f32[]{:T(128)} %bitcast.101, f32[]{:T(128)} %bitcast.100, f32[]{:T(128)} %bitcast.99, f32[]{:T(128)} %bitcast.98, ...), kind=kOutput, calls=%fused_computation.133 | convolution fusion | flops 4534824960 | bytes 21233796 | tf_op jit(solution)/shard_map/rni,io->rno/dot_general | solution.py:127
  1087.7 39.7 %convolution_bitcast_fusion = f32[1,256,8192]{2,1,0:T(8,128)S(1)} fusion(f32[36,8,64,128]{3,2,1,0:T(8,128)S(1)} %bitcast.245, f32[]{:T(128)} %bitcast.104, f32[]{:T(128)} %bitcast.103, f32[]{:T(128)} %bitcast.102, f32[]{:T(128)} %bitcast.101, f32[]{:T(128)} %bitcast.100, f32[]{:T(128)} %bitcast.99, f32[]{:T(128)} %bitcast.98, f32[]{:T(128)} %bitcast.97, ...), kind=kOutput, calls=%fused_computation.138 | convolution fusion | flops 7255056384 | bytes 17825924 | tf_op jit(solution)/shard_map/ry,rx->xy/dot_general | solution.py:134
  1127.5 6.2 pad_maximum_fusion.1
  (171 shorter events, 135.2 us)
Async XLA Ops:
  4.3 30.3 %all-to-all-start = ((s32[4,12,1]{1,2,0:T(1,128)}), s32[4,12,1]{1,2,0:T(1,128)S(1)}, u32[]{:S(2)}, u32[]{:S(2)}) async-start(s32[4,12,1]{1,2,0:T(1,128)} %bitcast.44), calls=%async_computation | async-start | bytes 4096 | tf_op jit(solution)/shard_map/all_to_all | solution.py:233
  34.6 13.4 %all-to-all-start.1 = ((f32[4,12,1024]{2,1,0:T(8,128)}), f32[4,12,1024]{2,1,0:T(8,128)S(1)}, u32[]{:S(2)}, u32[]{:S(2)}) async-start(f32[4,12,1024]{2,1,0:T(8,128)} %all_to_all.71), calls=%async_computation.1 | async-start | bytes 524288 | tf_op jit(solution)/shard_map/all_to_all | solution.py:231
  48.0 10.3 all-to-all-start.2
  131.6 9.9 copy-start.3
  161.0 16.4 %copy-start.1 = (f32[256,64,128]{2,1,0:T(8,128)S(1)}, f32[256,64,128]{2,1,0:T(8,128)}, u32[]{:S(2)}) copy-start(f32[256,64,128]{2,1,0:T(8,128)} %get-tuple-element.287) | copy-start | bytes 25165828
  206.7 99.1 %all-to-all-start.5 = ((f32[256,8,1024]{0,2,1:T(8,128)}), f32[256,8,1024]{0,2,1:T(8,128)}, u32[]{:S(2)}, u32[]{:S(2)}) async-start(f32[256,8,1024]{0,2,1:T(8,128)} %bitcast.249), calls=%async_computation.5 | async-start | bytes 16777216 | tf_op jit(solution)/shard_map/all_to_all | solution.py:256
  305.9 99.4 %all-to-all-start.3 = ((f32[256,8,1024]{0,2,1:T(8,128)}), f32[256,8,1024]{0,2,1:T(8,128)}, u32[]{:S(2)}, u32[]{:S(2)}) async-start(f32[256,8,1024]{0,2,1:T(8,128)} %bitcast.248), calls=%async_computation.3 | async-start | bytes 16777216 | tf_op jit(solution)/shard_map/all_to_all | solution.py:249
  405.3 186.1 %all-to-all-start.6 = ((f32[2048,4,256]{0,2,1:T(8,128)}), f32[2048,4,256]{0,2,1:T(8,128)}, u32[]{:S(2)}, u32[]{:S(2)}) async-start(f32[2048,4,256]{0,2,1:T(8,128)} %all_to_all.84), calls=%async_computation.6 | async-start | bytes 16777216 | tf_op jit(solution)/shard_map/all_to_all | solution.py:255
  591.4 188.4 %all-to-all-start.4 = ((f32[2048,4,256]{0,2,1:T(8,128)}), f32[2048,4,256]{0,2,1:T(8,128)}, u32[]{:S(2)}, u32[]{:S(2)}) async-start(f32[2048,4,256]{0,2,1:T(8,128)} %all_to_all.78), calls=%async_computation.4 | async-start | bytes 16777216 | tf_op jit(solution)/shard_map/all_to_all | solution.py:248
  626.7 12.8 %copy-start.2 = (f32[256,64,128]{2,1,0:T(8,128)S(1)}, f32[256,64,128]{2,1,0:T(8,128)}, u32[]{:S(2)}) copy-start(f32[256,64,128]{2,1,0:T(8,128)} %reshape_reshape.7) | copy-start | bytes 25165828
  873.8 5.9 copy-start
  879.7 15.1 %copy-start.6 = (f32[2,33]{1,0:T(2,128)S(1)}, f32[2,33]{1,0:T(2,128)}, u32[]{:S(2)}) copy-start(f32[2,33]{1,0:T(2,128)} %param.19) | copy-start | bytes 796
  888.2 26.0 %collective-permute-start.1 = (f32[16,8192]{1,0:T(8,128)S(1)}, f32[16,8192]{1,0:T(8,128)S(1)}, u32[]{:S(2)}, u32[]{:S(2)}) collective-permute-start(f32[16,8192]{1,0:T(8,128)S(1)} %slice.598), channel_id=1, source_target_pairs={{1,0},{2,1},{3,2},{4,3},{5,4},{6,5},{7,6},{8,7},{9,8},{10,9},{11,1... | collective-permute-start | bytes 1572872 | tf_op jit(solution)/shard_map/ppermute | solution.py:29
  889.8 27.0 %collective-permute-start = (f32[16,8192]{1,0:T(8,128)S(1)}, f32[16,8192]{1,0:T(8,128)S(1)}, u32[]{:S(2)}, u32[]{:S(2)}) collective-permute-start(f32[16,8192]{1,0:T(8,128)S(1)} %slice.596), channel_id=1, source_target_pairs={{0,1},{1,2},{2,3},{3,4},{4,5},{5,6},{6,7},{7,8},{8,9},{9,10},{10,1... | collective-permute-start | bytes 1572872 | tf_op jit(solution)/shard_map/ppermute | solution.py:28
  929.0 4.8 copy-start.4
  963.2 87.6 %slice-start = ((s8[9437184]{0:T(1024)(128)(4,1)}), s8[4194304]{0:T(1024)(128)(4,1)S(1)}, s32[]{:S(2)}) async-start(s8[9437184]{0:T(1024)(128)(4,1)} %bitcast.233), calls=%async_computation.7 | async-start | bytes 8388608
  963.2 87.6 %slice-start.1 = ((s8[9437184]{0:T(1024)(128)(4,1)}), s8[4194304]{0:T(1024)(128)(4,1)S(1)}, s32[]{:S(2)}) async-start(s8[9437184]{0:T(1024)(128)(4,1)} %bitcast.233), calls=%async_computation.8 | async-start | bytes 8388608
  963.2 87.6 %slice-start.3 = ((s8[9437184]{0:T(1024)(128)(4,1)}), s8[4194304]{0:T(1024)(128)(4,1)S(1)}, s32[]{:S(2)}) async-start(s8[9437184]{0:T(1024)(128)(4,1)} %bitcast.235), calls=%async_computation.10 | async-start | bytes 8388608
  963.2 87.6 %slice-start.4 = ((s8[9437184]{0:T(1024)(128)(4,1)}), s8[4194304]{0:T(1024)(128)(4,1)S(1)}, s32[]{:S(2)}) async-start(s8[9437184]{0:T(1024)(128)(4,1)} %bitcast.235), calls=%async_computation.11 | async-start | bytes 8388608
  1005.0 45.8 %slice-start.2 = ((s8[9437184]{0:T(1024)(128)(4,1)}), s8[1048576]{0:T(1024)(128)(4,1)S(1)}, s32[]{:S(2)}) async-start(s8[9437184]{0:T(1024)(128)(4,1)} %bitcast.233), calls=%async_computation.9 | async-start | bytes 2097152
  1005.0 45.8 %slice-start.5 = ((s8[9437184]{0:T(1024)(128)(4,1)}), s8[1048576]{0:T(1024)(128)(4,1)S(1)}, s32[]{:S(2)}) async-start(s8[9437184]{0:T(1024)(128)(4,1)} %bitcast.235), calls=%async_computation.12 | async-start | bytes 2097152
  1087.7 39.8 %copy-start.5 = (f32[1,256,8192]{2,1,0:T(8,128)S(1)}, f32[1,256,8192]{2,1,0:T(8,128)}, u32[]{:S(2)}) copy-start(f32[1,256,8192]{2,1,0:T(8,128)} %convolution_bitcast_fusion.1) | copy-start | bytes 25165828
where the time goes:
time: 1140 us; the launch traced here: 1130 us
  waiting for transfers between devices  434 us (38%)
  matrix products  422 us (37%)
  local copies, waits for them, and re-layouts  210 us (18%)
  starting transfers between devices  43.1 us (4%)
  other arithmetic  21.5 us (2%)
    all_to_all x1, waiting for transfers between devices, per_device(): lax.all_to_all(lax.all_to_all(rows_imag, 'row', split_axis=1, concat_axis...  159 us
    all_to_all x1, waiting for transfers between devices, per_device(): lax.all_to_all(lax.all_to_all(rows_real, 'row', split_axis=1, concat_axis...  131 us
    dot_general x2, matrix products, smooth_across(): return jnp.einsum('ry,rx->xy', field, matrix, precision=HIGHEST)  85.5 us
    dot_general x2, matrix products, smooth_along_rows(): jnp.einsum('rni,io->rno', windows, matrix, precision=HIGHEST)  78.6 us
    all_to_all x1, waiting for transfers between devices, per_device(): lax.all_to_all(rows_real, 'row', split_axis=1, concat_axis=0, tiled=True)  73.3 us
    all_to_all x1, waiting for transfers between devices, per_device(): lax.all_to_all(rows_imag, 'row', split_axis=1, concat_axis=0, tiled=True)  53.6 us
    dot_general x2, matrix products, transform_last(): jnp.einsum('...ab,ak->...kb', real_part, cos_one, precision=HIGHEST)  38.9 us
    dot_general x2, matrix products, transform_last(): jnp.einsum('...kb,bq->...qk', turned_real, cos_two, precision=HIGHEST)  33.2 us
  transfers between devices with their start and end apart: 9, of which 7 were waited for; matrix products, arithmetic and copies ran while one was open for 14% of the time, Pallas kernels for 0%

commit v1 on v0

--- a/solution.py
+++ b/solution.py
@@ -2,7 +2,10 @@
 
 import jax
 import jax.numpy as jnp
+import numpy as np
 from jax import lax
+from jax.experimental import pallas as pl
+from jax.experimental.pallas import tpu as pltpu
 from jax.sharding import PartitionSpec as P
 
 G = 8192
@@ -13,9 +16,14 @@
 WSTEPS = 1024
 KW = 33
 NSCALE = 2
-
+HALO = (KW - 1) // 2
+RADIX = 8
+LANES = 128
 
 HIGHEST = lax.Precision.HIGHEST
+F32 = jnp.float32
+BF16 = jnp.bfloat16
+ROOT_HALF = math.sqrt(0.5)
 
 
 def with_halo(array, sides, width):
@@ -45,14 +53,20 @@
     return result
 
 
+def rotated_visibilities(vis_block, phase_steps):
+    angles = phase_steps.astype(vis_block.dtype) * (2.0 * math.pi / WSTEPS)
+    cosine = jnp.cos(angles)
+    sine_part = jnp.sin(angles)
+    return (
+        vis_block[0] * cosine + vis_block[1] * sine_part,
+        vis_block[1] * cosine - vis_block[0] * sine_part,
+    )
+
+
 def make_subgrids(vis_block, pos_block, phase_steps, grid_kernel, number):
     along_rows = kernel_taps(pos_block[0], grid_kernel).reshape(number, VPS, SUB)
     along_cols = kernel_taps(pos_block[1], grid_kernel).reshape(number, VPS, SUB)
-    angles = phase_steps.astype(grid_kernel.dtype) * (2.0 * math.pi / WSTEPS)
-    cosine = jnp.cos(angles)
-    sine_part = jnp.sin(angles)
-    rotated_real = vis_block[0] * cosine + vis_block[1] * sine_part
-    rotated_imag = vis_block[1] * cosine - vis_block[0] * sine_part
+    rotated_real, rotated_imag = rotated_visibilities(vis_block, phase_steps)
     weighted_real = along_rows * rotated_real.reshape(number, VPS, 1)
     weighted_imag = along_rows * rotated_imag.reshape(number, VPS, 1)
     sub_real = jnp.einsum("sja,sjb->sab", weighted_real, along_cols, precision=HIGHEST)
@@ -135,12 +149,10 @@
 
 
 def slot_numbers(bucket_keys, buckets, capacity):
-    onehot = (bucket_keys[:, None] == jnp.arange(buckets, dtype=jnp.int32)[None, :]).astype(
-        jnp.int32
-    )
-    before = jnp.cumsum(onehot, axis=0) - onehot
-    rank_within = jnp.sum(before * onehot, axis=1)
-    return bucket_keys * capacity + rank_within
+    count = bucket_keys.shape[0]
+    index = jnp.arange(count, dtype=jnp.int32)
+    same = (bucket_keys[:, None] == bucket_keys[None, :]) & (index[None, :] < index[:, None])
+    return bucket_keys * capacity + jnp.sum(same.astype(jnp.int32), axis=1)
 
 
 def place_blocks(piece_real, piece_imag, owner, start, buckets, width):
@@ -175,7 +187,7 @@
     return (placed_real, placed_imag)
 
 
-def per_device(
+def general_device(
     vis, vis_pos, vis_w, subgrid_tile, subgrid_group, subgrid_col, grid_kernel, scale_kernels
 ):
     row_devices = lax.axis_size("row")
@@ -278,9 +290,415 @@
     return jnp.stack(results)
 
 
+def split(value):
+    high = value.astype(BF16)
+    return high, (value - high.astype(F32)).astype(BF16)
+
+
+def split_outside(value):
+    high = lax.reduce_precision(value, 8, 7)
+    return high.astype(BF16), (value - high).astype(BF16)
+
+
+def split_table(table):
+    table = np.asarray(table, np.float64)
+    high = table.astype(BF16)
+    return high, (table - high.astype(np.float64)).astype(BF16)
+
+
+def turn(steps, length):
+    angle = 2.0 * np.pi * (np.asarray(steps, np.int64) % length) / length
+    return np.cos(angle), np.sin(angle)
+
+
+def dot(left, right, left_dim=1, right_dim=0):
+    return lax.dot_general(
+        left, right, (((left_dim,), (right_dim,)), ((), ())), preferred_element_type=F32
+    )
+
+
+def dot3(left_high, left_low, right_high, right_low, left_dim=1, right_dim=0):
+    return (
+        dot(left_high, right_high, left_dim, right_dim)
+        + dot(left_high, right_low, left_dim, right_dim)
+        + dot(left_low, right_high, left_dim, right_dim)
+    )
+
+
+def subgrid_kernel(pos_ref, rot_ref, taps_ref, out_ref):
+    span = 2 * VPS
+    table = taps_ref[...]
+
+    def taps(position):
+        step = position & (OVER - 1)
+        cell = position >> (OVER.bit_length() - 1)
+        values = jnp.zeros((SUP, span), F32)
+        for s in range(OVER):
+            values = jnp.where(step == s, table[:, s : s + 1], values)
+        offset = lax.broadcasted_iota(jnp.int32, (SUB, span), 0) - cell
+        result = jnp.zeros((SUB, span), F32)
+        for t in range(SUP):
+            result = jnp.where(offset == t, values[t : t + 1, :], result)
+        return result
+
+    first = lax.broadcasted_iota(jnp.int32, (SUB, LANES), 1) < LANES // 2
+
+    def pair(p, carry):
+        here = pl.ds(pl.multiple_of(p * span, span), span)
+        along_rows = taps(pos_ref[0:1, here])
+        along_cols = taps(pos_ref[1:2, here])
+        weighted = jnp.concatenate(
+            [along_rows * rot_ref[0:1, here], along_rows * rot_ref[1:2, here]], axis=0
+        )
+        weighted = jnp.concatenate(split(weighted), axis=0)
+        cols = jnp.concatenate(split(along_cols), axis=0)
+        sums = []
+        for s in range(2):
+            part = slice(s * VPS, (s + 1) * VPS)
+            product = dot(cols[:, part], weighted[:, part], 1, 1)
+            total = product[:SUB] + product[SUB:]
+            sums.append(total + pltpu.roll(total, LANES // 2, 1))
+        out_ref[pl.ds(pl.multiple_of(p * SUB, SUB), SUB), :] = jnp.where(first, sums[0], sums[1])
+        return carry
+
+    lax.fori_loop(0, out_ref.shape[0] // SUB, pair, 0)
+
+
+def radix_eight(real, imag):
+    def four(r, i):
+        a, b = (r[0] + r[2], i[0] + i[2])
+        c, d = (r[0] - r[2], i[0] - i[2])
+        e, f = (r[1] + r[3], i[1] + i[3])
+        g, h = (r[1] - r[3], i[1] - i[3])
+        return [(a + e, b + f), (c - h, d + g), (a - e, b - f), (c + h, d - g)]
+
+    low = four(
+        [real[n] + real[n + 4] for n in range(4)], [imag[n] + imag[n + 4] for n in range(4)]
+    )
+    dr = [real[n] - real[n + 4] for n in range(4)]
+    di = [imag[n] - imag[n + 4] for n in range(4)]
+    high = four(
+        [dr[0], (dr[1] - di[1]) * ROOT_HALF, -di[2], (dr[3] + di[3]) * -ROOT_HALF],
+        [di[0], (dr[1] + di[1]) * ROOT_HALF, dr[2], (dr[3] - di[3]) * ROOT_HALF],
+    )
+    return [(low, high)[c % 2][c // 2] for c in range(8)]
+
+
+def row_kernel(
+    info_ref, *refs, blocks, part, per_class
+):
+    xs = refs[:blocks]
+    turn_ref, high_ref, low_ref, out_ref, real_ref, imag_ref, uh_ref, ul_ref = refs[blocks:]
+    rows = real_ref.shape[0]
+    chunk = 256
+
+    def clear(n, carry):
+        here = pl.ds(pl.multiple_of(n * chunk, chunk), chunk)
+        real_ref[here, :] = jnp.zeros((chunk, LANES), F32)
+        imag_ref[here, :] = jnp.zeros((chunk, LANES), F32)
+        return carry
+
+    lax.fori_loop(0, rows // chunk, clear, 0)
+    owner = lax.broadcasted_iota(jnp.int32, (SUB, LANES), 1) // SUB
+    for b in range(blocks):
+        pairs = xs[b].shape[0] // SUB
+
+        def place(p, carry, b=b, pairs=pairs):
+            piece = xs[b][pl.ds(pl.multiple_of(p * SUB, SUB), SUB), :]
+            for s in range(2):
+                number = b * 2 * pairs + 2 * p + s
+                start = info_ref[0, number]
+                group = info_ref[1, number]
+                for dest, at in ((real_ref, 2 * s), (imag_ref, 2 * s + 1)):
+                    shift = (group * SUB + (LANES - at * SUB)) & (LANES - 1)
+                    moved = jnp.where(owner == group, pltpu.roll(piece, shift, 1), 0.0)
+                    dest[pl.ds(start, SUB), :] += moved
+            return carry
+
+        lax.fori_loop(0, pairs, place, 0)
+
+    step = 16
+
+    def classes(n, carry):
+        first = pl.multiple_of(n * step, step)
+        real = [real_ref[pl.ds(k * part + first, step), :] for k in range(RADIX)]
+        imag = [imag_ref[pl.ds(k * part + first, step), :] for k in range(RADIX)]
+        turns = turn_ref[pl.ds(first, step), :]
+        for c, (ur, ui) in enumerate(radix_eight(real, imag)):
+            cosine = turns[:, c : c + 1]
+            sine = turns[:, RADIX + c : RADIX + c + 1]
+            vr = ur * cosine - ui * sine
+            vi = ur * sine + ui * cosine
+            high, low = split(jnp.concatenate([vr, vi], axis=1))
+            uh_ref[c, pl.ds(first, step), :] = high
+            ul_ref[c, pl.ds(first, step), :] = low
+        return carry
+
+    lax.fori_loop(0, part // step, classes, 0)
+    dests = out_ref.shape[0]
+    half = dests * per_class
+    for c in range(RADIX):
+        total = dot3(high_ref[...], low_ref[...], uh_ref[c], ul_ref[c])
+        real = total[:half, :LANES] - total[half:, LANES:]
+        imag = total[:half, LANES:] + total[half:, :LANES]
+        for d in range(dests):
+            mine = slice(d * per_class, (d + 1) * per_class)
+            here = slice(c * per_class, (c + 1) * per_class)
+            out_ref[d, here, :LANES] = real[mine]
+            out_ref[d, here, LANES:] = imag[mine]
+
+
+def column_kernel(
+    rows_ref, bh_ref, bl_ref, hat_ref, eh_ref, el_ref, th_ref, tl_ref, fh_ref, fl_ref,
+    out_ref, qt_ref, qh_ref, ql_ref, corr_ref, v_ref, o_ref, sem,
+):
+    t = pl.program_id(0)
+    tiles = pl.num_programs(0)
+    bands = rows_ref.shape[0]
+    width = qh_ref.shape[1]
+    per_scale = width // NSCALE
+    keys = bands * LANES // RADIX
+
+    @pl.when(t == 0)
+    def prepare():
+        for i in range(bands):
+            high, low = split(rows_ref[i])
+            product = dot3(high, low, bh_ref[...], bl_ref[...], 0, 0)
+            for lane in range(width // LANES):
+                cols = slice(lane * LANES, (lane + 1) * LANES)
+                qt_ref[0, lane, i * LANES : (i + 1) * LANES, :] = product[:LANES, cols]
+                qt_ref[1, lane, i * LANES : (i + 1) * LANES, :] = product[LANES:, cols]
+        edge = jnp.zeros((width, LANES), F32)
+        for m in range(RADIX):
+            parts = []
+            for lane in range(width // LANES):
+                parts.append(
+                    jnp.concatenate(
+                        [
+                            qt_ref[ri, lane, pl.ds(m, keys, stride=RADIX), :].T
+                            for ri in range(2)
+                        ],
+                        axis=1,
+                    )
+                )
+            q = jnp.concatenate(parts, axis=0)
+            high, low = split(q)
+            edge = edge + dot3(high, low, eh_ref[m], el_ref[m])
+            for scale in range(NSCALE):
+                mine = slice(scale * per_scale, (scale + 1) * per_scale)
+                qr, qi = q[mine, :keys], q[mine, keys:]
+                kr = hat_ref[scale, 0, m : m + 1, :]
+                ki = hat_ref[scale, 1, m : m + 1, :]
+                high, low = split(
+                    jnp.concatenate([qr * kr - qi * ki, qr * ki + qi * kr], axis=1)
+                )
+                qh_ref[m, mine, :] = high
+                ql_ref[m, mine, :] = low
+        high, low = split(edge)
+        for scale in range(NSCALE):
+            mine = slice(scale * per_scale, (scale + 1) * per_scale)
+            corr_ref[mine, :] = dot3(high[mine], low[mine], th_ref[scale], tl_ref[scale])
+
+    for m in range(RADIX):
+        v_ref[m] = dot3(qh_ref[m], ql_ref[m], fh_ref[0, m], fl_ref[0, m])
+
+    slot = lax.rem(t, 2)
+
+    def copy(which, tile, at):
+        return pltpu.make_async_copy(
+            o_ref.at[which, at],
+            out_ref.at[:, pl.ds(pl.multiple_of((at * tiles + tile) * LANES, LANES), LANES)],
+            sem.at[which, at],
+        )
+
+    @pl.when(t >= 2)
+    def reuse():
+        for at in range(RADIX):
+            copy(slot, t - 2, at).wait()
+
+    step = 16
+    is_first = (t == 0).astype(F32)
+    is_last = (t == tiles - 1).astype(F32)
+
+    def combine(n, carry):
+        here = pl.ds(pl.multiple_of(n * step, step), step)
+        r = [v_ref[m, here, :LANES] for m in range(RADIX)]
+        i = [v_ref[m, here, LANES:] if m % 4 else None for m in range(RADIX)]
+        s0, s1, s2, s3 = (r[m] + r[m + 4] for m in range(4))
+        d0, d1, d3 = r[0] - r[4], r[1] - r[5], r[3] - r[7]
+        i1, i3 = i[1] + i[5], i[3] + i[7]
+        j1, j2, j3 = i[1] - i[5], i[2] - i[6], i[3] - i[7]
+        a, b, c, d = s0 + s2, s0 - s2, s1 + s3, i1 - i3
+        e, f = d0 - j2, d0 + j2
+        g = ((d1 - j1) - (d3 + j3)) * ROOT_HALF
+        h = ((d1 + j1) - (d3 - j3)) * ROOT_HALF
+        outs = [
+            a + c - is_first * corr_ref[here, :LANES],
+            e + g,
+            b - d,
+            f - h,
+            a - c,
+            e - g,
+            b + d,
+            f + h - is_last * corr_ref[here, LANES:],
+        ]
+        for at in range(RADIX):
+            o_ref[slot, at, here, :] = outs[at]
+        return carry
+
+    lax.fori_loop(0, width // step, combine, 0)
+    for at in range(RADIX):
+        copy(slot, t, at).start()
+
+    @pl.when(t == tiles - 1)
+    def finish():
+        for at in range(RADIX):
+            copy(1 - slot, t - 1, at).wait()
+            copy(slot, t, at).wait()
+
+
+def whole(shape):
+    return pl.BlockSpec(shape, lambda *_: (0,) * len(shape))
+
+
+def spread_taps(index, scale_kernels):
+    index = jnp.asarray(index, jnp.int32)[None]
+    out = jnp.zeros((NSCALE,) + index.shape[1:], F32)
+    for u in range(KW):
+        out = jnp.where(index == u, scale_kernels[:, u][:, None, None], out)
+    return out
+
+
+def kernel_device(
+    vis, vis_pos, vis_w, subgrid_tile, subgrid_group, subgrid_col, grid_kernel, scale_kernels
+):
+    nr = lax.axis_size("row")
+    nc = lax.axis_size("col")
+    row, col = lax.axis_index("row"), lax.axis_index("col")
+    tile_width = G // nc
+    stride = G // nr
+    cols_here = G // (nr * nc)
+    window = cols_here + 2 * HALO
+    per_class = window // RADIX
+    part = G // RADIX
+    subs = subgrid_col.shape[0]
+    width = NSCALE * cols_here
+
+    shifts = [[(i, (i + d) % nc) for i in range(nc)] for d in range(1, nc)]
+    info = jnp.stack([subgrid_tile[:, 0] * tile_width + subgrid_col, subgrid_group[:, 0]])
+    infos = jnp.concatenate([info] + [lax.ppermute(info, "col", s) for s in shifts], axis=1)
+
+    rotated = jnp.stack(rotated_visibilities(vis, vis_w))
+    subgrids = pl.pallas_call(
+        subgrid_kernel,
+        out_shape=jax.ShapeDtypeStruct((subs // 2 * SUB, LANES), F32),
+        compiler_params=pltpu.CompilerParams(vmem_limit_bytes=32 * 2**20),
+        name="subgrids",
+    )(vis_pos, rotated, grid_kernel.T)
+    blocks = [subgrids] + [lax.ppermute(subgrids, "col", s) for s in shifts]
+
+    inner = np.arange(part)
+    cosine, sine = turn(
+        (stride * np.arange(nr)[:, None] + RADIX * np.arange(per_class)[None, :]).reshape(-1, 1)
+        * inner,
+        G,
+    )
+    table_high, table_low = split_table(np.concatenate([cosine, sine], axis=0))
+    first_q = np.arange(nc)[:, None, None] * cols_here - HALO
+    cosine, sine = turn((first_q + np.arange(RADIX)) * inner[None, :, None], G)
+    turns = np.concatenate([cosine, sine], axis=2).astype(np.float32)
+    turns = lax.dynamic_index_in_dim(jnp.asarray(turns), col, 0, keepdims=False)
+    vmem = pl.BlockSpec(memory_space=pltpu.VMEM)
+    rows = pl.pallas_call(
+        lambda *refs: row_kernel(*refs, blocks=nc, part=part, per_class=per_class),
+        out_shape=jax.ShapeDtypeStruct((nr, window, 2 * LANES), F32),
+        in_specs=[pl.BlockSpec(memory_space=pltpu.SMEM)] + [vmem] * (nc + 3),
+        out_specs=vmem,
+        scratch_shapes=[
+            pltpu.VMEM((G, LANES), F32),
+            pltpu.VMEM((G, LANES), F32),
+            pltpu.VMEM((RADIX, part, 2 * LANES), BF16),
+            pltpu.VMEM((RADIX, part, 2 * LANES), BF16),
+        ],
+        compiler_params=pltpu.CompilerParams(vmem_limit_bytes=48 * 2**20),
+        name="rows",
+    )(infos, *blocks, turns, jnp.asarray(table_high), jnp.asarray(table_low))
+
+    rows = lax.all_to_all(rows, "row", split_axis=0, concat_axis=0, tiled=True)
+
+    place = (RADIX * np.arange(per_class)[None, :] + np.arange(RADIX)[:, None]).reshape(-1)
+    distance = place[:, None] - np.arange(cols_here)[None, :]
+    distance = np.where((distance >= 0) & (distance < KW), distance, -1)
+    at_q = (row * nc + col) * cols_here - HALO + jnp.asarray(place, jnp.int32)
+    inside = ((at_q >= 0) & (at_q < G)).astype(F32) * (1.0 / G)
+    across = spread_taps(distance, scale_kernels) * inside[None, :, None]
+    across = jnp.concatenate([across[m] for m in range(NSCALE)], axis=1)
+    bh, bl = split_outside(across)
+    per_band = LANES // RADIX // nc
+    keys = (
+        np.arange(nr)[:, None, None] * stride
+        + np.arange(nc)[None, :, None] * (stride // nc)
+        + np.arange(per_band)[None, None, :] * RADIX
+    ).reshape(-1)
+    k_of = np.arange(RADIX)[:, None] + keys[None, :]
+    cosine, sine = turn((np.arange(KW) - HALO)[:, None] * k_of.reshape(1, -1), G)
+    hat = jnp.dot(
+        scale_kernels,
+        jnp.asarray(np.concatenate([cosine, sine], axis=1), F32),
+        precision=HIGHEST,
+    ).reshape(NSCALE, 2, RADIX, keys.size)
+    near = np.arange(-HALO, HALO)
+    cosine, sine = turn(k_of[:, :, None] * near, G)
+    edge = np.zeros((RADIX, 2 * keys.size, LANES))
+    edge[:, : keys.size, : 2 * HALO] = cosine
+    edge[:, keys.size :, : 2 * HALO] = -sine
+    eh, el = split_table(edge)
+    wrap = np.full((LANES, 2 * LANES), -1)
+    for e in range(HALO):
+        for p in range(e + 1):
+            wrap[e, p] = e - p
+        for j in range(e, HALO):
+            wrap[HALO + e, 2 * LANES - HALO + j] = e + 2 * HALO - j
+    th, tl = split_outside(spread_taps(wrap, scale_kernels))
+    tiles = part // LANES
+    cosine, sine = turn(k_of[:, :, None] * np.arange(part), G)
+    table = np.concatenate(
+        [
+            np.stack([cosine, sine], axis=2),
+            np.stack([-sine, cosine], axis=2),
+        ],
+        axis=1,
+    )
+    table = table.reshape(RADIX, 2 * keys.size, 2, tiles, LANES).transpose(3, 0, 1, 2, 4)
+    fh, fl = split_table(table.reshape(tiles, RADIX, 2 * keys.size, 2 * LANES))
+    table_spec = pl.BlockSpec((1, RADIX, 2 * keys.size, 2 * LANES), lambda t: (t, 0, 0, 0))
+    operands = (rows, bh, bl, hat, jnp.asarray(eh), jnp.asarray(el), th, tl)
+    out = pl.pallas_call(
+        column_kernel,
+        grid=(tiles,),
+        out_shape=jax.ShapeDtypeStruct((width, G), F32),
+        in_specs=[whole(o.shape) for o in operands] + [table_spec, table_spec],
+        out_specs=pl.BlockSpec(memory_space=pl.ANY),
+        scratch_shapes=[
+            pltpu.VMEM((2, width // LANES, nr * LANES, LANES), F32),
+            pltpu.VMEM((RADIX, width, 2 * keys.size), BF16),
+            pltpu.VMEM((RADIX, width, 2 * keys.size), BF16),
+            pltpu.VMEM((width, 2 * LANES), F32),
+            pltpu.VMEM((RADIX, width, 2 * LANES), F32),
+            pltpu.VMEM((2, RADIX, width, LANES), F32),
+            pltpu.SemaphoreType.DMA((2, RADIX)),
+        ],
+        compiler_params=pltpu.CompilerParams(vmem_limit_bytes=56 * 2**20),
+        name="columns",
+    )(*operands, jnp.asarray(fh), jnp.asarray(fl))
+    return out.reshape(NSCALE, cols_here, G)
+
+
 def solution(mesh):
+    nr, nc = mesh.shape["row"], mesh.shape["col"]
+    fits = nr == RADIX and nc * SUB == LANES
     return jax.shard_map(
-        per_device,
+        kernel_device if fits else general_device,
         mesh=mesh,
         in_specs=(
             P(None, ("row", "col")),

time: 1140 us -> 170 us (0.15)
  waiting for transfers between devices: 434 us -> 10.9 us
  matrix products: 422 us -> 0.29 us
  local copies, waits for them, and re-layouts: 210 us -> 65.4 us
  Pallas kernels: 0 us -> 59.9 us
  starting transfers between devices: 43.1 us -> 20 us
  other arithmetic: 21.5 us -> 10 us
    all_to_all x7 -> x1, waiting for transfers between devices: 429 us -> 0.01 us  [kernel_device(): rows = lax.all_to_all(rows, 'row', split_axis=0, concat_axis=0, tiled=True)]
    dot_general x38 -> x1, matrix products: 422 us -> 0.29 us  [kernel_device(): jnp.dot(scale_kernels, jnp.asarray(np.concatenate([cosine, sine], axis=1)...]
    all_to_all x11 -> x0, local copies, waits for them, and re-layouts: 61.7 us -> none  [the longest x2 18 us: per_device(): lax.all_to_all(lax.all_to_all(rows_imag, 'row', split_axis=1, concat_axis...]
    pallas_call x0 -> x3, Pallas kernels: none -> 59.9 us  [the longest x1 30.2 us: kernel_device(): pl.pallas_call(column_kernel, grid=(tiles,), out_shape=jax.ShapeDtypeStru...]
    slice x21 -> x3, local copies, waits for them, and re-layouts: 35.1 us -> 1.88 us  [the longest x1 0.97 us: rotated_visibilities(): vis_block[1] * sine_part]
    all_to_all x7 -> x1, starting transfers between devices: 36.8 us -> 3.93 us  [kernel_device(): rows = lax.all_to_all(rows, 'row', split_axis=0, concat_axis=0, tiled=True)]
    unnamed x34 -> x209, local copies, waits for them, and re-layouts: 30.2 us -> 62.4 us
    transpose x2 -> x0, local copies, waits for them, and re-layouts: 20.9 us -> none  [reorder(): return field.reshape(col_devices, row_devices, group_rows, pencil_cols).t...]
  transfers between devices with their start and end apart: 9 -> 7, of which waited for: 7 -> 2; matrix products, arithmetic and copies ran while one was open for 14% -> 41% of each run, Pallas kernels for 0% -> 0%
where the time goes in v1:
time: 170 us; the launch traced here: 168 us
  local copies, waits for them, and re-layouts  65.4 us (38%)
  Pallas kernels  59.9 us (35%)
  starting transfers between devices  20 us (12%)
  waiting for transfers between devices  10.9 us (6%)
  other arithmetic  10 us (6%)
    unnamed x209, local copies, waits for them, and re-layouts  62.4 us
    pallas_call x1, Pallas kernels, kernel_device(): pl.pallas_call(column_kernel, grid=(tiles,), out_shape=jax.ShapeDtypeStru...  30.2 us
    pallas_call x1, Pallas kernels, kernel_device(): pl.pallas_call(lambda *refs: row_kernel(*refs, blocks=nc, part=part, per_...  23.5 us
    ppermute x3, waiting for transfers between devices, kernel_device(): lax.ppermute(info, 'col', s)  10.9 us
    ppermute x3, starting transfers between devices, kernel_device(): lax.ppermute(info, 'col', s)  9.93 us
    pallas_call x1, Pallas kernels, kernel_device(): pl.pallas_call(subgrid_kernel, out_shape=jax.ShapeDtypeStruct((subs // 2...  6.2 us
    ppermute x3, starting transfers between devices, kernel_device(): blocks = [subgrids] + [lax.ppermute(subgrids, 'col', s) for s in shifts]  6.11 us
    all_to_all x1, starting transfers between devices, kernel_device(): rows = lax.all_to_all(rows, 'row', split_axis=0, concat_axis=0, tiled=True)  3.93 us
  transfers between devices with their start and end apart: 7, of which 2 were waited for; matrix products, arithmetic and copies ran while one was open for 41% of the time, Pallas kernels for 0%

profile of v1, /device:TPU:0, one launch (start us, length us, event | category | flops | bytes accessed | tf_op | source)
XLA Modules:
  0.0 167.6 jit_solution(9275947031917594516)
XLA Ops:
  0.9 1.0 fusion.7
  3.6 6.2 %subgrids.1.refs_1_ = f32[512,128]{1,0:T(8,128)S(1)} custom-call(s32[2,8192]{1,0:T(2,128)S(1)} %copy-done.2, f32[2,8192]{1,0:T(2,128)S(1)} %pad_maximum_fusion.1.rot_ref, f32[8,8]{1,0:T(8,128)S(1)} %bitcast.28), custom_call_target="tpu_custom_call" | custom-call | tf_op jit(solution)/shard_map/subgrids/pallas_call | solution.py:592
  9.9 5.1 %collective-permute-start.5 = (f32[512,128]{1,0:T(8,128)S(1)}, f32[512,128]{1,0:T(8,128)S(1)}, u32[]{:S(2)}, u32[]{:S(2)}) collective-permute-start(f32[512,128]{1,0:T(8,128)S(1)} %subgrids.1.refs_1_), channel_id=1, source_target_pairs={{0,3},{1,0},{2,1},{3,2},{4,7},{5,4},{6,5},{7,6},{8,11},{9,8},{10,9... | collective-permute-start | bytes 786440 | tf_op jit(solution)/shard_map/ppermute | solution.py:598
  15.0 1.0 collective-permute-start.3
  17.3 2.8 %collective-permute-start.2 = (s32[2,32]{1,0:T(2,128)S(1)}, s32[2,32]{1,0:T(2,128)S(1)}, u32[]{:S(2)}, u32[]{:S(2)}) collective-permute-start(s32[2,32]{1,0:T(2,128)S(1)} %pad_add_fusion), channel_id=1, source_target_pairs={{0,3},{1,0},{2,1},{3,2},{4,7},{5,4},{6,5},{7,6},{8,11},{9,8},{10,9... | collective-permute-start | bytes 776 | tf_op jit(solution)/shard_map/ppermute | solution.py:589
  20.1 1.1 collective-permute-start.1
  21.2 10.7 %collective-permute-done.2 = s32[2,32]{1,0:T(2,128)S(1)} collective-permute-done((s32[2,32]{1,0:T(2,128)S(1)}, s32[2,32]{1,0:T(2,128)S(1)}, u32[]{:S(2)}, u32[]{:S(2)}) %collective-permute-start.2) | collective-permute-done | bytes 288 | tf_op jit(solution)/shard_map/ppermute | solution.py:589
  31.9 6.0 %collective-permute-start = (s32[2,32]{1,0:T(2,128)S(1)}, s32[2,32]{1,0:T(2,128)S(1)}, u32[]{:S(2)}, u32[]{:S(2)}) collective-permute-start(s32[2,32]{1,0:T(2,128)S(1)} %pad_add_fusion), channel_id=1, source_target_pairs={{0,1},{1,2},{2,3},{3,0},{4,5},{5,6},{6,7},{7,4},{8,9},{9,10},{10,1... | collective-permute-start | bytes 776 | tf_op jit(solution)/shard_map/ppermute | solution.py:589
  37.9 1.1 dynamic-slice_bitcast_fusion.refs_5_
  40.0 1.3 copy-done.1
  41.2 23.5 %rows.1 = f32[8,288,256]{2,1,0:T(8,128)} custom-call(s32[2,128]{1,0:T(2,128)S(1)} %pad_add_fusion.1.refs_0_, f32[512,128]{1,0:T(8,128)S(1)} %subgrids.1.refs_1_, f32[512,128]{1,0:T(8,128)S(1)} %collective-permute-done.3.refs_2_, f32[512,128]{1,0:T(8,128)S(1)} %collective-permute-done.4.refs_3_, f32[512,128]{1,0:T(8,128)S(1)} %collective-permute-done.5.refs_4_, ...), custom_call_target="tpu_custom_call" | custom-call | tf_op jit(solution)/shard_map/rows/pallas_call | solution.py:612
  64.7 3.9 %all-to-all-start = ((f32[8,288,256]{2,1,0:T(8,128)}), f32[8,288,256]{2,1,0:T(8,128)S(1)}, u32[]{:S(2)}, u32[]{:S(2)}) async-start(f32[8,288,256]{2,1,0:T(8,128)} %rows.1), calls=%async_computation | async-start | bytes 4718592 | tf_op jit(solution)/shard_map/all_to_all | solution.py:627
  69.8 1.4 copy.88
  71.2 1.4 copy.87
  72.5 1.4 copy.86
  73.9 1.4 copy.85
  75.3 1.4 copy.84
  76.7 1.4 copy.83
  78.1 1.4 copy.82
  79.5 1.4 copy.81
  80.9 1.4 copy.80
  82.3 1.4 copy.79
  83.7 1.4 copy.78
  85.1 1.4 copy.77
  86.5 1.4 copy.76
  87.9 1.4 copy.75
  89.3 1.4 copy.74
  90.7 1.4 copy.73
  92.1 1.4 copy.72
  93.5 1.4 copy.71
  94.9 1.4 copy.70
  96.3 1.4 copy.69
  97.7 1.4 copy.68
  99.0 1.4 copy.67
  100.5 1.4 copy.66
  101.8 1.4 copy.65
  103.3 1.4 copy.64
  104.6 1.4 copy.63
  106.0 1.4 copy.62
  107.4 1.4 copy.61
  108.8 1.4 copy.60
  110.2 1.4 copy.59
  111.6 1.4 copy.58
  113.0 1.4 copy.57
  128.4 3.7 %select_multiply_fusion = f32[2,288,256]{2,1,0:T(8,128)S(1)} fusion(f32[288]{0:T(512)S(1)} %fusion.5, f32[2]{0:T(128)S(1)} %get-tuple-element.37, f32[2]{0:T(128)S(1)} %get-tuple-element.6, f32[2]{0:T(128)S(1)} %get-tuple-element.7, f32[2]{0:T(128)S(1)} %get-tuple-element.8, f32[2]{0:T(128)S(1)} %get-tuple-element.9, f32[2]{0:T(128)S(1)} %get-tuple-element.10, ...), kind=kLoop, calls=%fused_computation.5 | loop fusion | flops 5013504 | bytes 3024264 | tf_op jit(solution)/shard_map/mul | solution.py:634
  133.4 1.7 %fusion.1 = (bf16[2,128,256]{2,1,0:T(8,128)(2,1)}, f32[2,128,256]{2,1,0:T(8,128)S(1)}) fusion(f32[2]{0:T(128)S(1)} %get-tuple-element.37, pred[128,256]{1,0:T(8,128)(4,1)S(1)} %copy-done.37, f32[2]{0:T(128)S(1)} %get-tuple-element.6, pred[128,256]{1,0:T(8,128)(4,1)S(1)} %copy-done.36, f32[2]{0:T(128)S(1)} %get-tuple-element.7, ...), kind=kLoop, calls=%fused_computation.11 | loop fusion | flops 2293760 | bytes 1442048 | tf_op jit(solution)/shard_map/convert_element_type | solution.py:300
  135.8 1.4 copy-done.3
  137.2 30.2 %columns.1 = f32[512,8192]{1,0:T(8,128)} custom-call(f32[8,288,256]{2,1,0:T(8,128)} %copy-done.3, bf16[288,512]{1,0:T(8,128)(2,1)} %get-tuple-element.41.bh_ref, bf16[288,512]{1,0:T(8,128)(2,1)} %get-tuple-element.40.bl_ref, f32[2,2,8,128]{3,2,1,0:T(8,128)} %bitcast.33, bf16[8,256,128]{2,1,0:T(8,128)(2,1)} %constant.30.clone.eh_ref, ...), custom_call_target="tpu_custom_call" | custom-call | tf_op jit(solution)/shard_map/columns/pallas_call | solution.py:676
  (194 shorter events, 21.2 us)
Async XLA Ops:
  0.0 39.9 %copy-start = (bf16[576,1024]{1,0:T(8,128)(2,1)S(1)}, bf16[576,1024]{1,0:T(8,128)(2,1)}, u32[]{:S(2)}) copy-start(bf16[576,1024]{1,0:T(8,128)(2,1)} %constant.25.clone.refs_7_) | copy-start | bytes 3538948
  9.9 30.1 %collective-permute-start.5 = (f32[512,128]{1,0:T(8,128)S(1)}, f32[512,128]{1,0:T(8,128)S(1)}, u32[]{:S(2)}, u32[]{:S(2)}) collective-permute-start(f32[512,128]{1,0:T(8,128)S(1)} %subgrids.1.refs_1_), channel_id=1, source_target_pairs={{0,3},{1,0},{2,1},{3,2},{4,7},{5,4},{6,5},{7,6},{8,11},{9,8},{10,9... | collective-permute-start | bytes 786440 | tf_op jit(solution)/shard_map/ppermute | solution.py:598
  15.0 25.0 %collective-permute-start.4 = (f32[512,128]{1,0:T(8,128)S(1)}, f32[512,128]{1,0:T(8,128)S(1)}, u32[]{:S(2)}, u32[]{:S(2)}) collective-permute-start(f32[512,128]{1,0:T(8,128)S(1)} %subgrids.1.refs_1_), channel_id=1, source_target_pairs={{0,2},{1,3},{2,0},{3,1},{4,6},{5,7},{6,4},{7,5},{8,10},{9,11},{10,... | collective-permute-start | bytes 786440 | tf_op jit(solution)/shard_map/ppermute | solution.py:598
  15.0 25.0 %collective-permute-start.3 = (f32[512,128]{1,0:T(8,128)S(1)}, f32[512,128]{1,0:T(8,128)S(1)}, u32[]{:S(2)}, u32[]{:S(2)}) collective-permute-start(f32[512,128]{1,0:T(8,128)S(1)} %subgrids.1.refs_1_), channel_id=1, source_target_pairs={{0,1},{1,2},{2,3},{3,0},{4,5},{5,6},{6,7},{7,4},{8,9},{9,10},{10,1... | collective-permute-start | bytes 786440 | tf_op jit(solution)/shard_map/ppermute | solution.py:598
  17.3 14.6 %collective-permute-start.2 = (s32[2,32]{1,0:T(2,128)S(1)}, s32[2,32]{1,0:T(2,128)S(1)}, u32[]{:S(2)}, u32[]{:S(2)}) collective-permute-start(s32[2,32]{1,0:T(2,128)S(1)} %pad_add_fusion), channel_id=1, source_target_pairs={{0,3},{1,0},{2,1},{3,2},{4,7},{5,4},{6,5},{7,6},{8,11},{9,8},{10,9... | collective-permute-start | bytes 776 | tf_op jit(solution)/shard_map/ppermute | solution.py:589
  20.1 18.8 %collective-permute-start.1 = (s32[2,32]{1,0:T(2,128)S(1)}, s32[2,32]{1,0:T(2,128)S(1)}, u32[]{:S(2)}, u32[]{:S(2)}) collective-permute-start(s32[2,32]{1,0:T(2,128)S(1)} %pad_add_fusion), channel_id=1, source_target_pairs={{0,2},{1,3},{2,0},{3,1},{4,6},{5,7},{6,4},{7,5},{8,10},{9,11},{10,... | collective-permute-start | bytes 776 | tf_op jit(solution)/shard_map/ppermute | solution.py:589
  31.9 7.3 %collective-permute-start = (s32[2,32]{1,0:T(2,128)S(1)}, s32[2,32]{1,0:T(2,128)S(1)}, u32[]{:S(2)}, u32[]{:S(2)}) collective-permute-start(s32[2,32]{1,0:T(2,128)S(1)} %pad_add_fusion), channel_id=1, source_target_pairs={{0,1},{1,2},{2,3},{3,0},{4,5},{5,6},{6,7},{7,4},{8,9},{9,10},{10,1... | collective-permute-start | bytes 776 | tf_op jit(solution)/shard_map/ppermute | solution.py:589
  64.7 71.1 %all-to-all-start = ((f32[8,288,256]{2,1,0:T(8,128)}), f32[8,288,256]{2,1,0:T(8,128)S(1)}, u32[]{:S(2)}, u32[]{:S(2)}) async-start(f32[8,288,256]{2,1,0:T(8,128)} %rows.1), calls=%async_computation | async-start | bytes 4718592 | tf_op jit(solution)/shard_map/all_to_all | solution.py:627
  68.6 45.9 %copy-start.65 = (pred[288,256]{1,0:T(32,128)(4,1)S(1)}, pred[288,256]{1,0:T(32,128)(4,1)}, u32[]{:S(2)}) copy-start(pred[288,256]{1,0:T(32,128)(4,1)} %constant.38) | copy-start | bytes 221188
  68.6 46.0 %copy-start.64 = (pred[288,256]{1,0:T(32,128)(4,1)S(1)}, pred[288,256]{1,0:T(32,128)(4,1)}, u32[]{:S(2)}) copy-start(pred[288,256]{1,0:T(32,128)(4,1)} %constant.39) | copy-start | bytes 221188
  68.7 46.0 %copy-start.63 = (pred[288,256]{1,0:T(32,128)(4,1)S(1)}, pred[288,256]{1,0:T(32,128)(4,1)}, u32[]{:S(2)}) copy-start(pred[288,256]{1,0:T(32,128)(4,1)} %constant.40) | copy-start | bytes 221188
  68.7 46.0 %copy-start.62 = (pred[288,256]{1,0:T(32,128)(4,1)S(1)}, pred[288,256]{1,0:T(32,128)(4,1)}, u32[]{:S(2)}) copy-start(pred[288,256]{1,0:T(32,128)(4,1)} %constant.41) | copy-start | bytes 221188
  68.7 46.1 %copy-start.61 = (pred[288,256]{1,0:T(32,128)(4,1)S(1)}, pred[288,256]{1,0:T(32,128)(4,1)}, u32[]{:S(2)}) copy-start(pred[288,256]{1,0:T(32,128)(4,1)} %constant.42) | copy-start | bytes 221188
  68.7 46.1 %copy-start.60 = (pred[288,256]{1,0:T(32,128)(4,1)S(1)}, pred[288,256]{1,0:T(32,128)(4,1)}, u32[]{:S(2)}) copy-start(pred[288,256]{1,0:T(32,128)(4,1)} %constant.43) | copy-start | bytes 221188
  68.7 46.1 %copy-start.59 = (pred[288,256]{1,0:T(32,128)(4,1)S(1)}, pred[288,256]{1,0:T(32,128)(4,1)}, u32[]{:S(2)}) copy-start(pred[288,256]{1,0:T(32,128)(4,1)} %constant.44) | copy-start | bytes 221188
  68.7 46.2 %copy-start.58 = (pred[288,256]{1,0:T(32,128)(4,1)S(1)}, pred[288,256]{1,0:T(32,128)(4,1)}, u32[]{:S(2)}) copy-start(pred[288,256]{1,0:T(32,128)(4,1)} %constant.45) | copy-start | bytes 221188
  68.7 46.2 %copy-start.57 = (pred[288,256]{1,0:T(32,128)(4,1)S(1)}, pred[288,256]{1,0:T(32,128)(4,1)}, u32[]{:S(2)}) copy-start(pred[288,256]{1,0:T(32,128)(4,1)} %constant.46) | copy-start | bytes 221188
  68.7 46.2 %copy-start.56 = (pred[288,256]{1,0:T(32,128)(4,1)S(1)}, pred[288,256]{1,0:T(32,128)(4,1)}, u32[]{:S(2)}) copy-start(pred[288,256]{1,0:T(32,128)(4,1)} %constant.47) | copy-start | bytes 221188
  68.8 46.3 %copy-start.55 = (pred[288,256]{1,0:T(32,128)(4,1)S(1)}, pred[288,256]{1,0:T(32,128)(4,1)}, u32[]{:S(2)}) copy-start(pred[288,256]{1,0:T(32,128)(4,1)} %constant.48) | copy-start | bytes 221188
  68.8 45.6 %copy-start.69 = (pred[288,256]{1,0:T(32,128)(4,1)S(1)}, pred[288,256]{1,0:T(32,128)(4,1)}, u32[]{:S(2)}) copy-start(pred[288,256]{1,0:T(32,128)(4,1)} %constant.34) | copy-start | bytes 221188
  68.8 45.6 %copy-start.68 = (pred[288,256]{1,0:T(32,128)(4,1)S(1)}, pred[288,256]{1,0:T(32,128)(4,1)}, u32[]{:S(2)}) copy-start(pred[288,256]{1,0:T(32,128)(4,1)} %constant.35) | copy-start | bytes 221188
  68.8 45.7 %copy-start.67 = (pred[288,256]{1,0:T(32,128)(4,1)S(1)}, pred[288,256]{1,0:T(32,128)(4,1)}, u32[]{:S(2)}) copy-start(pred[288,256]{1,0:T(32,128)(4,1)} %constant.36) | copy-start | bytes 221188
  68.8 45.7 %copy-start.66 = (pred[288,256]{1,0:T(32,128)(4,1)S(1)}, pred[288,256]{1,0:T(32,128)(4,1)}, u32[]{:S(2)}) copy-start(pred[288,256]{1,0:T(32,128)(4,1)} %constant.37) | copy-start | bytes 221188
  68.8 47.2 %copy-start.54 = (pred[288,256]{1,0:T(32,128)(4,1)S(1)}, pred[288,256]{1,0:T(32,128)(4,1)}, u32[]{:S(2)}) copy-start(pred[288,256]{1,0:T(32,128)(4,1)} %constant.50) | copy-start | bytes 221188
  69.2 47.5 %copy-start.53 = (pred[288,256]{1,0:T(32,128)(4,1)S(1)}, pred[288,256]{1,0:T(32,128)(4,1)}, u32[]{:S(2)}) copy-start(pred[288,256]{1,0:T(32,128)(4,1)} %constant.51) | copy-start | bytes 221188
  69.8 47.6 %copy-start.52 = (pred[288,256]{1,0:T(32,128)(4,1)S(1)}, pred[288,256]{1,0:T(32,128)(4,1)}, u32[]{:S(2)}) copy-start(pred[288,256]{1,0:T(32,128)(4,1)} %constant.52) | copy-start | bytes 221188
  73.9 44.1 %copy-start.51 = (pred[288,256]{1,0:T(32,128)(4,1)S(1)}, pred[288,256]{1,0:T(32,128)(4,1)}, u32[]{:S(2)}) copy-start(pred[288,256]{1,0:T(32,128)(4,1)} %constant.53) | copy-start | bytes 221188
  76.7 42.0 %copy-start.50 = (pred[288,256]{1,0:T(32,128)(4,1)S(1)}, pred[288,256]{1,0:T(32,128)(4,1)}, u32[]{:S(2)}) copy-start(pred[288,256]{1,0:T(32,128)(4,1)} %constant.184) | copy-start | bytes 221188
  79.5 39.8 %copy-start.49 = (pred[288,256]{1,0:T(32,128)(4,1)S(1)}, pred[288,256]{1,0:T(32,128)(4,1)}, u32[]{:S(2)}) copy-start(pred[288,256]{1,0:T(32,128)(4,1)} %constant.185) | copy-start | bytes 221188
  82.3 37.7 %copy-start.48 = (pred[288,256]{1,0:T(32,128)(4,1)S(1)}, pred[288,256]{1,0:T(32,128)(4,1)}, u32[]{:S(2)}) copy-start(pred[288,256]{1,0:T(32,128)(4,1)} %constant.186) | copy-start | bytes 221188
  86.5 34.2 %copy-start.47 = (pred[288,256]{1,0:T(32,128)(4,1)S(1)}, pred[288,256]{1,0:T(32,128)(4,1)}, u32[]{:S(2)}) copy-start(pred[288,256]{1,0:T(32,128)(4,1)} %constant.187) | copy-start | bytes 221188
  89.3 32.0 %copy-start.46 = (pred[288,256]{1,0:T(32,128)(4,1)S(1)}, pred[288,256]{1,0:T(32,128)(4,1)}, u32[]{:S(2)}) copy-start(pred[288,256]{1,0:T(32,128)(4,1)} %constant.188) | copy-start | bytes 221188
  92.1 29.9 %copy-start.45 = (pred[288,256]{1,0:T(32,128)(4,1)S(1)}, pred[288,256]{1,0:T(32,128)(4,1)}, u32[]{:S(2)}) copy-start(pred[288,256]{1,0:T(32,128)(4,1)} %constant.189) | copy-start | bytes 221188
  94.9 27.7 %copy-start.44 = (pred[288,256]{1,0:T(32,128)(4,1)S(1)}, pred[288,256]{1,0:T(32,128)(4,1)}, u32[]{:S(2)}) copy-start(pred[288,256]{1,0:T(32,128)(4,1)} %constant.190) | copy-start | bytes 221188
  99.0 24.2 %copy-start.43 = (pred[288,256]{1,0:T(32,128)(4,1)S(1)}, pred[288,256]{1,0:T(32,128)(4,1)}, u32[]{:S(2)}) copy-start(pred[288,256]{1,0:T(32,128)(4,1)} %constant.191) | copy-start | bytes 221188
  101.8 22.1 %copy-start.42 = (pred[288,256]{1,0:T(32,128)(4,1)S(1)}, pred[288,256]{1,0:T(32,128)(4,1)}, u32[]{:S(2)}) copy-start(pred[288,256]{1,0:T(32,128)(4,1)} %constant.192) | copy-start | bytes 221188
  104.6 20.0 %copy-start.41 = (pred[288,256]{1,0:T(32,128)(4,1)S(1)}, pred[288,256]{1,0:T(32,128)(4,1)}, u32[]{:S(2)}) copy-start(pred[288,256]{1,0:T(32,128)(4,1)} %constant.193) | copy-start | bytes 221188
  107.4 17.8 %copy-start.40 = (pred[288,256]{1,0:T(32,128)(4,1)S(1)}, pred[288,256]{1,0:T(32,128)(4,1)}, u32[]{:S(2)}) copy-start(pred[288,256]{1,0:T(32,128)(4,1)} %constant.194) | copy-start | bytes 221188
  111.6 14.3 %copy-start.39 = (pred[288,256]{1,0:T(32,128)(4,1)S(1)}, pred[288,256]{1,0:T(32,128)(4,1)}, u32[]{:S(2)}) copy-start(pred[288,256]{1,0:T(32,128)(4,1)} %constant.195) | copy-start | bytes 221188
  114.4 12.2 %copy-start.38 = (pred[288,256]{1,0:T(32,128)(4,1)S(1)}, pred[288,256]{1,0:T(32,128)(4,1)}, u32[]{:S(2)}) copy-start(pred[288,256]{1,0:T(32,128)(4,1)} %constant.196) | copy-start | bytes 221188
  114.4 13.7 %copy-start.70 = (s32[288]{0:T(512)S(1)}, s32[288]{0:T(512)}, u32[]{:S(2)}) copy-start(s32[288]{0:T(512)} %constant.26.clone) | copy-start | bytes 3460
  128.1 5.0 %copy-start.6 = (pred[128,256]{1,0:T(8,128)(4,1)S(1)}, pred[128,256]{1,0:T(8,128)(4,1)}, u32[]{:S(2)}) copy-start(pred[128,256]{1,0:T(8,128)(4,1)} %copy.88) | copy-start | bytes 98308
  128.1 5.0 %copy-start.7 = (pred[128,256]{1,0:T(8,128)(4,1)S(1)}, pred[128,256]{1,0:T(8,128)(4,1)}, u32[]{:S(2)}) copy-start(pred[128,256]{1,0:T(8,128)(4,1)} %copy.87) | copy-start | bytes 98308
  128.1 5.0 %copy-start.8 = (pred[128,256]{1,0:T(8,128)(4,1)S(1)}, pred[128,256]{1,0:T(8,128)(4,1)}, u32[]{:S(2)}) copy-start(pred[128,256]{1,0:T(8,128)(4,1)} %copy.86) | copy-start | bytes 98308
  128.2 5.0 %copy-start.9 = (pred[128,256]{1,0:T(8,128)(4,1)S(1)}, pred[128,256]{1,0:T(8,128)(4,1)}, u32[]{:S(2)}) copy-start(pred[128,256]{1,0:T(8,128)(4,1)} %copy.85) | copy-start | bytes 98308
  128.2 5.0 %copy-start.10 = (pred[128,256]{1,0:T(8,128)(4,1)S(1)}, pred[128,256]{1,0:T(8,128)(4,1)}, u32[]{:S(2)}) copy-start(pred[128,256]{1,0:T(8,128)(4,1)} %copy.84) | copy-start | bytes 98308
  128.2 5.0 %copy-start.11 = (pred[128,256]{1,0:T(8,128)(4,1)S(1)}, pred[128,256]{1,0:T(8,128)(4,1)}, u32[]{:S(2)}) copy-start(pred[128,256]{1,0:T(8,128)(4,1)} %copy.83) | copy-start | bytes 98308
  128.2 5.0 %copy-start.12 = (pred[128,256]{1,0:T(8,128)(4,1)S(1)}, pred[128,256]{1,0:T(8,128)(4,1)}, u32[]{:S(2)}) copy-start(pred[128,256]{1,0:T(8,128)(4,1)} %copy.82) | copy-start | bytes 98308
  (30 other events, 136.0 us)

commit v2 on v1

--- a/solution.py
+++ b/solution.py
@@ -18,6 +18,7 @@
 NSCALE = 2
 HALO = (KW - 1) // 2
 RADIX = 8
+CLASSES = 16
 LANES = 128
 
 HIGHEST = lax.Precision.HIGHEST
@@ -295,11 +296,6 @@
     return high, (value - high.astype(F32)).astype(BF16)
 
 
-def split_outside(value):
-    high = lax.reduce_precision(value, 8, 7)
-    return high.astype(BF16), (value - high).astype(BF16)
-
-
 def split_table(table):
     table = np.asarray(table, np.float64)
     high = table.astype(BF16)
@@ -325,16 +321,40 @@
     )
 
 
-def subgrid_kernel(pos_ref, rot_ref, taps_ref, out_ref):
+def turned_back(steps):
+    quarter = WSTEPS // 4
+    turns = (steps + quarter // 2) >> (quarter.bit_length() - 1)
+    angle = (steps - turns * quarter).astype(F32) * (2.0 * math.pi / WSTEPS)
+    square = angle * angle
+    cosine = 1.0 + square * (
+        -1 / 2 + square * (1 / 24 + square * (-1 / 720 + square * (1 / 40320 - square / 3628800)))
+    )
+    sine = angle * (
+        1.0 + square * (-1 / 6 + square * (1 / 120 + square * (-1 / 5040 + square / 362880)))
+    )
+    odd = (turns & 1) == 1
+    first, second = jnp.where(odd, sine, cosine), jnp.where(odd, cosine, sine)
+    first = jnp.where(((turns + 1) & 2) == 2, -first, first)
+    return first, jnp.where((turns & 2) == 2, -second, second)
+
+
+def subgrid_kernel(pos_ref, vis_ref, phase_ref, taps_ref, info_ref, out_ref):
     span = 2 * VPS
-    table = taps_ref[...]
+    pairs = vis_ref.shape[1] // span
+    diagonal = lax.broadcasted_iota(jnp.int32, (OVER, SUP), 0) == lax.broadcasted_iota(
+        jnp.int32, (OVER, SUP), 1
+    )
+    table = [
+        jnp.sum(jnp.where(diagonal, taps_ref[s : s + 1, :], 0.0), axis=1, keepdims=True)
+        for s in range(OVER)
+    ]
 
     def taps(position):
         step = position & (OVER - 1)
         cell = position >> (OVER.bit_length() - 1)
         values = jnp.zeros((SUP, span), F32)
         for s in range(OVER):
-            values = jnp.where(step == s, table[:, s : s + 1], values)
+            values = jnp.where(step == s, table[s], values)
         offset = lax.broadcasted_iota(jnp.int32, (SUB, span), 0) - cell
         result = jnp.zeros((SUB, span), F32)
         for t in range(SUP):
@@ -347,8 +367,14 @@
         here = pl.ds(pl.multiple_of(p * span, span), span)
         along_rows = taps(pos_ref[0:1, here])
         along_cols = taps(pos_ref[1:2, here])
+        cosine, sine = turned_back(phase_ref[0:1, here])
+        real, imag = vis_ref[0:1, here], vis_ref[1:2, here]
         weighted = jnp.concatenate(
-            [along_rows * rot_ref[0:1, here], along_rows * rot_ref[1:2, here]], axis=0
+            [
+                along_rows * (real * cosine + imag * sine),
+                along_rows * (imag * cosine - real * sine),
+            ],
+            axis=0,
         )
         weighted = jnp.concatenate(split(weighted), axis=0)
         cols = jnp.concatenate(split(along_cols), axis=0)
@@ -361,7 +387,10 @@
         out_ref[pl.ds(pl.multiple_of(p * SUB, SUB), SUB), :] = jnp.where(first, sums[0], sums[1])
         return carry
 
-    lax.fori_loop(0, out_ref.shape[0] // SUB, pair, 0)
+    lax.fori_loop(0, pairs, pair, 0, unroll=4)
+    out_ref[pairs * SUB :, :] = jnp.broadcast_to(
+        info_ref[...], (out_ref.shape[0] - pairs * SUB, LANES)
+    )
 
 
 def radix_eight(real, imag):
@@ -406,16 +435,15 @@
         def place(p, carry, b=b, pairs=pairs):
             piece = xs[b][pl.ds(pl.multiple_of(p * SUB, SUB), SUB), :]
             for s in range(2):
-                number = b * 2 * pairs + 2 * p + s
-                start = info_ref[0, number]
-                group = info_ref[1, number]
+                start = info_ref[b, 2 * p + s].astype(jnp.int32)
+                group = info_ref[b, 2 * pairs + 2 * p + s].astype(jnp.int32)
                 for dest, at in ((real_ref, 2 * s), (imag_ref, 2 * s + 1)):
                     shift = (group * SUB + (LANES - at * SUB)) & (LANES - 1)
                     moved = jnp.where(owner == group, pltpu.roll(piece, shift, 1), 0.0)
                     dest[pl.ds(start, SUB), :] += moved
             return carry
 
-        lax.fori_loop(0, pairs, place, 0)
+        lax.fori_loop(0, pairs, place, 0, unroll=4)
 
     step = 16
 
@@ -434,7 +462,7 @@
             ul_ref[c, pl.ds(first, step), :] = low
         return carry
 
-    lax.fori_loop(0, part // step, classes, 0)
+    lax.fori_loop(0, part // step, classes, 0, unroll=4)
     dests = out_ref.shape[0]
     half = dests * per_class
     for c in range(RADIX):
@@ -448,8 +476,59 @@
             out_ref[d, here, LANES:] = imag[mine]
 
 
+def band_kernel(taps_ref, across_ref, wrap_ref, inside_ref, out_ref, th_ref, tl_ref):
+    def spread(index, scale):
+        out = jnp.zeros(index.shape, F32)
+        for u in range(KW):
+            out = jnp.where(index == u, taps_ref[scale, u], out)
+        return out
+
+    across, wrap = across_ref[...], wrap_ref[...]
+    rows = across.shape[0]
+    for scale in range(NSCALE):
+        cols = slice(scale * across.shape[1], (scale + 1) * across.shape[1])
+        high, low = split(spread(across, scale) * inside_ref[...])
+        out_ref[:rows, cols] = high
+        out_ref[rows : 2 * rows, cols] = high
+        out_ref[2 * rows :, cols] = low
+        cols = slice(scale * wrap.shape[1], (scale + 1) * wrap.shape[1])
+        th_ref[:, cols], tl_ref[:, cols] = split(spread(wrap, scale))
+
+
+COS1, COS3 = math.cos(math.pi / 8), math.cos(3 * math.pi / 8)
+
+
+def real_sixteen(h0, h8, x, y):
+    a, b = h0 + h8, h0 - h8
+    c, d = x[2] + x[6], (x[2] - x[6]) * ROOT_HALF
+    even = [a + x[4] + c, b + d, a - x[4], b - d, a + x[4] - c]
+    e, f = x[1] - x[7], x[3] - x[5]
+    g, h = x[1] + x[7], x[3] + x[5]
+    odd = [g + h, e * COS1 + f * COS3, (g - h) * ROOT_HALF, e * COS3 - f * COS1]
+    cosines = [even[n] + odd[n] for n in range(4)] + [even[4]]
+    cosines += [even[n] - odd[n] for n in (3, 2, 1, 0)]
+    k = (y[2] + y[6]) * ROOT_HALF
+    even = [None, k + y[4], y[2] - y[6], k - y[4]]
+    e, f = y[1] + y[7], y[3] + y[5]
+    odd = [
+        None,
+        e * COS3 + f * COS1,
+        (y[1] - y[7] + y[3] - y[5]) * ROOT_HALF,
+        e * COS1 - f * COS3,
+        y[1] - y[7] - y[3] + y[5],
+    ]
+    sines = [None] + [even[n] + odd[n] for n in (1, 2, 3)] + [odd[4]]
+    sines += [odd[n] - even[n] for n in (3, 2, 1)]
+    out = [None] * 16
+    out[0], out[8] = cosines[0], cosines[8]
+    for n in range(1, 8):
+        out[n] = cosines[n] - sines[n]
+        out[16 - n] = cosines[n] + sines[n]
+    return out
+
+
 def column_kernel(
-    rows_ref, bh_ref, bl_ref, hat_ref, eh_ref, el_ref, th_ref, tl_ref, fh_ref, fl_ref,
+    rows_ref, across_ref, hat_ref, eh_ref, el_ref, th_ref, tl_ref, fh_ref, fl_ref,
     out_ref, qt_ref, qh_ref, ql_ref, corr_ref, v_ref, o_ref, sem,
 ):
     t = pl.program_id(0)
@@ -457,49 +536,49 @@
     bands = rows_ref.shape[0]
     width = qh_ref.shape[1]
     per_scale = width // NSCALE
-    keys = bands * LANES // RADIX
+    keys = LANES // 2
 
     @pl.when(t == 0)
     def prepare():
         for i in range(bands):
             high, low = split(rows_ref[i])
-            product = dot3(high, low, bh_ref[...], bl_ref[...], 0, 0)
+            product = dot(jnp.concatenate([high, low, high], axis=0), across_ref[...], 0, 0)
             for lane in range(width // LANES):
                 cols = slice(lane * LANES, (lane + 1) * LANES)
                 qt_ref[0, lane, i * LANES : (i + 1) * LANES, :] = product[:LANES, cols]
                 qt_ref[1, lane, i * LANES : (i + 1) * LANES, :] = product[LANES:, cols]
         edge = jnp.zeros((width, LANES), F32)
-        for m in range(RADIX):
-            parts = []
-            for lane in range(width // LANES):
-                parts.append(
-                    jnp.concatenate(
-                        [
-                            qt_ref[ri, lane, pl.ds(m, keys, stride=RADIX), :].T
-                            for ri in range(2)
-                        ],
-                        axis=1,
+        half = CLASSES // 2
+        for slot in range(half):
+            halves = []
+            for m in (slot, CLASSES - slot if slot else half):
+                parts = []
+                for lane in range(width // LANES):
+                    here = pl.ds(m, keys, stride=CLASSES)
+                    pair = [qt_ref[ri, lane, here, :] for ri in range(2)]
+                    parts.append(jnp.concatenate(pair, axis=0).T)
+                halves.append(jnp.concatenate(parts, axis=0))
+            high, low = split(jnp.concatenate(halves, axis=1))
+            edge = edge + dot3(high, low, eh_ref[slot], el_ref[slot])
+            for at, m in enumerate((slot, CLASSES - slot if slot else half)):
+                q = halves[at]
+                turned = pltpu.roll(q, keys, 1)
+                lanes = slice(at * LANES, (at + 1) * LANES)
+                for scale in range(NSCALE):
+                    mine = slice(scale * per_scale, (scale + 1) * per_scale)
+                    high, low = split(
+                        q[mine] * hat_ref[scale, 0, m : m + 1, :]
+                        + turned[mine] * hat_ref[scale, 1, m : m + 1, :]
                     )
-                )
-            q = jnp.concatenate(parts, axis=0)
-            high, low = split(q)
-            edge = edge + dot3(high, low, eh_ref[m], el_ref[m])
-            for scale in range(NSCALE):
-                mine = slice(scale * per_scale, (scale + 1) * per_scale)
-                qr, qi = q[mine, :keys], q[mine, keys:]
-                kr = hat_ref[scale, 0, m : m + 1, :]
-                ki = hat_ref[scale, 1, m : m + 1, :]
-                high, low = split(
-                    jnp.concatenate([qr * kr - qi * ki, qr * ki + qi * kr], axis=1)
-                )
-                qh_ref[m, mine, :] = high
-                ql_ref[m, mine, :] = low
+                    qh_ref[slot, mine, lanes] = high
+                    ql_ref[slot, mine, lanes] = low
         high, low = split(edge)
         for scale in range(NSCALE):
             mine = slice(scale * per_scale, (scale + 1) * per_scale)
-            corr_ref[mine, :] = dot3(high[mine], low[mine], th_ref[scale], tl_ref[scale])
-
-    for m in range(RADIX):
+            cols = slice(scale * 2 * LANES, (scale + 1) * 2 * LANES)
+            corr_ref[mine, :] = dot3(high[mine], low[mine], th_ref[:, cols], tl_ref[:, cols])
+
+    for m in range(CLASSES // 2):
         v_ref[m] = dot3(qh_ref[m], ql_ref[m], fh_ref[0, m], fl_ref[0, m])
 
     slot = lax.rem(t, 2)
@@ -513,60 +592,37 @@
 
     @pl.when(t >= 2)
     def reuse():
-        for at in range(RADIX):
+        for at in range(CLASSES):
             copy(slot, t - 2, at).wait()
 
-    step = 16
+    step = 8
     is_first = (t == 0).astype(F32)
     is_last = (t == tiles - 1).astype(F32)
 
     def combine(n, carry):
         here = pl.ds(pl.multiple_of(n * step, step), step)
-        r = [v_ref[m, here, :LANES] for m in range(RADIX)]
-        i = [v_ref[m, here, LANES:] if m % 4 else None for m in range(RADIX)]
-        s0, s1, s2, s3 = (r[m] + r[m + 4] for m in range(4))
-        d0, d1, d3 = r[0] - r[4], r[1] - r[5], r[3] - r[7]
-        i1, i3 = i[1] + i[5], i[3] + i[7]
-        j1, j2, j3 = i[1] - i[5], i[2] - i[6], i[3] - i[7]
-        a, b, c, d = s0 + s2, s0 - s2, s1 + s3, i1 - i3
-        e, f = d0 - j2, d0 + j2
-        g = ((d1 - j1) - (d3 + j3)) * ROOT_HALF
-        h = ((d1 + j1) - (d3 - j3)) * ROOT_HALF
-        outs = [
-            a + c - is_first * corr_ref[here, :LANES],
-            e + g,
-            b - d,
-            f - h,
-            a - c,
-            e - g,
-            b + d,
-            f + h - is_last * corr_ref[here, LANES:],
-        ]
-        for at in range(RADIX):
+        x = [v_ref[m, here, :LANES] for m in range(CLASSES // 2)]
+        y = [v_ref[m, here, LANES:] for m in range(CLASSES // 2)]
+        outs = real_sixteen(x[0], y[0], x, y)
+        outs[0] = outs[0] - is_first * corr_ref[here, :LANES]
+        outs[-1] = outs[-1] - is_last * corr_ref[here, LANES:]
+        for at in range(CLASSES):
             o_ref[slot, at, here, :] = outs[at]
         return carry
 
-    lax.fori_loop(0, width // step, combine, 0)
-    for at in range(RADIX):
+    lax.fori_loop(0, width // step, combine, 0, unroll=4)
+    for at in range(CLASSES):
         copy(slot, t, at).start()
 
     @pl.when(t == tiles - 1)
     def finish():
-        for at in range(RADIX):
+        for at in range(CLASSES):
             copy(1 - slot, t - 1, at).wait()
             copy(slot, t, at).wait()
 
 
 def whole(shape):
     return pl.BlockSpec(shape, lambda *_: (0,) * len(shape))
-
-
-def spread_taps(index, scale_kernels):
-    index = jnp.asarray(index, jnp.int32)[None]
-    out = jnp.zeros((NSCALE,) + index.shape[1:], F32)
-    for u in range(KW):
-        out = jnp.where(index == u, scale_kernels[:, u][:, None, None], out)
-    return out
 
 
 def kernel_device(
@@ -584,18 +640,19 @@
     subs = subgrid_col.shape[0]
     width = NSCALE * cols_here
 
-    shifts = [[(i, (i + d) % nc) for i in range(nc)] for d in range(1, nc)]
-    info = jnp.stack([subgrid_tile[:, 0] * tile_width + subgrid_col, subgrid_group[:, 0]])
-    infos = jnp.concatenate([info] + [lax.ppermute(info, "col", s) for s in shifts], axis=1)
-
-    rotated = jnp.stack(rotated_visibilities(vis, vis_w))
+    corner = subgrid_tile[:, 0] * tile_width + subgrid_col
+    info = jnp.concatenate([corner, subgrid_group[:, 0]]).astype(F32)
+    info = jnp.pad(info, (0, LANES - info.shape[0]))[None]
+    rows_of_pairs = subs // 2 * SUB
     subgrids = pl.pallas_call(
         subgrid_kernel,
-        out_shape=jax.ShapeDtypeStruct((subs // 2 * SUB, LANES), F32),
+        out_shape=jax.ShapeDtypeStruct((rows_of_pairs + 8, LANES), F32),
         compiler_params=pltpu.CompilerParams(vmem_limit_bytes=32 * 2**20),
         name="subgrids",
-    )(vis_pos, rotated, grid_kernel.T)
+    )(vis_pos, vis, vis_w[None], grid_kernel, info)
+    shifts = [[(i, (i + d) % nc) for i in range(nc)] for d in range(1, nc)]
     blocks = [subgrids] + [lax.ppermute(subgrids, "col", s) for s in shifts]
+    infos = jnp.concatenate([b[rows_of_pairs : rows_of_pairs + 1] for b in blocks], axis=0)
 
     inner = np.arange(part)
     cosine, sine = turn(
@@ -631,48 +688,67 @@
     distance = np.where((distance >= 0) & (distance < KW), distance, -1)
     at_q = (row * nc + col) * cols_here - HALO + jnp.asarray(place, jnp.int32)
     inside = ((at_q >= 0) & (at_q < G)).astype(F32) * (1.0 / G)
-    across = spread_taps(distance, scale_kernels) * inside[None, :, None]
-    across = jnp.concatenate([across[m] for m in range(NSCALE)], axis=1)
-    bh, bl = split_outside(across)
-    per_band = LANES // RADIX // nc
-    keys = (
-        np.arange(nr)[:, None, None] * stride
-        + np.arange(nc)[None, :, None] * (stride // nc)
-        + np.arange(per_band)[None, None, :] * RADIX
-    ).reshape(-1)
-    k_of = np.arange(RADIX)[:, None] + keys[None, :]
-    cosine, sine = turn((np.arange(KW) - HALO)[:, None] * k_of.reshape(1, -1), G)
-    hat = jnp.dot(
-        scale_kernels,
-        jnp.asarray(np.concatenate([cosine, sine], axis=1), F32),
-        precision=HIGHEST,
-    ).reshape(NSCALE, 2, RADIX, keys.size)
-    near = np.arange(-HALO, HALO)
-    cosine, sine = turn(k_of[:, :, None] * near, G)
-    edge = np.zeros((RADIX, 2 * keys.size, LANES))
-    edge[:, : keys.size, : 2 * HALO] = cosine
-    edge[:, keys.size :, : 2 * HALO] = -sine
-    eh, el = split_table(edge)
     wrap = np.full((LANES, 2 * LANES), -1)
     for e in range(HALO):
         for p in range(e + 1):
             wrap[e, p] = e - p
         for j in range(e, HALO):
             wrap[HALO + e, 2 * LANES - HALO + j] = e + 2 * HALO - j
-    th, tl = split_outside(spread_taps(wrap, scale_kernels))
-    tiles = part // LANES
-    cosine, sine = turn(k_of[:, :, None] * np.arange(part), G)
-    table = np.concatenate(
+    across, th, tl = pl.pallas_call(
+        band_kernel,
+        out_shape=[jax.ShapeDtypeStruct((3 * window, width), BF16)]
+        + [jax.ShapeDtypeStruct((LANES, NSCALE * 2 * LANES), BF16)] * 2,
+        in_specs=[pl.BlockSpec(memory_space=pltpu.SMEM)] + [vmem] * 3,
+        out_specs=[vmem] * 3,
+        compiler_params=pltpu.CompilerParams(vmem_limit_bytes=32 * 2**20),
+        name="bands",
+    )(
+        scale_kernels,
+        jnp.asarray(distance, jnp.int32),
+        jnp.asarray(wrap, jnp.int32),
+        inside[:, None],
+    )
+    per_band = LANES // CLASSES // nc
+    keys = (
+        np.arange(nr)[:, None, None] * stride
+        + np.arange(nc)[None, :, None] * (stride // nc)
+        + np.arange(per_band)[None, None, :] * CLASSES
+    ).reshape(-1)
+    k_of = np.arange(CLASSES)[:, None] + keys[None, :]
+    cosine, sine = turn((np.arange(KW) - HALO)[:, None, None] * k_of, G)
+    hat_table = np.stack(
         [
-            np.stack([cosine, sine], axis=2),
-            np.stack([-sine, cosine], axis=2),
+            np.concatenate([cosine, cosine], axis=2),
+            np.concatenate([-sine, sine], axis=2),
         ],
         axis=1,
     )
-    table = table.reshape(RADIX, 2 * keys.size, 2, tiles, LANES).transpose(3, 0, 1, 2, 4)
-    fh, fl = split_table(table.reshape(tiles, RADIX, 2 * keys.size, 2 * LANES))
-    table_spec = pl.BlockSpec((1, RADIX, 2 * keys.size, 2 * LANES), lambda t: (t, 0, 0, 0))
-    operands = (rows, bh, bl, hat, jnp.asarray(eh), jnp.asarray(el), th, tl)
+    hat = jnp.dot(
+        scale_kernels, jnp.asarray(hat_table.reshape(KW, -1), F32), precision=HIGHEST
+    ).reshape(NSCALE, 2, CLASSES, 2 * keys.size)
+    near = np.arange(-HALO, HALO)
+    cosine, sine = turn(k_of[:, :, None] * near, G)
+    edge = np.zeros((CLASSES, 2 * keys.size, LANES))
+    edge[:, : keys.size, : 2 * HALO] = cosine
+    edge[:, keys.size :, : 2 * HALO] = -sine
+    half = CLASSES // 2
+    others = [CLASSES - m if m else half for m in range(half)]
+    eh, el = split_table(np.concatenate([edge[:half], edge[others]], axis=1))
+    span = G // CLASSES
+    tiles = span // LANES
+    cosine, sine = turn(k_of[:, :, None] * np.arange(span), G)
+    real = np.concatenate([cosine, -sine], axis=1)
+    imag = np.concatenate([sine, cosine], axis=1)
+    none = np.zeros_like(real[0])
+    table = [np.block([[real[0], none], [none, real[half]]])]
+    for m in range(1, half):
+        other = CLASSES - m
+        table.append(np.block([[real[m], imag[m]], [real[other], -imag[other]]]))
+    table = np.stack(table).reshape(half, 4 * keys.size, 2, tiles, LANES)
+    table = table.transpose(3, 0, 1, 2, 4).reshape(tiles, half, 4 * keys.size, 2 * LANES)
+    fh, fl = split_table(table)
+    table_spec = pl.BlockSpec((1,) + table.shape[1:], lambda t: (t, 0, 0, 0))
+    operands = (rows, across, hat, jnp.asarray(eh), jnp.asarray(el), th, tl)
     out = pl.pallas_call(
         column_kernel,
         grid=(tiles,),
@@ -681,12 +757,12 @@
         out_specs=pl.BlockSpec(memory_space=pl.ANY),
         scratch_shapes=[
             pltpu.VMEM((2, width // LANES, nr * LANES, LANES), F32),
-            pltpu.VMEM((RADIX, width, 2 * keys.size), BF16),
-            pltpu.VMEM((RADIX, width, 2 * keys.size), BF16),
+            pltpu.VMEM((half, width, 4 * keys.size), BF16),
+            pltpu.VMEM((half, width, 4 * keys.size), BF16),
             pltpu.VMEM((width, 2 * LANES), F32),
-            pltpu.VMEM((RADIX, width, 2 * LANES), F32),
-            pltpu.VMEM((2, RADIX, width, LANES), F32),
-            pltpu.SemaphoreType.DMA((2, RADIX)),
+            pltpu.VMEM((half, width, 2 * LANES), F32),
+            pltpu.VMEM((2, CLASSES, width, LANES), F32),
+            pltpu.SemaphoreType.DMA((2, CLASSES)),
         ],
         compiler_params=pltpu.CompilerParams(vmem_limit_bytes=56 * 2**20),
         name="columns",

time: 170 us -> 113 us (0.66)
  local copies, waits for them, and re-layouts: 65.4 us -> 11.1 us
  waiting for transfers between devices: 10.9 us -> 43.4 us
  Pallas kernels: 59.9 us -> 45.3 us
  starting transfers between devices: 20 us -> 10.1 us
  other arithmetic: 10 us -> 1.42 us
    unnamed x209 -> x31, local copies, waits for them, and re-layouts: 62.4 us -> 9.93 us
    all_to_all x1, waiting for transfers between devices: 0.01 us -> 22.9 us  [kernel_device(): rows = lax.all_to_all(rows, 'row', split_axis=0, concat_axis=0, tiled=True)]
    ppermute x3, waiting for transfers between devices: 0.01 us -> 20.6 us  [kernel_device(): blocks = [subgrids] + [lax.ppermute(subgrids, 'col', s) for s in shifts]]
    ppermute x3 -> x0, waiting for transfers between devices: 10.9 us -> none  [kernel_device(): lax.ppermute(info, 'col', s)]
    ppermute x3 -> x0, starting transfers between devices: 9.93 us -> none  [kernel_device(): lax.ppermute(info, 'col', s)]
    pallas_call x1, Pallas kernels: 30.2 us -> 22.1 us  [kernel_device(): pl.pallas_call(column_kernel, grid=(tiles,), out_shape=jax.ShapeDtypeStru...]
    pallas_call x1, Pallas kernels: 23.5 us -> 17 us  [kernel_device(): pl.pallas_call(lambda *refs: row_kernel(*refs, blocks=nc, part=part, per_...]
    mul x1 -> x0, other arithmetic: 3.72 us -> none  [kernel_device(): across = spread_taps(distance, scale_kernels) * inside[None, :, None]]
  transfers between devices with their start and end apart: 7 -> 4, of which waited for: 2 -> 3; matrix products, arithmetic and copies ran while one was open for 41% -> 2% of each run, Pallas kernels for 0% -> 3%
where the time goes in v2:
time: 113 us; the launch traced here: 112 us
  Pallas kernels  45.3 us (40%)
  waiting for transfers between devices  43.4 us (38%)
  local copies, waits for them, and re-layouts  11.1 us (10%)
  starting transfers between devices  10.1 us (9%)
  other arithmetic  1.42 us (1%)
    all_to_all x1, waiting for transfers between devices, kernel_device(): rows = lax.all_to_all(rows, 'row', split_axis=0, concat_axis=0, tiled=True)  22.9 us
    pallas_call x1, Pallas kernels, kernel_device(): pl.pallas_call(column_kernel, grid=(tiles,), out_shape=jax.ShapeDtypeStru...  22.1 us
    ppermute x3, waiting for transfers between devices, kernel_device(): blocks = [subgrids] + [lax.ppermute(subgrids, 'col', s) for s in shifts]  20.6 us
    pallas_call x1, Pallas kernels, kernel_device(): pl.pallas_call(lambda *refs: row_kernel(*refs, blocks=nc, part=part, per_...  17 us
    unnamed x31, local copies, waits for them, and re-layouts  9.93 us
    ppermute x3, starting transfers between devices, kernel_device(): blocks = [subgrids] + [lax.ppermute(subgrids, 'col', s) for s in shifts]  6.11 us
    all_to_all x1, starting transfers between devices, kernel_device(): rows = lax.all_to_all(rows, 'row', split_axis=0, concat_axis=0, tiled=True)  3.94 us
    pallas_call x1, Pallas kernels, kernel_device(): pl.pallas_call(subgrid_kernel, out_shape=jax.ShapeDtypeStruct((rows_of_pa...  3.26 us
  transfers between devices with their start and end apart: 4, of which 3 were waited for; matrix products, arithmetic and copies ran while one was open for 2% of the time, Pallas kernels for 3%

profile of v2, /device:TPU:0, one launch (start us, length us, event | category | flops | bytes accessed | tf_op | source)
XLA Modules:
  0.0 112.1 jit_solution(16806733491755998785)
XLA Ops:
  0.0 0.7 bitcast_add_fusion
  0.7 0.7 add_convert_fusion
  1.4 0.0 copy-start.7
  1.4 0.8 copy-done.7
  2.3 0.0 copy-start.8
  2.3 0.8 copy-done.8
  3.1 0.0 copy-start.9
  3.1 0.8 copy-done.9
  3.9 0.0 copy-start.10
  3.9 0.7 copy-done.10
  4.5 3.3 %subgrids.1.refs_1_ = f32[520,128]{1,0:T(8,128)S(1)} custom-call(s32[2,8192]{1,0:T(2,128)S(1)} %copy-done.7, f32[2,8192]{1,0:T(2,128)S(1)} %copy-done.8, s32[1,8192]{1,0:T(1,128)S(1)} %bitcast.16, f32[8,8]{1,0:T(8,128)S(1)} %copy-done.10, f32[1,128]{1,0:T(1,128)S(1)} %pad_bitcast_fusion.info_ref), custom_call_target="tpu_custom_call" | custom-call | tf_op jit(solution)/shard_map/subgrids/pallas_call | solution.py:647
  7.8 5.1 %collective-permute-start.2 = (f32[520,128]{1,0:T(8,128)S(1)}, f32[520,128]{1,0:T(8,128)S(1)}, u32[]{:S(2)}, u32[]{:S(2)}) collective-permute-start(f32[520,128]{1,0:T(8,128)S(1)} %subgrids.1.refs_1_), channel_id=1, source_target_pairs={{0,3},{1,0},{2,1},{3,2},{4,7},{5,4},{6,5},{7,6},{8,11},{9,8},{10,9... | collective-permute-start | bytes 798728 | tf_op jit(solution)/shard_map/ppermute | solution.py:654
  12.9 0.0 collective-permute-start.1
  12.9 1.0 collective-permute-start
  13.9 1.1 dynamic-slice_bitcast_fusion.refs_5_
  15.0 4.7 %collective-permute-done.2.refs_4_ = f32[520,128]{1,0:T(8,128)S(1)} collective-permute-done((f32[520,128]{1,0:T(8,128)S(1)}, f32[520,128]{1,0:T(8,128)S(1)}, u32[]{:S(2)}, u32[]{:S(2)}) %collective-permute-start.2) | collective-permute-done | bytes 266272 | tf_op jit(solution)/shard_map/ppermute | solution.py:654
  19.8 15.8 %collective-permute-done.1.refs_3_ = f32[520,128]{1,0:T(8,128)S(1)} collective-permute-done((f32[520,128]{1,0:T(8,128)S(1)}, f32[520,128]{1,0:T(8,128)S(1)}, u32[]{:S(2)}, u32[]{:S(2)}) %collective-permute-start.1) | collective-permute-done | bytes 266272 | tf_op jit(solution)/shard_map/ppermute | solution.py:654
  35.6 0.0 collective-permute-done.refs_2_
  35.6 0.0 copy-start
  35.6 1.3 %copy-done = bf16[576,1024]{1,0:T(8,128)(2,1)S(1)} copy-done((bf16[576,1024]{1,0:T(8,128)(2,1)S(1)}, bf16[576,1024]{1,0:T(8,128)(2,1)}, u32[]{:S(2)}) %copy-start) | copy-done | bytes 1179672
  36.9 0.0 copy-start.1
  36.9 1.3 %copy-done.1 = bf16[576,1024]{1,0:T(8,128)(2,1)S(1)} copy-done((bf16[576,1024]{1,0:T(8,128)(2,1)S(1)}, bf16[576,1024]{1,0:T(8,128)(2,1)}, u32[]{:S(2)}) %copy-start.1) | copy-done | bytes 1179672
  38.1 17.0 %rows.1 = f32[8,288,256]{2,1,0:T(8,128)} custom-call(f32[4,128]{1,0:T(4,128)S(1)} %pad_maximum_fusion.refs_0_, f32[520,128]{1,0:T(8,128)S(1)} %subgrids.1.refs_1_, f32[520,128]{1,0:T(8,128)S(1)} %collective-permute-done.refs_2_, f32[520,128]{1,0:T(8,128)S(1)} %collective-permute-done.1.refs_3_, f32[520,128]{1,0:T(8,128)S(1)} %collective-permute-done.2.refs_4_, ...), custom_call_target="tpu_custom_call" | custom-call | tf_op jit(solution)/shard_map/rows/pallas_call | solution.py:669
  55.2 0.0 copy-start.11
  55.2 0.0 copy-start.13
  55.2 0.0 copy-start.14
  55.2 0.0 copy-start.3
  55.2 0.0 copy-start.6
  55.2 3.9 %all-to-all-start = ((f32[8,288,256]{2,1,0:T(8,128)}), f32[8,288,256]{2,1,0:T(8,128)S(1)}, u32[]{:S(2)}, u32[]{:S(2)}) async-start(f32[8,288,256]{2,1,0:T(8,128)} %rows.1), calls=%async_computation | async-start | bytes 4718592 | tf_op jit(solution)/shard_map/all_to_all | solution.py:684
  59.1 0.0 copy-done.11
  59.1 0.0 copy-done.13
  59.2 0.5 convolution_bitcast_fusion
  59.6 0.6 copy.21
  60.2 0.0 copy-done.14
  60.3 0.1 broadcast_in_dim.12.inside_ref
  60.4 0.0 copy-done.3
  60.4 0.0 copy-done.6
  60.4 3.0 %bands.1 = (bf16[864,512]{1,0:T(8,128)(2,1)S(1)}, bf16[128,512]{1,0:T(8,128)(2,1)S(1)}, bf16[128,512]{1,0:T(8,128)(2,1)S(1)}) custom-call(f32[2,33]{1,0:T(2,128)S(1)} %copy-done.11, s32[288,256]{1,0:T(8,128)S(1)} %copy-done.3, s32[128,256]{1,0:T(8,128)S(1)} %copy-done.6, f32[288,1]{1,0:T(8,128)S(1)} %broadcast_in_dim.12.inside_ref), custom_call_target="tpu_custom_call" | custom-call | tf_op jit(solution)/shard_map/bands/pallas_call | solution.py:697
  63.4 0.0 copy-start.2
  63.4 0.9 copy-done.2
  64.3 0.0 copy-start.4
  64.3 0.6 copy-done.4
  65.0 0.0 copy-start.5
  65.0 0.7 copy-done.5
  65.6 22.9 %all-to-all-done.rows_ref = f32[8,288,256]{2,1,0:T(8,128)S(1)} async-done(((f32[8,288,256]{2,1,0:T(8,128)}), f32[8,288,256]{2,1,0:T(8,128)S(1)}, u32[]{:S(2)}, u32[]{:S(2)}) %all-to-all-start) | async-done | bytes 2359328 | tf_op jit(solution)/shard_map/all_to_all | solution.py:684
  88.5 0.0 copy-start.12
  88.5 1.4 %copy-done.12 = f32[8,288,256]{2,1,0:T(8,128)} copy-done((f32[8,288,256]{2,1,0:T(8,128)}, f32[8,288,256]{2,1,0:T(8,128)S(1)}, u32[]{:S(2)}) %copy-start.12) | copy-done | bytes 2359320
  89.9 22.1 %columns.1 = f32[512,8192]{1,0:T(8,128)} custom-call(f32[8,288,256]{2,1,0:T(8,128)} %copy-done.12, bf16[864,512]{1,0:T(8,128)(2,1)} %copy-done.2, f32[2,2,16,128]{3,2,1,0:T(8,128)} %bitcast.17, bf16[8,256,128]{2,1,0:T(8,128)(2,1)} %constant.61.clone.eh_ref, bf16[8,256,128]{2,1,0:T(8,128)(2,1)} %constant.62.clone.el_ref, bf16[128,512]{1,0:T(8,128)(2,1)} %copy-done.4, ...), custom_call_target="tpu_custom_call" | custom-call | tf_op jit(solution)/shard_map/columns/pallas_call | solution.py:752
  (7 shorter events, 0.0 us)
Async XLA Ops:
  1.4 0.8 copy-start.7
  2.3 0.8 copy-start.8
  3.1 0.8 copy-start.9
  3.9 0.7 copy-start.10
  7.8 11.9 %collective-permute-start.2 = (f32[520,128]{1,0:T(8,128)S(1)}, f32[520,128]{1,0:T(8,128)S(1)}, u32[]{:S(2)}, u32[]{:S(2)}) collective-permute-start(f32[520,128]{1,0:T(8,128)S(1)} %subgrids.1.refs_1_), channel_id=1, source_target_pairs={{0,3},{1,0},{2,1},{3,2},{4,7},{5,4},{6,5},{7,6},{8,11},{9,8},{10,9... | collective-permute-start | bytes 798728 | tf_op jit(solution)/shard_map/ppermute | solution.py:654
  12.9 22.7 %collective-permute-start.1 = (f32[520,128]{1,0:T(8,128)S(1)}, f32[520,128]{1,0:T(8,128)S(1)}, u32[]{:S(2)}, u32[]{:S(2)}) collective-permute-start(f32[520,128]{1,0:T(8,128)S(1)} %subgrids.1.refs_1_), channel_id=1, source_target_pairs={{0,2},{1,3},{2,0},{3,1},{4,6},{5,7},{6,4},{7,5},{8,10},{9,11},{10,... | collective-permute-start | bytes 798728 | tf_op jit(solution)/shard_map/ppermute | solution.py:654
  12.9 22.7 %collective-permute-start = (f32[520,128]{1,0:T(8,128)S(1)}, f32[520,128]{1,0:T(8,128)S(1)}, u32[]{:S(2)}, u32[]{:S(2)}) collective-permute-start(f32[520,128]{1,0:T(8,128)S(1)} %subgrids.1.refs_1_), channel_id=1, source_target_pairs={{0,1},{1,2},{2,3},{3,0},{4,5},{5,6},{6,7},{7,4},{8,9},{9,10},{10,1... | collective-permute-start | bytes 798728 | tf_op jit(solution)/shard_map/ppermute | solution.py:654
  35.6 1.3 %copy-start = (bf16[576,1024]{1,0:T(8,128)(2,1)S(1)}, bf16[576,1024]{1,0:T(8,128)(2,1)}, u32[]{:S(2)}) copy-start(bf16[576,1024]{1,0:T(8,128)(2,1)} %constant.56.clone.refs_7_) | copy-start | bytes 3538948
  36.9 1.3 %copy-start.1 = (bf16[576,1024]{1,0:T(8,128)(2,1)S(1)}, bf16[576,1024]{1,0:T(8,128)(2,1)}, u32[]{:S(2)}) copy-start(bf16[576,1024]{1,0:T(8,128)(2,1)} %constant.55.clone.refs_6_) | copy-start | bytes 3538948
  55.2 4.0 %copy-start.11 = (f32[2,33]{1,0:T(2,128)S(1)}, f32[2,33]{1,0:T(2,128)}, u32[]{:S(2)}) copy-start(f32[2,33]{1,0:T(2,128)} %taps_ref.3) | copy-start | bytes 796
  55.2 4.0 %copy-start.13 = (f32[33,4096]{1,0:T(8,128)S(1)}, f32[33,4096]{1,0:T(8,128)}, u32[]{:S(2)}) copy-start(f32[33,4096]{1,0:T(8,128)} %constant.60.clone) | copy-start | bytes 1622020
  55.2 5.1 %copy-start.14 = (s32[288]{0:T(512)S(1)}, s32[288]{0:T(512)}, u32[]{:S(2)}) copy-start(s32[288]{0:T(512)} %constant.57.clone) | copy-start | bytes 3460
  55.2 5.2 %copy-start.3 = (s32[288,256]{1,0:T(8,128)S(1)}, s32[288,256]{1,0:T(8,128)}, u32[]{:S(2)}) copy-start(s32[288,256]{1,0:T(8,128)} %constant.58.clone.across_ref) | copy-start | bytes 884740
  55.2 5.2 %copy-start.6 = (s32[128,256]{1,0:T(8,128)S(1)}, s32[128,256]{1,0:T(8,128)}, u32[]{:S(2)}) copy-start(s32[128,256]{1,0:T(8,128)} %constant.59.clone.wrap_ref) | copy-start | bytes 393220
  55.2 33.3 %all-to-all-start = ((f32[8,288,256]{2,1,0:T(8,128)}), f32[8,288,256]{2,1,0:T(8,128)S(1)}, u32[]{:S(2)}, u32[]{:S(2)}) async-start(f32[8,288,256]{2,1,0:T(8,128)} %rows.1), calls=%async_computation | async-start | bytes 4718592 | tf_op jit(solution)/shard_map/all_to_all | solution.py:684
  63.4 0.9 copy-start.2
  64.3 0.6 copy-start.4
  65.0 0.7 copy-start.5
  88.5 1.4 %copy-start.12 = (f32[8,288,256]{2,1,0:T(8,128)}, f32[8,288,256]{2,1,0:T(8,128)S(1)}, u32[]{:S(2)}) copy-start(f32[8,288,256]{2,1,0:T(8,128)S(1)} %all-to-all-done.rows_ref) | copy-start | bytes 7077892

commit v3 on v2

--- a/solution.py
+++ b/solution.py
@@ -321,26 +321,9 @@
     )
 
 
-def turned_back(steps):
-    quarter = WSTEPS // 4
-    turns = (steps + quarter // 2) >> (quarter.bit_length() - 1)
-    angle = (steps - turns * quarter).astype(F32) * (2.0 * math.pi / WSTEPS)
-    square = angle * angle
-    cosine = 1.0 + square * (
-        -1 / 2 + square * (1 / 24 + square * (-1 / 720 + square * (1 / 40320 - square / 3628800)))
-    )
-    sine = angle * (
-        1.0 + square * (-1 / 6 + square * (1 / 120 + square * (-1 / 5040 + square / 362880)))
-    )
-    odd = (turns & 1) == 1
-    first, second = jnp.where(odd, sine, cosine), jnp.where(odd, cosine, sine)
-    first = jnp.where(((turns + 1) & 2) == 2, -first, first)
-    return first, jnp.where((turns & 2) == 2, -second, second)
-
-
-def subgrid_kernel(pos_ref, vis_ref, phase_ref, taps_ref, info_ref, out_ref):
+def subgrid_kernel(packed_ref, taps_ref, out_ref):
     span = 2 * VPS
-    pairs = vis_ref.shape[1] // span
+    pairs = out_ref.shape[0] // SUB
     diagonal = lax.broadcasted_iota(jnp.int32, (OVER, SUP), 0) == lax.broadcasted_iota(
         jnp.int32, (OVER, SUP), 1
     )
@@ -365,16 +348,10 @@
 
     def pair(p, carry):
         here = pl.ds(pl.multiple_of(p * span, span), span)
-        along_rows = taps(pos_ref[0:1, here])
-        along_cols = taps(pos_ref[1:2, here])
-        cosine, sine = turned_back(phase_ref[0:1, here])
-        real, imag = vis_ref[0:1, here], vis_ref[1:2, here]
+        along_rows = taps(packed_ref[2:3, here].astype(jnp.int32))
+        along_cols = taps(packed_ref[3:4, here].astype(jnp.int32))
         weighted = jnp.concatenate(
-            [
-                along_rows * (real * cosine + imag * sine),
-                along_rows * (imag * cosine - real * sine),
-            ],
-            axis=0,
+            [along_rows * packed_ref[0:1, here], along_rows * packed_ref[1:2, here]], axis=0
         )
         weighted = jnp.concatenate(split(weighted), axis=0)
         cols = jnp.concatenate(split(along_cols), axis=0)
@@ -387,10 +364,7 @@
         out_ref[pl.ds(pl.multiple_of(p * SUB, SUB), SUB), :] = jnp.where(first, sums[0], sums[1])
         return carry
 
-    lax.fori_loop(0, pairs, pair, 0, unroll=4)
-    out_ref[pairs * SUB :, :] = jnp.broadcast_to(
-        info_ref[...], (out_ref.shape[0] - pairs * SUB, LANES)
-    )
+    lax.fori_loop(0, pairs, pair, 0, unroll=8)
 
 
 def radix_eight(real, imag):
@@ -413,11 +387,11 @@
     return [(low, high)[c % 2][c // 2] for c in range(8)]
 
 
-def row_kernel(
-    info_ref, *refs, blocks, part, per_class
-):
+def row_kernel(info_ref, *refs, blocks, part, per_class, tile_width):
     xs = refs[:blocks]
-    turn_ref, high_ref, low_ref, out_ref, real_ref, imag_ref, uh_ref, ul_ref = refs[blocks:]
+    turn_ref, tables_ref, out_ref, real_ref, imag_ref, uh_ref, ul_ref, both_ref, sem = refs[blocks:]
+    fetch = pltpu.make_async_copy(tables_ref, both_ref, sem)
+    fetch.start()
     rows = real_ref.shape[0]
     chunk = 256
 
@@ -435,8 +409,11 @@
         def place(p, carry, b=b, pairs=pairs):
             piece = xs[b][pl.ds(pl.multiple_of(p * SUB, SUB), SUB), :]
             for s in range(2):
-                start = info_ref[b, 2 * p + s].astype(jnp.int32)
-                group = info_ref[b, 2 * pairs + 2 * p + s].astype(jnp.int32)
+                number = 2 * p + s
+                tile, group, start = (
+                    info_ref[b, n * 2 * pairs + number].astype(jnp.int32) for n in range(3)
+                )
+                start = tile * tile_width + start
                 for dest, at in ((real_ref, 2 * s), (imag_ref, 2 * s + 1)):
                     shift = (group * SUB + (LANES - at * SUB)) & (LANES - 1)
                     moved = jnp.where(owner == group, pltpu.roll(piece, shift, 1), 0.0)
@@ -465,8 +442,9 @@
     lax.fori_loop(0, part // step, classes, 0, unroll=4)
     dests = out_ref.shape[0]
     half = dests * per_class
+    fetch.wait()
     for c in range(RADIX):
-        total = dot3(high_ref[...], low_ref[...], uh_ref[c], ul_ref[c])
+        total = dot3(both_ref[0], both_ref[1], uh_ref[c], ul_ref[c])
         real = total[:half, :LANES] - total[half:, LANES:]
         imag = total[:half, LANES:] + total[half:, :LANES]
         for d in range(dests):
@@ -528,101 +506,104 @@
 
 
 def column_kernel(
-    rows_ref, across_ref, hat_ref, eh_ref, el_ref, th_ref, tl_ref, fh_ref, fl_ref,
-    out_ref, qt_ref, qh_ref, ql_ref, corr_ref, v_ref, o_ref, sem,
+    rows_ref, across_ref, hat_ref, th_ref, tl_ref, tables_ref,
+    out_ref, qt_ref, qh_ref, ql_ref, corr_ref, va_ref, vb_ref, o_ref, f_ref, sem, table_sem,
 ):
-    t = pl.program_id(0)
-    tiles = pl.num_programs(0)
+    tiles = tables_ref.shape[0] - 1
+    fetches = [
+        pltpu.make_async_copy(tables_ref.at[n], f_ref.at[n], table_sem.at[n])
+        for n in range(tiles + 1)
+    ]
+    for fetch in fetches:
+        fetch.start()
     bands = rows_ref.shape[0]
     width = qh_ref.shape[1]
     per_scale = width // NSCALE
     keys = LANES // 2
-
-    @pl.when(t == 0)
-    def prepare():
-        for i in range(bands):
-            high, low = split(rows_ref[i])
-            product = dot(jnp.concatenate([high, low, high], axis=0), across_ref[...], 0, 0)
+    half = CLASSES // 2
+
+    for i in range(bands):
+        high, low = split(rows_ref[i])
+        product = dot(jnp.concatenate([high, low, high], axis=0), across_ref[...], 0, 0)
+        for lane in range(width // LANES):
+            cols = slice(lane * LANES, (lane + 1) * LANES)
+            qt_ref[0, lane, i * LANES : (i + 1) * LANES, :] = product[:LANES, cols]
+            qt_ref[1, lane, i * LANES : (i + 1) * LANES, :] = product[LANES:, cols]
+    edge = jnp.zeros((width, LANES), F32)
+    fetches[0].wait()
+    for slot in range(half):
+        halves = []
+        for m in (slot, CLASSES - slot if slot else half):
+            parts = []
             for lane in range(width // LANES):
-                cols = slice(lane * LANES, (lane + 1) * LANES)
-                qt_ref[0, lane, i * LANES : (i + 1) * LANES, :] = product[:LANES, cols]
-                qt_ref[1, lane, i * LANES : (i + 1) * LANES, :] = product[LANES:, cols]
-        edge = jnp.zeros((width, LANES), F32)
-        half = CLASSES // 2
-        for slot in range(half):
-            halves = []
-            for m in (slot, CLASSES - slot if slot else half):
-                parts = []
-                for lane in range(width // LANES):
-                    here = pl.ds(m, keys, stride=CLASSES)
-                    pair = [qt_ref[ri, lane, here, :] for ri in range(2)]
-                    parts.append(jnp.concatenate(pair, axis=0).T)
-                halves.append(jnp.concatenate(parts, axis=0))
-            high, low = split(jnp.concatenate(halves, axis=1))
-            edge = edge + dot3(high, low, eh_ref[slot], el_ref[slot])
-            for at, m in enumerate((slot, CLASSES - slot if slot else half)):
-                q = halves[at]
-                turned = pltpu.roll(q, keys, 1)
-                lanes = slice(at * LANES, (at + 1) * LANES)
-                for scale in range(NSCALE):
-                    mine = slice(scale * per_scale, (scale + 1) * per_scale)
-                    high, low = split(
-                        q[mine] * hat_ref[scale, 0, m : m + 1, :]
-                        + turned[mine] * hat_ref[scale, 1, m : m + 1, :]
-                    )
-                    qh_ref[slot, mine, lanes] = high
-                    ql_ref[slot, mine, lanes] = low
-        high, low = split(edge)
-        for scale in range(NSCALE):
-            mine = slice(scale * per_scale, (scale + 1) * per_scale)
-            cols = slice(scale * 2 * LANES, (scale + 1) * 2 * LANES)
-            corr_ref[mine, :] = dot3(high[mine], low[mine], th_ref[:, cols], tl_ref[:, cols])
-
-    for m in range(CLASSES // 2):
-        v_ref[m] = dot3(qh_ref[m], ql_ref[m], fh_ref[0, m], fl_ref[0, m])
-
-    slot = lax.rem(t, 2)
-
-    def copy(which, tile, at):
+                here = pl.ds(m, keys, stride=CLASSES)
+                pair = [qt_ref[ri, lane, here, :] for ri in range(2)]
+                parts.append(jnp.concatenate(pair, axis=0).T)
+            halves.append(jnp.concatenate(parts, axis=0))
+        high, low = split(jnp.concatenate(halves, axis=1))
+        edge = edge + dot3(
+            high, low, f_ref[0, 0, slot, :, :LANES], f_ref[0, 1, slot, :, :LANES]
+        )
+        for at, m in enumerate((slot, CLASSES - slot if slot else half)):
+            q = halves[at]
+            turned = pltpu.roll(q, keys, 1)
+            lanes = slice(at * LANES, (at + 1) * LANES)
+            for scale in range(NSCALE):
+                mine = slice(scale * per_scale, (scale + 1) * per_scale)
+                high, low = split(
+                    q[mine] * hat_ref[scale, 0, m : m + 1, :]
+                    + turned[mine] * hat_ref[scale, 1, m : m + 1, :]
+                )
+                qh_ref[slot, mine, lanes] = high
+                ql_ref[slot, mine, lanes] = low
+    high, low = split(edge)
+    for scale in range(NSCALE):
+        mine = slice(scale * per_scale, (scale + 1) * per_scale)
+        cols = slice(scale * 2 * LANES, (scale + 1) * 2 * LANES)
+        corr_ref[mine, :] = dot3(high[mine], low[mine], th_ref[:, cols], tl_ref[:, cols])
+
+    def copy(tile, at):
+        first = (at * tiles + tile) * LANES
         return pltpu.make_async_copy(
-            o_ref.at[which, at],
-            out_ref.at[:, pl.ds(pl.multiple_of((at * tiles + tile) * LANES, LANES), LANES)],
-            sem.at[which, at],
+            o_ref.at[tile % 2, at], out_ref.at[:, first : first + LANES], sem.at[tile % 2, at]
         )
 
-    @pl.when(t >= 2)
-    def reuse():
+    step = 8
+
+    def combine(v_ref, tile, first, last):
+        for n in range(first, last, step):
+            here = slice(n, n + step)
+            x = [v_ref[m, here, :LANES] for m in range(half)]
+            y = [v_ref[m, here, LANES:] for m in range(half)]
+            outs = real_sixteen(x[0], y[0], x, y)
+            if tile == 0:
+                outs[0] = outs[0] - corr_ref[here, :LANES]
+            if tile == tiles - 1:
+                outs[-1] = outs[-1] - corr_ref[here, LANES:]
+            for at in range(CLASSES):
+                o_ref[tile % 2, at, here, :] = outs[at]
+
+    share = width // half
+    for tile in range(tiles + 1):
+        now, before = (va_ref, vb_ref) if tile % 2 == 0 else (vb_ref, va_ref)
+        if tile >= 3:
+            for at in range(CLASSES):
+                copy(tile - 3, at).wait()
+        if tile < tiles:
+            fetches[tile + 1].wait()
+        for m in range(half):
+            if tile < tiles:
+                now[m] = dot3(
+                    qh_ref[m], ql_ref[m], f_ref[tile + 1, 0, m], f_ref[tile + 1, 1, m]
+                )
+            if tile > 0:
+                combine(before, tile - 1, m * share, (m + 1) * share)
+        if tile > 0:
+            for at in range(CLASSES):
+                copy(tile - 1, at).start()
+    for tile in range(max(tiles - 2, 0), tiles):
         for at in range(CLASSES):
-            copy(slot, t - 2, at).wait()
-
-    step = 8
-    is_first = (t == 0).astype(F32)
-    is_last = (t == tiles - 1).astype(F32)
-
-    def combine(n, carry):
-        here = pl.ds(pl.multiple_of(n * step, step), step)
-        x = [v_ref[m, here, :LANES] for m in range(CLASSES // 2)]
-        y = [v_ref[m, here, LANES:] for m in range(CLASSES // 2)]
-        outs = real_sixteen(x[0], y[0], x, y)
-        outs[0] = outs[0] - is_first * corr_ref[here, :LANES]
-        outs[-1] = outs[-1] - is_last * corr_ref[here, LANES:]
-        for at in range(CLASSES):
-            o_ref[slot, at, here, :] = outs[at]
-        return carry
-
-    lax.fori_loop(0, width // step, combine, 0, unroll=4)
-    for at in range(CLASSES):
-        copy(slot, t, at).start()
-
-    @pl.when(t == tiles - 1)
-    def finish():
-        for at in range(CLASSES):
-            copy(1 - slot, t - 1, at).wait()
-            copy(slot, t, at).wait()
-
-
-def whole(shape):
-    return pl.BlockSpec(shape, lambda *_: (0,) * len(shape))
+            copy(tile, at).wait()
 
 
 def kernel_device(
@@ -640,19 +621,38 @@
     subs = subgrid_col.shape[0]
     width = NSCALE * cols_here
 
-    corner = subgrid_tile[:, 0] * tile_width + subgrid_col
-    info = jnp.concatenate([corner, subgrid_group[:, 0]]).astype(F32)
-    info = jnp.pad(info, (0, LANES - info.shape[0]))[None]
-    rows_of_pairs = subs // 2 * SUB
-    subgrids = pl.pallas_call(
-        subgrid_kernel,
-        out_shape=jax.ShapeDtypeStruct((rows_of_pairs + 8, LANES), F32),
-        compiler_params=pltpu.CompilerParams(vmem_limit_bytes=32 * 2**20),
-        name="subgrids",
-    )(vis_pos, vis, vis_w[None], grid_kernel, info)
+    info = jnp.concatenate([subgrid_tile[:, 0], subgrid_group[:, 0], subgrid_col]).astype(F32)
+    info = jnp.pad(info, (0, LANES - info.shape[0]))
+    here = vis.shape[1]
+    packed = jnp.concatenate(
+        [
+            jnp.concatenate(
+                [jnp.stack(rotated_visibilities(vis, vis_w)), vis_pos.astype(F32)], axis=0
+            ),
+            jnp.broadcast_to(info[None], (4, LANES)),
+        ],
+        axis=1,
+    )
     shifts = [[(i, (i + d) % nc) for i in range(nc)] for d in range(1, nc)]
-    blocks = [subgrids] + [lax.ppermute(subgrids, "col", s) for s in shifts]
-    infos = jnp.concatenate([b[rows_of_pairs : rows_of_pairs + 1] for b in blocks], axis=0)
+    packs = [packed] + [lax.ppermute(packed, "col", s) for s in shifts]
+
+    def grid_block(pack):
+        return pl.pallas_call(
+            subgrid_kernel,
+            out_shape=jax.ShapeDtypeStruct((subs // 2 * SUB, LANES), F32),
+            cost_estimate=pl.CostEstimate(
+                flops=2 * 4 * subs * VPS * 4 * SUB * 2 * SUB,
+                bytes_accessed=2**21,
+                transcendentals=0,
+            ),
+            compiler_params=pltpu.CompilerParams(vmem_limit_bytes=32 * 2**20),
+            name="subgrids",
+        )(pack, grid_kernel)
+
+    blocks = [grid_block(pack) for pack in packs[:2]]
+    blocks[1], *packs[2:] = lax.optimization_barrier((blocks[1], *packs[2:]))
+    blocks += [grid_block(pack) for pack in packs[2:]]
+    infos = jnp.concatenate([pack[:1, here:] for pack in packs], axis=0)
 
     inner = np.arange(part)
     cosine, sine = turn(
@@ -660,26 +660,32 @@
         * inner,
         G,
     )
-    table_high, table_low = split_table(np.concatenate([cosine, sine], axis=0))
+    tables = np.stack(split_table(np.concatenate([cosine, sine], axis=0)))
     first_q = np.arange(nc)[:, None, None] * cols_here - HALO
     cosine, sine = turn((first_q + np.arange(RADIX)) * inner[None, :, None], G)
     turns = np.concatenate([cosine, sine], axis=2).astype(np.float32)
     turns = lax.dynamic_index_in_dim(jnp.asarray(turns), col, 0, keepdims=False)
     vmem = pl.BlockSpec(memory_space=pltpu.VMEM)
     rows = pl.pallas_call(
-        lambda *refs: row_kernel(*refs, blocks=nc, part=part, per_class=per_class),
+        lambda *refs: row_kernel(
+            *refs, blocks=nc, part=part, per_class=per_class, tile_width=tile_width
+        ),
         out_shape=jax.ShapeDtypeStruct((nr, window, 2 * LANES), F32),
-        in_specs=[pl.BlockSpec(memory_space=pltpu.SMEM)] + [vmem] * (nc + 3),
+        in_specs=[pl.BlockSpec(memory_space=pltpu.SMEM)]
+        + [vmem] * (nc + 1)
+        + [pl.BlockSpec(memory_space=pl.ANY)],
         out_specs=vmem,
         scratch_shapes=[
             pltpu.VMEM((G, LANES), F32),
             pltpu.VMEM((G, LANES), F32),
             pltpu.VMEM((RADIX, part, 2 * LANES), BF16),
             pltpu.VMEM((RADIX, part, 2 * LANES), BF16),
+            pltpu.VMEM(tables.shape, BF16),
+            pltpu.SemaphoreType.DMA,
         ],
         compiler_params=pltpu.CompilerParams(vmem_limit_bytes=48 * 2**20),
         name="rows",
-    )(infos, *blocks, turns, jnp.asarray(table_high), jnp.asarray(table_low))
+    )(infos, *blocks, turns, jnp.asarray(tables))
 
     rows = lax.all_to_all(rows, "row", split_axis=0, concat_axis=0, tiled=True)
 
@@ -728,12 +734,12 @@
     ).reshape(NSCALE, 2, CLASSES, 2 * keys.size)
     near = np.arange(-HALO, HALO)
     cosine, sine = turn(k_of[:, :, None] * near, G)
-    edge = np.zeros((CLASSES, 2 * keys.size, LANES))
+    edge = np.zeros((CLASSES, 2 * keys.size, 2 * LANES))
     edge[:, : keys.size, : 2 * HALO] = cosine
     edge[:, keys.size :, : 2 * HALO] = -sine
     half = CLASSES // 2
     others = [CLASSES - m if m else half for m in range(half)]
-    eh, el = split_table(np.concatenate([edge[:half], edge[others]], axis=1))
+    edge = np.concatenate([edge[:half], edge[others]], axis=1)
     span = G // CLASSES
     tiles = span // LANES
     cosine, sine = turn(k_of[:, :, None] * np.arange(span), G)
@@ -746,14 +752,12 @@
         table.append(np.block([[real[m], imag[m]], [real[other], -imag[other]]]))
     table = np.stack(table).reshape(half, 4 * keys.size, 2, tiles, LANES)
     table = table.transpose(3, 0, 1, 2, 4).reshape(tiles, half, 4 * keys.size, 2 * LANES)
-    fh, fl = split_table(table)
-    table_spec = pl.BlockSpec((1,) + table.shape[1:], lambda t: (t, 0, 0, 0))
-    operands = (rows, across, hat, jnp.asarray(eh), jnp.asarray(el), th, tl)
+    tables = np.stack(split_table(np.concatenate([edge[None], table], axis=0)), axis=1)
+    operands = (rows, across, hat, th, tl)
     out = pl.pallas_call(
         column_kernel,
-        grid=(tiles,),
         out_shape=jax.ShapeDtypeStruct((width, G), F32),
-        in_specs=[whole(o.shape) for o in operands] + [table_spec, table_spec],
+        in_specs=[vmem] * len(operands) + [pl.BlockSpec(memory_space=pl.ANY)],
         out_specs=pl.BlockSpec(memory_space=pl.ANY),
         scratch_shapes=[
             pltpu.VMEM((2, width // LANES, nr * LANES, LANES), F32),
@@ -761,12 +765,15 @@
             pltpu.VMEM((half, width, 4 * keys.size), BF16),
             pltpu.VMEM((width, 2 * LANES), F32),
             pltpu.VMEM((half, width, 2 * LANES), F32),
+            pltpu.VMEM((half, width, 2 * LANES), F32),
             pltpu.VMEM((2, CLASSES, width, LANES), F32),
+            pltpu.VMEM(tables.shape, BF16),
             pltpu.SemaphoreType.DMA((2, CLASSES)),
+            pltpu.SemaphoreType.DMA((tables.shape[0],)),
         ],
         compiler_params=pltpu.CompilerParams(vmem_limit_bytes=56 * 2**20),
         name="columns",
-    )(*operands, jnp.asarray(fh), jnp.asarray(fl))
+    )(*operands, jnp.asarray(tables))
     return out.reshape(NSCALE, cols_here, G)
 
 

time: 113 us -> 103 us (0.912)
  waiting for transfers between devices: 43.4 us -> 26.8 us
  Pallas kernels: 45.3 us -> 54.2 us
  local copies, waits for them, and re-layouts: 11.1 us -> 7.13 us
  other arithmetic: 1.42 us -> 2.67 us
    ppermute x3, waiting for transfers between devices: 20.6 us -> 3.9 us  [kernel_device(): packs = [packed] + [lax.ppermute(packed, 'col', s) for s in shifts]]
    pallas_call x2 -> x5, Pallas kernels: 25.3 us -> 34.1 us  [the longest x1 22.8 us: kernel_device(): pl.pallas_call(column_kernel, out_shape=jax.ShapeDtypeStruct((width, G),...]
    unnamed x31 -> x23, local copies, waits for them, and re-layouts: 9.93 us -> 4.96 us
  transfers between devices with their start and end apart: 4 -> 4, of which waited for: 3 -> 2; matrix products, arithmetic and copies ran while one was open for 2% -> 2% of each run, Pallas kernels for 3% -> 9%
where the time goes in v3:
time: 103 us; the launch traced here: 102 us
  Pallas kernels  54.2 us (53%)
  waiting for transfers between devices  26.8 us (26%)
  starting transfers between devices  10.1 us (10%)
  local copies, waits for them, and re-layouts  7.13 us (7%)
  other arithmetic  2.67 us (3%)
    all_to_all x1, waiting for transfers between devices, kernel_device(): rows = lax.all_to_all(rows, 'row', split_axis=0, concat_axis=0, tiled=True)  22.9 us
    pallas_call x1, Pallas kernels, kernel_device(): pl.pallas_call(column_kernel, out_shape=jax.ShapeDtypeStruct((width, G),...  22.8 us
    pallas_call x1, Pallas kernels, kernel_device(): pl.pallas_call(lambda *refs: row_kernel(*refs, blocks=nc, part=part, per_...  17 us
    pallas_call x4, Pallas kernels, grid_block(): pl.pallas_call(subgrid_kernel, out_shape=jax.ShapeDtypeStruct((subs // 2...  11.3 us
    ppermute x3, starting transfers between devices, kernel_device(): packs = [packed] + [lax.ppermute(packed, 'col', s) for s in shifts]  6.11 us
    unnamed x23, local copies, waits for them, and re-layouts  4.96 us
    all_to_all x1, starting transfers between devices, kernel_device(): rows = lax.all_to_all(rows, 'row', split_axis=0, concat_axis=0, tiled=True)  3.94 us
    ppermute x3, waiting for transfers between devices, kernel_device(): packs = [packed] + [lax.ppermute(packed, 'col', s) for s in shifts]  3.9 us
  transfers between devices with their start and end apart: 4, of which 2 were waited for; matrix products, arithmetic and copies ran while one was open for 2% of the time, Pallas kernels for 9%

profile of v3, /device:TPU:0, one launch (start us, length us, event | category | flops | bytes accessed | tf_op | source)
XLA Modules:
  0.0 101.7 jit_solution(8127913707051485987)
XLA Ops:
  0.0 0.0 copy-start.7
  0.0 0.8 add_convert_fusion
  0.8 0.9 convert_element_type.14
  1.7 1.0 fusion.4
  2.6 0.9 multiply_add_fusion
  3.5 0.1 maximum_maximum_fusion.packed_ref
  3.7 5.1 %collective-permute-start.2 = (f32[4,8320]{1,0:T(4,128)S(1)}, f32[4,8320]{1,0:T(4,128)S(1)}, u32[]{:S(2)}, u32[]{:S(2)}) collective-permute-start(f32[4,8320]{1,0:T(4,128)S(1)} %maximum_maximum_fusion.packed_ref), channel_id=1, source_target_pairs={{0,3},{1,0},{2,1},{3,2},{4,7},{5,4},{6,5},{7,6},{8,11},{9,8},{10,9... | collective-permute-start | bytes 399368 | tf_op jit(solution)/shard_map/ppermute | solution.py:637
  8.8 0.0 collective-permute-start.1
  8.8 1.0 collective-permute-start
  9.8 1.1 %dynamic-slice_bitcast_fusion.refs_5_ = f32[1024,16]{1,0:T(8,128)S(1)} fusion(f32[4,1024,16]{2,1,0:T(8,128)} %constant.46.clone, s32[]{:T(128)S(6)} %select_n.4), kind=kLoop, calls=%fused_computation.1 | loop fusion | bytes 131076 | tf_op jit(solution)/shard_map/jit(dynamic_index_in_dim)/squeeze | solution.py:667
  10.9 0.0 copy-start.6
  10.9 0.7 copy-done.6
  11.5 2.8 %subgrids.5.refs_1_ = f32[512,128]{1,0:T(8,128)S(1)} custom-call(f32[4,8320]{1,0:T(4,128)S(1)} %maximum_maximum_fusion.packed_ref, f32[8,8]{1,0:T(8,128)S(1)} %copy-done.6), custom_call_target="tpu_custom_call" | custom-call | flops 536870912 | bytes 2097152 | tf_op jit(solution)/shard_map/subgrids/pallas_call | solution.py:640
  14.4 3.9 %collective-permute-done.packed_ref = f32[4,8320]{1,0:T(4,128)S(1)} collective-permute-done((f32[4,8320]{1,0:T(4,128)S(1)}, f32[4,8320]{1,0:T(4,128)S(1)}, u32[]{:S(2)}, u32[]{:S(2)}) %collective-permute-start) | collective-permute-done | bytes 133152 | tf_op jit(solution)/shard_map/ppermute | solution.py:637
  18.3 0.0 copy-done.7
  18.3 2.8 %subgrids.4.refs_2_ = f32[512,128]{1,0:T(8,128)S(1)} custom-call(f32[4,8320]{1,0:T(4,128)S(1)} %collective-permute-done.packed_ref, f32[8,8]{1,0:T(8,128)S(1)} %copy-done.7), custom_call_target="tpu_custom_call" | custom-call | flops 536870912 | bytes 2097152 | tf_op jit(solution)/shard_map/subgrids/pallas_call | solution.py:640
  21.1 0.0 collective-permute-done.2.packed_ref
  21.1 0.0 collective-permute-done.1.packed_ref
  21.2 2.8 %subgrids.7.refs_4_ = f32[512,128]{1,0:T(8,128)S(1)} custom-call(f32[4,8320]{1,0:T(4,128)S(1)} %collective-permute-done.2.packed_ref, f32[8,8]{1,0:T(8,128)S(1)} %copy-done.7), custom_call_target="tpu_custom_call" | custom-call | flops 536870912 | bytes 2097152 | tf_op jit(solution)/shard_map/subgrids/pallas_call | solution.py:640
  24.0 2.8 %subgrids.6.refs_3_ = f32[512,128]{1,0:T(8,128)S(1)} custom-call(f32[4,8320]{1,0:T(4,128)S(1)} %collective-permute-done.1.packed_ref, f32[8,8]{1,0:T(8,128)S(1)} %copy-done.7), custom_call_target="tpu_custom_call" | custom-call | flops 536870912 | bytes 2097152 | tf_op jit(solution)/shard_map/subgrids/pallas_call | solution.py:640
  26.9 17.0 %rows.1 = f32[8,288,256]{2,1,0:T(8,128)} custom-call(f32[4,128]{1,0:T(4,128)S(1)} %pad_maximum_fusion.refs_0_, f32[512,128]{1,0:T(8,128)S(1)} %subgrids.5.refs_1_, f32[512,128]{1,0:T(8,128)S(1)} %subgrids.4.refs_2_, f32[512,128]{1,0:T(8,128)S(1)} %subgrids.6.refs_3_, f32[512,128]{1,0:T(8,128)S(1)} %subgrids.7.refs_4_, ...), custom_call_target="tpu_custom_call" | custom-call | tf_op jit(solution)/shard_map/rows/pallas_call | solution.py:669
  43.9 0.0 copy-start.5
  43.9 0.0 copy-start.9
  43.9 0.0 copy-start.10
  44.0 0.0 copy-start.1
  44.0 0.0 copy-start.4
  44.0 3.9 %all-to-all-start = ((f32[8,288,256]{2,1,0:T(8,128)}), f32[8,288,256]{2,1,0:T(8,128)S(1)}, u32[]{:S(2)}, u32[]{:S(2)}) async-start(f32[8,288,256]{2,1,0:T(8,128)} %rows.1), calls=%async_computation | async-start | bytes 4718592 | tf_op jit(solution)/shard_map/all_to_all | solution.py:690
  47.9 0.0 copy-done.5
  47.9 0.0 copy-done.9
  48.0 0.5 convolution_bitcast_fusion
  48.4 0.6 copy.17
  49.1 0.0 copy-done.10
  49.1 0.1 broadcast_in_dim.11.inside_ref
  49.2 0.0 copy-done.1
  49.2 0.0 copy-done.4
  49.2 3.0 %bands.1 = (bf16[864,512]{1,0:T(8,128)(2,1)S(1)}, bf16[128,512]{1,0:T(8,128)(2,1)S(1)}, bf16[128,512]{1,0:T(8,128)(2,1)S(1)}) custom-call(f32[2,33]{1,0:T(2,128)S(1)} %copy-done.5, s32[288,256]{1,0:T(8,128)S(1)} %copy-done.1, s32[128,256]{1,0:T(8,128)S(1)} %copy-done.4, f32[288,1]{1,0:T(8,128)S(1)} %broadcast_in_dim.11.inside_ref), custom_call_target="tpu_custom_call" | custom-call | tf_op jit(solution)/shard_map/bands/pallas_call | solution.py:703
  52.2 0.0 copy-start
  52.2 0.9 copy-done
  53.1 0.0 copy-start.2
  53.1 0.6 copy-done.2
  53.8 0.0 copy-start.3
  53.8 0.6 copy-done.3
  54.4 22.9 %all-to-all-done.rows_ref = f32[8,288,256]{2,1,0:T(8,128)S(1)} async-done(((f32[8,288,256]{2,1,0:T(8,128)}), f32[8,288,256]{2,1,0:T(8,128)S(1)}, u32[]{:S(2)}, u32[]{:S(2)}) %all-to-all-start) | async-done | bytes 2359328 | tf_op jit(solution)/shard_map/all_to_all | solution.py:690
  77.3 0.0 copy-start.8
  77.3 1.4 %copy-done.8 = f32[8,288,256]{2,1,0:T(8,128)} copy-done((f32[8,288,256]{2,1,0:T(8,128)}, f32[8,288,256]{2,1,0:T(8,128)S(1)}, u32[]{:S(2)}) %copy-start.8) | copy-done | bytes 2359320
  78.7 22.8 %columns.1 = f32[512,8192]{1,0:T(8,128)} custom-call(f32[8,288,256]{2,1,0:T(8,128)} %copy-done.8, bf16[864,512]{1,0:T(8,128)(2,1)} %copy-done, f32[2,2,16,128]{3,2,1,0:T(8,128)} %bitcast.22, bf16[128,512]{1,0:T(8,128)(2,1)} %copy-done.2, bf16[128,512]{1,0:T(8,128)(2,1)} %copy-done.3, bf16[5,2,8,256,256]{4,3,2,1,0:T(8,128)(2,1)} %constant.52.clone.tables_ref), custom_call_target="tpu_custom_call" | custom-call | tf_op jit(solution)/shard_map/columns/pallas_call | solution.py:757
  (7 shorter events, 0.0 us)
Async XLA Ops:
  0.0 18.3 %copy-start.7 = (f32[8,8]{1,0:T(8,128)S(1)}, f32[8,8]{1,0:T(8,128)}, u32[]{:S(2)}) copy-start(f32[8,8]{1,0:T(8,128)} %taps_ref.8) | copy-start | bytes 772
  3.7 17.5 %collective-permute-start.2 = (f32[4,8320]{1,0:T(4,128)S(1)}, f32[4,8320]{1,0:T(4,128)S(1)}, u32[]{:S(2)}, u32[]{:S(2)}) collective-permute-start(f32[4,8320]{1,0:T(4,128)S(1)} %maximum_maximum_fusion.packed_ref), channel_id=1, source_target_pairs={{0,3},{1,0},{2,1},{3,2},{4,7},{5,4},{6,5},{7,6},{8,11},{9,8},{10,9... | collective-permute-start | bytes 399368 | tf_op jit(solution)/shard_map/ppermute | solution.py:637
  8.8 12.4 %collective-permute-start.1 = (f32[4,8320]{1,0:T(4,128)S(1)}, f32[4,8320]{1,0:T(4,128)S(1)}, u32[]{:S(2)}, u32[]{:S(2)}) collective-permute-start(f32[4,8320]{1,0:T(4,128)S(1)} %maximum_maximum_fusion.packed_ref), channel_id=1, source_target_pairs={{0,2},{1,3},{2,0},{3,1},{4,6},{5,7},{6,4},{7,5},{8,10},{9,11},{10,... | collective-permute-start | bytes 399368 | tf_op jit(solution)/shard_map/ppermute | solution.py:637
  8.8 9.5 %collective-permute-start = (f32[4,8320]{1,0:T(4,128)S(1)}, f32[4,8320]{1,0:T(4,128)S(1)}, u32[]{:S(2)}, u32[]{:S(2)}) collective-permute-start(f32[4,8320]{1,0:T(4,128)S(1)} %maximum_maximum_fusion.packed_ref), channel_id=1, source_target_pairs={{0,1},{1,2},{2,3},{3,0},{4,5},{5,6},{6,7},{7,4},{8,9},{9,10},{10,1... | collective-permute-start | bytes 399368 | tf_op jit(solution)/shard_map/ppermute | solution.py:637
  10.9 0.7 copy-start.6
  43.9 4.0 %copy-start.5 = (f32[2,33]{1,0:T(2,128)S(1)}, f32[2,33]{1,0:T(2,128)}, u32[]{:S(2)}) copy-start(f32[2,33]{1,0:T(2,128)} %taps_ref.9) | copy-start | bytes 796
  43.9 4.0 %copy-start.9 = (f32[33,4096]{1,0:T(8,128)S(1)}, f32[33,4096]{1,0:T(8,128)}, u32[]{:S(2)}) copy-start(f32[33,4096]{1,0:T(8,128)} %constant.51.clone) | copy-start | bytes 1622020
  43.9 5.1 %copy-start.10 = (s32[288]{0:T(512)S(1)}, s32[288]{0:T(512)}, u32[]{:S(2)}) copy-start(s32[288]{0:T(512)} %constant.48.clone) | copy-start | bytes 3460
  44.0 5.2 %copy-start.1 = (s32[288,256]{1,0:T(8,128)S(1)}, s32[288,256]{1,0:T(8,128)}, u32[]{:S(2)}) copy-start(s32[288,256]{1,0:T(8,128)} %constant.49.clone.across_ref) | copy-start | bytes 884740
  44.0 5.2 %copy-start.4 = (s32[128,256]{1,0:T(8,128)S(1)}, s32[128,256]{1,0:T(8,128)}, u32[]{:S(2)}) copy-start(s32[128,256]{1,0:T(8,128)} %constant.50.clone.wrap_ref) | copy-start | bytes 393220
  44.0 33.3 %all-to-all-start = ((f32[8,288,256]{2,1,0:T(8,128)}), f32[8,288,256]{2,1,0:T(8,128)S(1)}, u32[]{:S(2)}, u32[]{:S(2)}) async-start(f32[8,288,256]{2,1,0:T(8,128)} %rows.1), calls=%async_computation | async-start | bytes 4718592 | tf_op jit(solution)/shard_map/all_to_all | solution.py:690
  52.2 0.9 copy-start
  53.1 0.6 copy-start.2
  53.8 0.6 copy-start.3
  77.3 1.4 %copy-start.8 = (f32[8,288,256]{2,1,0:T(8,128)}, f32[8,288,256]{2,1,0:T(8,128)S(1)}, u32[]{:S(2)}) copy-start(f32[8,288,256]{2,1,0:T(8,128)S(1)} %all-to-all-done.rows_ref) | copy-start | bytes 7077892

commit v4 on v3

--- a/solution.py
+++ b/solution.py
@@ -389,7 +389,9 @@
 
 def row_kernel(info_ref, *refs, blocks, part, per_class, tile_width):
     xs = refs[:blocks]
-    turn_ref, tables_ref, out_ref, real_ref, imag_ref, uh_ref, ul_ref, both_ref, sem = refs[blocks:]
+    turn_ref, tables_ref = refs[blocks : blocks + 2]
+    outs = refs[blocks + 2 : -6]
+    real_ref, imag_ref, uh_ref, ul_ref, both_ref, sem = refs[-6:]
     fetch = pltpu.make_async_copy(tables_ref, both_ref, sem)
     fetch.start()
     rows = real_ref.shape[0]
@@ -440,18 +442,17 @@
         return carry
 
     lax.fori_loop(0, part // step, classes, 0, unroll=4)
-    dests = out_ref.shape[0]
-    half = dests * per_class
+    half = len(outs) * per_class
     fetch.wait()
     for c in range(RADIX):
         total = dot3(both_ref[0], both_ref[1], uh_ref[c], ul_ref[c])
         real = total[:half, :LANES] - total[half:, LANES:]
         imag = total[:half, LANES:] + total[half:, :LANES]
-        for d in range(dests):
+        here = slice(c * per_class, (c + 1) * per_class)
+        for d, out_ref in enumerate(outs):
             mine = slice(d * per_class, (d + 1) * per_class)
-            here = slice(c * per_class, (c + 1) * per_class)
-            out_ref[d, here, :LANES] = real[mine]
-            out_ref[d, here, LANES:] = imag[mine]
+            out_ref[here, :LANES] = real[mine]
+            out_ref[here, LANES:] = imag[mine]
 
 
 def band_kernel(taps_ref, across_ref, wrap_ref, inside_ref, out_ref, th_ref, tl_ref):
@@ -506,9 +507,12 @@
 
 
 def column_kernel(
-    rows_ref, across_ref, hat_ref, th_ref, tl_ref, tables_ref,
-    out_ref, qt_ref, qh_ref, ql_ref, corr_ref, va_ref, vb_ref, o_ref, f_ref, sem, table_sem,
+    row_ref, *refs,
 ):
+    *parts, across_ref, hat_ref, th_ref, tl_ref, tables_ref = refs[:-11]
+    out_ref, qt_ref, qh_ref, ql_ref, corr_ref, va_ref, vb_ref, o_ref, f_ref, sem, table_sem = refs[
+        -11:
+    ]
     tiles = tables_ref.shape[0] - 1
     fetches = [
         pltpu.make_async_copy(tables_ref.at[n], f_ref.at[n], table_sem.at[n])
@@ -516,19 +520,21 @@
     ]
     for fetch in fetches:
         fetch.start()
-    bands = rows_ref.shape[0]
+    bands = len(parts)
     width = qh_ref.shape[1]
     per_scale = width // NSCALE
     keys = LANES // 2
     half = CLASSES // 2
 
-    for i in range(bands):
-        high, low = split(rows_ref[i])
+    for d, part in enumerate(parts):
+        band = lax.rem(row_ref[0, 0] + (bands - d), bands)
+        here = pl.ds(pl.multiple_of(band * LANES, LANES), LANES)
+        high, low = split(part[...])
         product = dot(jnp.concatenate([high, low, high], axis=0), across_ref[...], 0, 0)
         for lane in range(width // LANES):
             cols = slice(lane * LANES, (lane + 1) * LANES)
-            qt_ref[0, lane, i * LANES : (i + 1) * LANES, :] = product[:LANES, cols]
-            qt_ref[1, lane, i * LANES : (i + 1) * LANES, :] = product[LANES:, cols]
+            qt_ref[0, lane, here, :] = product[:LANES, cols]
+            qt_ref[1, lane, here, :] = product[LANES:, cols]
     edge = jnp.zeros((width, LANES), F32)
     fetches[0].wait()
     for slot in range(half):
@@ -661,20 +667,20 @@
         G,
     )
     tables = np.stack(split_table(np.concatenate([cosine, sine], axis=0)))
-    first_q = np.arange(nc)[:, None, None] * cols_here - HALO
+    first_q = (np.arange(nr)[:, None] * stride + np.arange(nc) * cols_here).reshape(-1, 1, 1) - HALO
     cosine, sine = turn((first_q + np.arange(RADIX)) * inner[None, :, None], G)
     turns = np.concatenate([cosine, sine], axis=2).astype(np.float32)
-    turns = lax.dynamic_index_in_dim(jnp.asarray(turns), col, 0, keepdims=False)
+    turns = lax.dynamic_index_in_dim(jnp.asarray(turns), row * nc + col, 0, keepdims=False)
     vmem = pl.BlockSpec(memory_space=pltpu.VMEM)
     rows = pl.pallas_call(
         lambda *refs: row_kernel(
             *refs, blocks=nc, part=part, per_class=per_class, tile_width=tile_width
         ),
-        out_shape=jax.ShapeDtypeStruct((nr, window, 2 * LANES), F32),
+        out_shape=[jax.ShapeDtypeStruct((window, 2 * LANES), F32)] * nr,
         in_specs=[pl.BlockSpec(memory_space=pltpu.SMEM)]
         + [vmem] * (nc + 1)
         + [pl.BlockSpec(memory_space=pl.ANY)],
-        out_specs=vmem,
+        out_specs=[vmem] * nr,
         scratch_shapes=[
             pltpu.VMEM((G, LANES), F32),
             pltpu.VMEM((G, LANES), F32),
@@ -687,7 +693,9 @@
         name="rows",
     )(infos, *blocks, turns, jnp.asarray(tables))
 
-    rows = lax.all_to_all(rows, "row", split_axis=0, concat_axis=0, tiled=True)
+    rows = [rows[0]] + [
+        lax.ppermute(rows[d], "row", [(i, (i + d) % nr) for i in range(nr)]) for d in range(1, nr)
+    ]
 
     place = (RADIX * np.arange(per_class)[None, :] + np.arange(RADIX)[:, None]).reshape(-1)
     distance = place[:, None] - np.arange(cols_here)[None, :]
@@ -753,11 +761,13 @@
     table = np.stack(table).reshape(half, 4 * keys.size, 2, tiles, LANES)
     table = table.transpose(3, 0, 1, 2, 4).reshape(tiles, half, 4 * keys.size, 2 * LANES)
     tables = np.stack(split_table(np.concatenate([edge[None], table], axis=0)), axis=1)
-    operands = (rows, across, hat, th, tl)
+    operands = (*rows, across, hat, th, tl)
     out = pl.pallas_call(
         column_kernel,
         out_shape=jax.ShapeDtypeStruct((width, G), F32),
-        in_specs=[vmem] * len(operands) + [pl.BlockSpec(memory_space=pl.ANY)],
+        in_specs=[pl.BlockSpec(memory_space=pltpu.SMEM)]
+        + [vmem] * len(operands)
+        + [pl.BlockSpec(memory_space=pl.ANY)],
         out_specs=pl.BlockSpec(memory_space=pl.ANY),
         scratch_shapes=[
             pltpu.VMEM((2, width // LANES, nr * LANES, LANES), F32),
@@ -773,7 +783,7 @@
         ],
         compiler_params=pltpu.CompilerParams(vmem_limit_bytes=56 * 2**20),
         name="columns",
-    )(*operands, jnp.asarray(tables))
+    )(row.astype(jnp.int32).reshape(1, 1), *operands, jnp.asarray(tables))
     return out.reshape(NSCALE, cols_here, G)
 
 

time: 103 us -> 99.2 us (0.963)
  the two profiles are of different devices: /device:TPU:0 before, /device:TPU:19 now
where the time goes in v4:
time: 99.2 us; the launch traced here: 98.7 us
  Pallas kernels  52.7 us (53%)
  waiting for transfers between devices  19.9 us (20%)
  local copies, waits for them, and re-layouts  11.1 us (11%)
  starting transfers between devices  9.49 us (10%)
  other arithmetic  3.33 us (3%)
  matrix products  1.68 us (2%)
    pallas_call x1, Pallas kernels, kernel_device(): pl.pallas_call(column_kernel, out_shape=jax.ShapeDtypeStruct((width, G),...  22.7 us
    pallas_call x1, Pallas kernels, kernel_device(): pl.pallas_call(lambda *refs: row_kernel(*refs, blocks=nc, part=part, per_...  15.6 us
    ppermute x7, waiting for transfers between devices, kernel_device(): lax.ppermute(rows[d], 'row', [(i, (i + d) % nr) for i in range(nr)])  13.4 us
    pallas_call x4, Pallas kernels, grid_block(): pl.pallas_call(subgrid_kernel, out_shape=jax.ShapeDtypeStruct((subs // 2...  11.3 us
    unnamed x35, local copies, waits for them, and re-layouts  8.98 us
    ppermute x3, waiting for transfers between devices, kernel_device(): packs = [packed] + [lax.ppermute(packed, 'col', s) for s in shifts]  6.45 us
    ppermute x7, starting transfers between devices, kernel_device(): lax.ppermute(rows[d], 'row', [(i, (i + d) % nr) for i in range(nr)])  6.06 us
    ppermute x3, starting transfers between devices, kernel_device(): packs = [packed] + [lax.ppermute(packed, 'col', s) for s in shifts]  3.43 us
  transfers between devices with their start and end apart: 10, of which 4 were waited for; matrix products, arithmetic and copies ran while one was open for 4% of the time, Pallas kernels for 9%

profile of v4, /device:TPU:19, one launch (start us, length us, event | category | flops | bytes accessed | tf_op | source)
XLA Modules:
  0.0 98.7 jit_solution(4028118182122954678)
XLA Ops:
  0.0 0.8 add_convert_fusion
  0.8 0.9 convert_element_type.14
  1.6 1.0 fusion.4
  2.6 0.9 multiply_add_fusion
  3.5 0.1 maximum_maximum_fusion.packed_ref
  3.6 0.2 collective-permute-start.2
  3.9 3.2 %collective-permute-start.1 = (f32[4,8320]{1,0:T(4,128)S(1)}, f32[4,8320]{1,0:T(4,128)S(1)}, u32[]{:S(2)}, u32[]{:S(2)}) collective-permute-start(f32[4,8320]{1,0:T(4,128)S(1)} %maximum_maximum_fusion.packed_ref), channel_id=1, source_target_pairs={{0,2},{1,3},{2,0},{3,1},{4,6},{5,7},{6,4},{7,5},{8,10},{9,11},{10,... | collective-permute-start | bytes 399368 | tf_op jit(solution)/shard_map/ppermute | solution.py:643
  7.1 1.1 %dynamic-slice_bitcast_fusion.refs_5_ = f32[1024,16]{1,0:T(8,128)S(1)} fusion(f32[32,1024,16]{2,1,0:T(8,128)} %constant.47.clone, s32[]{:T(128)S(6)} %select_n.4), kind=kLoop, calls=%fused_computation.1 | loop fusion | bytes 131076 | tf_op jit(solution)/shard_map/jit(dynamic_index_in_dim)/squeeze | solution.py:673
  8.2 0.0 copy-start.7
  8.2 0.7 copy-done.7
  8.8 2.8 %subgrids.5.refs_1_ = f32[512,128]{1,0:T(8,128)S(1)} custom-call(f32[4,8320]{1,0:T(4,128)S(1)} %maximum_maximum_fusion.packed_ref, f32[8,8]{1,0:T(8,128)S(1)} %copy-done.7), custom_call_target="tpu_custom_call" | custom-call | flops 536870912 | bytes 2097152 | tf_op jit(solution)/shard_map/subgrids/pallas_call | solution.py:646
  11.7 6.4 %collective-permute-done.packed_ref = f32[4,8320]{1,0:T(4,128)S(1)} collective-permute-done((f32[4,8320]{1,0:T(4,128)S(1)}, f32[4,8320]{1,0:T(4,128)S(1)}, u32[]{:S(2)}, u32[]{:S(2)}) %collective-permute-start) | collective-permute-done | bytes 133152 | tf_op jit(solution)/shard_map/ppermute | solution.py:643
  18.1 0.7 copy-done.8
  18.8 2.8 %subgrids.4.refs_2_ = f32[512,128]{1,0:T(8,128)S(1)} custom-call(f32[4,8320]{1,0:T(4,128)S(1)} %collective-permute-done.packed_ref, f32[8,8]{1,0:T(8,128)S(1)} %copy-done.8), custom_call_target="tpu_custom_call" | custom-call | flops 536870912 | bytes 2097152 | tf_op jit(solution)/shard_map/subgrids/pallas_call | solution.py:646
  21.7 0.0 collective-permute-done.2.packed_ref
  21.7 2.8 %subgrids.7.refs_4_ = f32[512,128]{1,0:T(8,128)S(1)} custom-call(f32[4,8320]{1,0:T(4,128)S(1)} %collective-permute-done.2.packed_ref, f32[8,8]{1,0:T(8,128)S(1)} %copy-done.8), custom_call_target="tpu_custom_call" | custom-call | flops 536870912 | bytes 2097152 | tf_op jit(solution)/shard_map/subgrids/pallas_call | solution.py:646
  24.5 0.0 copy-start.9
  24.5 0.7 copy-done.9
  25.2 2.8 %subgrids.6.refs_3_ = f32[512,128]{1,0:T(8,128)S(1)} custom-call(f32[4,8320]{1,0:T(4,128)S(1)} %collective-permute-done.1.packed_ref, f32[8,8]{1,0:T(8,128)S(1)} %copy-done.9), custom_call_target="tpu_custom_call" | custom-call | flops 536870912 | bytes 2097152 | tf_op jit(solution)/shard_map/subgrids/pallas_call | solution.py:646
  28.1 15.6 %rows.1 = (f32[288,256]{1,0:T(8,128)S(1)}, f32[288,256]{1,0:T(8,128)S(1)}, f32[288,256]{1,0:T(8,128)S(1)}, f32[288,256]{1,0:T(8,128)S(1)}, f32[288,256]{1,0:T(8,...) custom-call(f32[4,128]{1,0:T(4,128)S(1)} %pad_maximum_fusion.refs_0_, ...), custom_call_target="tpu_custom_call" | custom-call | tf_op jit(solution)/shard_map/rows/pallas_call | solution.py:675
  43.8 0.7 copy-done.2
  44.5 2.4 %collective-permute-start.3 = (f32[288,256]{1,0:T(8,128)S(1)}, f32[288,256]{1,0:T(8,128)S(1)}, u32[]{:S(2)}, u32[]{:S(2)}) collective-permute-start(f32[288,256]{1,0:T(8,128)S(1)} %get-tuple-element.23), channel_id=1, source_target_pairs={{0,4},{4,8},{8,12},{12,16},{16,20},{20,24},{24,28},{28,0},{1,5},{5... | collective-permute-start | bytes 884744 | tf_op jit(solution)/shard_map/ppermute | solution.py:697
  46.8 1.2 %collective-permute-start.4 = (f32[288,256]{1,0:T(8,128)S(1)}, f32[288,256]{1,0:T(8,128)S(1)}, u32[]{:S(2)}, u32[]{:S(2)}) collective-permute-start(f32[288,256]{1,0:T(8,128)S(1)} %get-tuple-element.24), channel_id=1, source_target_pairs={{0,8},{4,12},{8,16},{12,20},{16,24},{20,28},{24,0},{28,4},{1,9},{5... | collective-permute-start | bytes 884744 | tf_op jit(solution)/shard_map/ppermute | solution.py:697
  48.0 0.6 collective-permute-start.6
  48.6 1.7 %collective-permute-start.7 = (f32[288,256]{1,0:T(8,128)S(1)}, f32[288,256]{1,0:T(8,128)S(1)}, u32[]{:S(2)}, u32[]{:S(2)}) collective-permute-start(f32[288,256]{1,0:T(8,128)S(1)} %get-tuple-element.27), channel_id=1, source_target_pairs={{0,20},{4,24},{8,28},{12,0},{16,4},{20,8},{24,12},{28,16},{1,21},{... | collective-permute-start | bytes 884744 | tf_op jit(solution)/shard_map/ppermute | solution.py:697
  50.3 2.9 %collective-permute-done.3.refs_1_ = f32[288,256]{1,0:T(8,128)S(1)} collective-permute-done((f32[288,256]{1,0:T(8,128)S(1)}, f32[288,256]{1,0:T(8,128)S(1)}, u32[]{:S(2)}, u32[]{:S(2)}) %collective-permute-start.3) | collective-permute-done | bytes 294944 | tf_op jit(solution)/shard_map/ppermute | solution.py:697
  53.2 0.2 collective-permute-start.8
  53.4 6.8 %collective-permute-done.4.refs_2_ = f32[288,256]{1,0:T(8,128)S(1)} collective-permute-done((f32[288,256]{1,0:T(8,128)S(1)}, f32[288,256]{1,0:T(8,128)S(1)}, u32[]{:S(2)}, u32[]{:S(2)}) %collective-permute-start.4) | collective-permute-done | bytes 294944 | tf_op jit(solution)/shard_map/ppermute | solution.py:697
  60.1 0.0 collective-permute-start.9
  60.1 1.7 %convolution_bitcast_fusion = f32[1,2,32,128]{3,1,2,0:T(2,128)S(1)} fusion(f32[33,4096]{1,0:T(8,128)} %constant.52.clone, f32[2,33]{1,0:T(2,128)} %taps_ref.9), kind=kOutput, calls=%fused_computation | convolution fusion | flops 3244032 | bytes 573704 | tf_op jit(solution)/shard_map/dot_general | solution.py:740
  61.8 0.6 copy.17
  62.4 0.7 fusion.3
  63.1 0.1 broadcast_in_dim.11.inside_ref
  63.2 0.0 copy-start.1
  63.2 1.0 copy-done.1
  64.2 0.9 copy-done.5
  65.1 0.7 copy-done.6
  65.8 3.0 %bands.1 = (bf16[864,512]{1,0:T(8,128)(2,1)S(1)}, bf16[128,512]{1,0:T(8,128)(2,1)S(1)}, bf16[128,512]{1,0:T(8,128)(2,1)S(1)}) custom-call(f32[2,33]{1,0:T(2,128)S(1)} %copy-done.6, s32[288,256]{1,0:T(8,128)S(1)} %copy-done.1, s32[128,256]{1,0:T(8,128)S(1)} %copy-done.5, f32[288,1]{1,0:T(8,128)S(1)} %broadcast_in_dim.11.inside_ref), custom_call_target="tpu_custom_call" | custom-call | tf_op jit(solution)/shard_map/bands/pallas_call | solution.py:711
  68.8 0.9 copy-done
  69.7 0.6 copy-done.3
  70.4 0.6 copy-done.4
  71.0 0.0 collective-permute-done.5.refs_3_
  71.0 0.0 collective-permute-done.6.refs_4_
  71.0 3.8 %collective-permute-done.7.refs_5_ = f32[288,256]{1,0:T(8,128)S(1)} collective-permute-done((f32[288,256]{1,0:T(8,128)S(1)}, f32[288,256]{1,0:T(8,128)S(1)}, u32[]{:S(2)}, u32[]{:S(2)}) %collective-permute-start.7) | collective-permute-done | bytes 294944 | tf_op jit(solution)/shard_map/ppermute | solution.py:697
  74.9 0.7 copy-done.14
  75.6 0.1 copy-done.15
  75.7 0.1 copy-done.16
  75.8 22.7 %columns.1 = f32[512,8192]{1,0:T(8,128)} custom-call(s32[1,1]{1,0:T(1,128)} %bitcast.row_ref, f32[288,256]{1,0:T(8,128)} %copy-done.2, f32[288,256]{1,0:T(8,128)} %copy-done.10, f32[288,256]{1,0:T(8,128)} %copy-done.11, f32[288,256]{1,0:T(8,128)} %copy-done.12, f32[288,256]{1,0:T(8,128)} %copy-done.13, f32[288,256]{1,0:T(8,128)} %copy-done.14, ...), custom_call_target="tpu_custom_call" | custom-call | tf_op jit(solution)/shard_map/columns/pallas_call | solution.py:765
  (29 shorter events, 0.1 us)
Async XLA Ops:
  3.6 18.0 %collective-permute-start.2 = (f32[4,8320]{1,0:T(4,128)S(1)}, f32[4,8320]{1,0:T(4,128)S(1)}, u32[]{:S(2)}, u32[]{:S(2)}) collective-permute-start(f32[4,8320]{1,0:T(4,128)S(1)} %maximum_maximum_fusion.packed_ref), channel_id=1, source_target_pairs={{0,3},{1,0},{2,1},{3,2},{4,7},{5,4},{6,5},{7,6},{8,11},{9,8},{10,9... | collective-permute-start | bytes 399368 | tf_op jit(solution)/shard_map/ppermute | solution.py:643
  3.9 17.8 %collective-permute-start.1 = (f32[4,8320]{1,0:T(4,128)S(1)}, f32[4,8320]{1,0:T(4,128)S(1)}, u32[]{:S(2)}, u32[]{:S(2)}) collective-permute-start(f32[4,8320]{1,0:T(4,128)S(1)} %maximum_maximum_fusion.packed_ref), channel_id=1, source_target_pairs={{0,2},{1,3},{2,0},{3,1},{4,6},{5,7},{6,4},{7,5},{8,10},{9,11},{10,... | collective-permute-start | bytes 399368 | tf_op jit(solution)/shard_map/ppermute | solution.py:643
  7.1 11.1 %collective-permute-start = (f32[4,8320]{1,0:T(4,128)S(1)}, f32[4,8320]{1,0:T(4,128)S(1)}, u32[]{:S(2)}, u32[]{:S(2)}) collective-permute-start(f32[4,8320]{1,0:T(4,128)S(1)} %maximum_maximum_fusion.packed_ref), channel_id=1, source_target_pairs={{0,1},{1,2},{2,3},{3,0},{4,5},{5,6},{6,7},{7,4},{8,9},{9,10},{10,1... | collective-permute-start | bytes 399368 | tf_op jit(solution)/shard_map/ppermute | solution.py:643
  8.2 0.7 copy-start.7
  18.1 0.7 copy-start.8
  24.5 0.7 copy-start.9
  43.7 0.7 copy-start.2
  44.5 8.7 %collective-permute-start.3 = (f32[288,256]{1,0:T(8,128)S(1)}, f32[288,256]{1,0:T(8,128)S(1)}, u32[]{:S(2)}, u32[]{:S(2)}) collective-permute-start(f32[288,256]{1,0:T(8,128)S(1)} %get-tuple-element.23), channel_id=1, source_target_pairs={{0,4},{4,8},{8,12},{12,16},{16,20},{20,24},{24,28},{28,0},{1,5},{5... | collective-permute-start | bytes 884744 | tf_op jit(solution)/shard_map/ppermute | solution.py:697
  46.8 13.3 %collective-permute-start.4 = (f32[288,256]{1,0:T(8,128)S(1)}, f32[288,256]{1,0:T(8,128)S(1)}, u32[]{:S(2)}, u32[]{:S(2)}) collective-permute-start(f32[288,256]{1,0:T(8,128)S(1)} %get-tuple-element.24), channel_id=1, source_target_pairs={{0,8},{4,12},{8,16},{12,20},{16,24},{20,28},{24,0},{28,4},{1,9},{5... | collective-permute-start | bytes 884744 | tf_op jit(solution)/shard_map/ppermute | solution.py:697
  48.0 23.0 %collective-permute-start.5 = (f32[288,256]{1,0:T(8,128)S(1)}, f32[288,256]{1,0:T(8,128)S(1)}, u32[]{:S(2)}, u32[]{:S(2)}) collective-permute-start(f32[288,256]{1,0:T(8,128)S(1)} %get-tuple-element.25), channel_id=1, source_target_pairs={{0,12},{4,16},{8,20},{12,24},{16,28},{20,0},{24,4},{28,8},{1,13},{... | collective-permute-start | bytes 884744 | tf_op jit(solution)/shard_map/ppermute | solution.py:697
  48.0 23.0 %collective-permute-start.6 = (f32[288,256]{1,0:T(8,128)S(1)}, f32[288,256]{1,0:T(8,128)S(1)}, u32[]{:S(2)}, u32[]{:S(2)}) collective-permute-start(f32[288,256]{1,0:T(8,128)S(1)} %get-tuple-element.26), channel_id=1, source_target_pairs={{0,16},{4,20},{8,24},{12,28},{16,0},{20,4},{24,8},{28,12},{1,17},{... | collective-permute-start | bytes 884744 | tf_op jit(solution)/shard_map/ppermute | solution.py:697
  48.6 26.2 %collective-permute-start.7 = (f32[288,256]{1,0:T(8,128)S(1)}, f32[288,256]{1,0:T(8,128)S(1)}, u32[]{:S(2)}, u32[]{:S(2)}) collective-permute-start(f32[288,256]{1,0:T(8,128)S(1)} %get-tuple-element.27), channel_id=1, source_target_pairs={{0,20},{4,24},{8,28},{12,0},{16,4},{20,8},{24,12},{28,16},{1,21},{... | collective-permute-start | bytes 884744 | tf_op jit(solution)/shard_map/ppermute | solution.py:697
  53.1 21.7 %copy-start.10 = (f32[288,256]{1,0:T(8,128)}, f32[288,256]{1,0:T(8,128)S(1)}, u32[]{:S(2)}) copy-start(f32[288,256]{1,0:T(8,128)S(1)} %collective-permute-done.3.refs_1_) | copy-start | bytes 884740
  53.2 21.7 %collective-permute-start.8 = (f32[288,256]{1,0:T(8,128)S(1)}, f32[288,256]{1,0:T(8,128)S(1)}, u32[]{:S(2)}, u32[]{:S(2)}) collective-permute-start(f32[288,256]{1,0:T(8,128)S(1)} %get-tuple-element.28), channel_id=1, source_target_pairs={{0,24},{4,28},{8,0},{12,4},{16,8},{20,12},{24,16},{28,20},{1,25},{... | collective-permute-start | bytes 884744 | tf_op jit(solution)/shard_map/ppermute | solution.py:697
  60.1 14.8 %copy-start.11 = (f32[288,256]{1,0:T(8,128)}, f32[288,256]{1,0:T(8,128)S(1)}, u32[]{:S(2)}) copy-start(f32[288,256]{1,0:T(8,128)S(1)} %collective-permute-done.4.refs_2_) | copy-start | bytes 884740
  60.1 14.7 %collective-permute-start.9 = (f32[288,256]{1,0:T(8,128)S(1)}, f32[288,256]{1,0:T(8,128)S(1)}, u32[]{:S(2)}, u32[]{:S(2)}) collective-permute-start(f32[288,256]{1,0:T(8,128)S(1)} %get-tuple-element.29), channel_id=1, source_target_pairs={{0,28},{4,0},{8,4},{12,8},{16,12},{20,16},{24,20},{28,24},{1,29},{... | collective-permute-start | bytes 884744 | tf_op jit(solution)/shard_map/ppermute | solution.py:697
  63.2 1.0 copy-start.1
  64.2 0.9 copy-start.5
  65.1 0.7 copy-start.6
  68.8 0.9 copy-start
  69.7 0.7 copy-start.3
  70.4 0.6 copy-start.4
  71.0 3.9 %copy-start.12 = (f32[288,256]{1,0:T(8,128)}, f32[288,256]{1,0:T(8,128)S(1)}, u32[]{:S(2)}) copy-start(f32[288,256]{1,0:T(8,128)S(1)} %collective-permute-done.5.refs_3_) | copy-start | bytes 884740
  71.0 3.9 %copy-start.13 = (f32[288,256]{1,0:T(8,128)}, f32[288,256]{1,0:T(8,128)S(1)}, u32[]{:S(2)}) copy-start(f32[288,256]{1,0:T(8,128)S(1)} %collective-permute-done.6.refs_4_) | copy-start | bytes 884740
  74.8 0.7 copy-start.14
  74.8 0.8 copy-start.15
  74.9 0.9 copy-start.16

commit v5 on v4

--- a/solution.py
+++ b/solution.py
@@ -781,7 +781,7 @@
             pltpu.SemaphoreType.DMA((2, CLASSES)),
             pltpu.SemaphoreType.DMA((tables.shape[0],)),
         ],
-        compiler_params=pltpu.CompilerParams(vmem_limit_bytes=56 * 2**20),
+        compiler_params=pltpu.CompilerParams(vmem_limit_bytes=52 * 2**20),
         name="columns",
     )(row.astype(jnp.int32).reshape(1, 1), *operands, jnp.asarray(tables))
     return out.reshape(NSCALE, cols_here, G)

time: 99.2 us -> 98.6 us (level)
  local copies, waits for them, and re-layouts: 11.1 us -> 8.4 us
  waiting for transfers between devices: 19.9 us -> 21.9 us
    unnamed x35 -> x17, local copies, waits for them, and re-layouts: 8.98 us -> 6.23 us
    ppermute x7, waiting for transfers between devices: 13.4 us -> 15.5 us  [kernel_device(): lax.ppermute(rows[d], 'row', [(i, (i + d) % nr) for i in range(nr)])]
where the time goes in v5:
time: 98.6 us; the launch traced here: 98 us
  Pallas kernels  52.9 us (54%)
  waiting for transfers between devices  21.9 us (22%)
  starting transfers between devices  9.55 us (10%)
  local copies, waits for them, and re-layouts  8.4 us (9%)
  other arithmetic  3.34 us (3%)
  matrix products  1.58 us (2%)
    pallas_call x1, Pallas kernels, kernel_device(): pl.pallas_call(column_kernel, out_shape=jax.ShapeDtypeStruct((width, G),...  22.3 us
    pallas_call x1, Pallas kernels, kernel_device(): pl.pallas_call(lambda *refs: row_kernel(*refs, blocks=nc, part=part, per_...  16.3 us
    ppermute x7, waiting for transfers between devices, kernel_device(): lax.ppermute(rows[d], 'row', [(i, (i + d) % nr) for i in range(nr)])  15.5 us
    pallas_call x4, Pallas kernels, grid_block(): pl.pallas_call(subgrid_kernel, out_shape=jax.ShapeDtypeStruct((subs // 2...  11.3 us
    ppermute x3, waiting for transfers between devices, kernel_device(): packs = [packed] + [lax.ppermute(packed, 'col', s) for s in shifts]  6.44 us
    unnamed x17, local copies, waits for them, and re-layouts  6.23 us
    ppermute x7, starting transfers between devices, kernel_device(): lax.ppermute(rows[d], 'row', [(i, (i + d) % nr) for i in range(nr)])  6.12 us
    ppermute x3, starting transfers between devices, kernel_device(): packs = [packed] + [lax.ppermute(packed, 'col', s) for s in shifts]  3.43 us
  transfers between devices with their start and end apart: 10, of which 4 were waited for; matrix products, arithmetic and copies ran while one was open for 4% of the time, Pallas kernels for 9%

profile of v5, /device:TPU:19, one launch (start us, length us, event | category | flops | bytes accessed | tf_op | source)
XLA Modules:
  0.0 98.0 jit_solution(4672629819779700392)
XLA Ops:
  0.0 0.8 add_convert_fusion
  0.8 0.9 convert_element_type.14
  1.6 1.0 fusion.4
  2.6 0.9 multiply_add_fusion
  3.5 0.1 maximum_maximum_fusion.packed_ref
  3.6 0.2 collective-permute-start.2
  3.9 3.2 %collective-permute-start.1 = (f32[4,8320]{1,0:T(4,128)S(1)}, f32[4,8320]{1,0:T(4,128)S(1)}, u32[]{:S(2)}, u32[]{:S(2)}) collective-permute-start(f32[4,8320]{1,0:T(4,128)S(1)} %maximum_maximum_fusion.packed_ref), channel_id=1, source_target_pairs={{0,2},{1,3},{2,0},{3,1},{4,6},{5,7},{6,4},{7,5},{8,10},{9,11},{10,... | collective-permute-start | bytes 399368 | tf_op jit(solution)/shard_map/ppermute | solution.py:643
  7.1 0.0 collective-permute-start
  7.1 1.1 %dynamic-slice_bitcast_fusion.refs_5_ = f32[1024,16]{1,0:T(8,128)S(1)} fusion(f32[32,1024,16]{2,1,0:T(8,128)} %constant.47.clone, s32[]{:T(128)S(6)} %select_n.4), kind=kLoop, calls=%fused_computation.1 | loop fusion | bytes 131076 | tf_op jit(solution)/shard_map/jit(dynamic_index_in_dim)/squeeze | solution.py:673
  8.2 0.0 copy-start.4
  8.2 0.7 copy-done.4
  8.8 2.8 %subgrids.5.refs_1_ = f32[512,128]{1,0:T(8,128)S(1)} custom-call(f32[4,8320]{1,0:T(4,128)S(1)} %maximum_maximum_fusion.packed_ref, f32[8,8]{1,0:T(8,128)S(1)} %copy-done.4), custom_call_target="tpu_custom_call" | custom-call | flops 536870912 | bytes 2097152 | tf_op jit(solution)/shard_map/subgrids/pallas_call | solution.py:646
  11.7 6.4 %collective-permute-done.packed_ref = f32[4,8320]{1,0:T(4,128)S(1)} collective-permute-done((f32[4,8320]{1,0:T(4,128)S(1)}, f32[4,8320]{1,0:T(4,128)S(1)}, u32[]{:S(2)}, u32[]{:S(2)}) %collective-permute-start) | collective-permute-done | bytes 133152 | tf_op jit(solution)/shard_map/ppermute | solution.py:643
  18.1 0.7 copy-done.5
  18.8 2.8 %subgrids.4.refs_2_ = f32[512,128]{1,0:T(8,128)S(1)} custom-call(f32[4,8320]{1,0:T(4,128)S(1)} %collective-permute-done.packed_ref, f32[8,8]{1,0:T(8,128)S(1)} %copy-done.5), custom_call_target="tpu_custom_call" | custom-call | flops 536870912 | bytes 2097152 | tf_op jit(solution)/shard_map/subgrids/pallas_call | solution.py:646
  21.7 0.0 collective-permute-done.2.packed_ref
  21.7 0.0 collective-permute-done.1.packed_ref
  21.7 2.8 %subgrids.7.refs_4_ = f32[512,128]{1,0:T(8,128)S(1)} custom-call(f32[4,8320]{1,0:T(4,128)S(1)} %collective-permute-done.2.packed_ref, f32[8,8]{1,0:T(8,128)S(1)} %copy-done.5), custom_call_target="tpu_custom_call" | custom-call | flops 536870912 | bytes 2097152 | tf_op jit(solution)/shard_map/subgrids/pallas_call | solution.py:646
  24.5 0.0 copy-start.6
  24.5 0.7 copy-done.6
  25.2 2.8 %subgrids.6.refs_3_ = f32[512,128]{1,0:T(8,128)S(1)} custom-call(f32[4,8320]{1,0:T(4,128)S(1)} %collective-permute-done.1.packed_ref, f32[8,8]{1,0:T(8,128)S(1)} %copy-done.6), custom_call_target="tpu_custom_call" | custom-call | flops 536870912 | bytes 2097152 | tf_op jit(solution)/shard_map/subgrids/pallas_call | solution.py:646
  28.1 16.3 %rows.1 = (f32[288,256]{1,0:T(8,128)S(1)}, f32[288,256]{1,0:T(8,128)}, f32[288,256]{1,0:T(8,128)S(1)}, f32[288,256]{1,0:T(8,128)S(1)}, f32[288,256]{1,0:T(8,128)...) custom-call(f32[4,128]{1,0:T(4,128)S(1)} %pad_maximum_fusion.refs_0_, ...), custom_call_target="tpu_custom_call" | custom-call | tf_op jit(solution)/shard_map/rows/pallas_call | solution.py:675
  44.4 2.4 %collective-permute-start.3 = (f32[288,256]{1,0:T(8,128)}, f32[288,256]{1,0:T(8,128)S(1)}, u32[]{:S(2)}, u32[]{:S(2)}) collective-permute-start(f32[288,256]{1,0:T(8,128)} %get-tuple-element.23), channel_id=1, source_target_pairs={{0,4},{4,8},{8,12},{12,16},{16,20},{20,24},{24,28},{28,0},{1,5},{5... | collective-permute-start | bytes 884744 | tf_op jit(solution)/shard_map/ppermute | solution.py:697
  46.8 1.2 %collective-permute-start.4 = (f32[288,256]{1,0:T(8,128)S(1)}, f32[288,256]{1,0:T(8,128)S(1)}, u32[]{:S(2)}, u32[]{:S(2)}) collective-permute-start(f32[288,256]{1,0:T(8,128)S(1)} %get-tuple-element.24), channel_id=1, source_target_pairs={{0,8},{4,12},{8,16},{12,20},{16,24},{20,28},{24,0},{28,4},{1,9},{5... | collective-permute-start | bytes 884744 | tf_op jit(solution)/shard_map/ppermute | solution.py:697
  48.0 0.0 collective-permute-start.5
  48.0 0.6 collective-permute-start.6
  48.6 1.7 %collective-permute-start.7 = (f32[288,256]{1,0:T(8,128)S(1)}, f32[288,256]{1,0:T(8,128)S(1)}, u32[]{:S(2)}, u32[]{:S(2)}) collective-permute-start(f32[288,256]{1,0:T(8,128)S(1)} %get-tuple-element.27), channel_id=1, source_target_pairs={{0,20},{4,24},{8,28},{12,0},{16,4},{20,8},{24,12},{28,16},{1,21},{... | collective-permute-start | bytes 884744 | tf_op jit(solution)/shard_map/ppermute | solution.py:697
  50.3 3.4 %collective-permute-done.3.refs_1_ = f32[288,256]{1,0:T(8,128)S(1)} collective-permute-done((f32[288,256]{1,0:T(8,128)}, f32[288,256]{1,0:T(8,128)S(1)}, u32[]{:S(2)}, u32[]{:S(2)}) %collective-permute-start.3) | collective-permute-done | bytes 294944 | tf_op jit(solution)/shard_map/ppermute | solution.py:697
  53.6 0.2 collective-permute-start.8
  53.9 6.7 %collective-permute-done.4.refs_2_ = f32[288,256]{1,0:T(8,128)S(1)} collective-permute-done((f32[288,256]{1,0:T(8,128)S(1)}, f32[288,256]{1,0:T(8,128)S(1)}, u32[]{:S(2)}, u32[]{:S(2)}) %collective-permute-start.4) | collective-permute-done | bytes 294944 | tf_op jit(solution)/shard_map/ppermute | solution.py:697
  60.5 0.0 collective-permute-start.9
  60.5 1.6 %convolution_bitcast_fusion = f32[1,2,32,128]{3,1,2,0:T(2,128)S(1)} fusion(f32[33,4096]{1,0:T(8,128)} %constant.52.clone, f32[2,33]{1,0:T(2,128)} %taps_ref.9), kind=kOutput, calls=%fused_computation | convolution fusion | flops 3244032 | bytes 573704 | tf_op jit(solution)/shard_map/dot_general | solution.py:740
  62.1 0.7 fusion.3
  62.8 0.1 broadcast_in_dim.11.inside_ref
  62.9 0.0 copy-start.1
  62.9 1.0 copy-done.1
  63.9 0.9 copy-done.2
  64.8 0.7 copy-done.3
  65.5 3.0 %bands.1 = (bf16[864,512]{1,0:T(8,128)(2,1)S(1)}, bf16[128,512]{1,0:T(8,128)(2,1)S(1)}, bf16[128,512]{1,0:T(8,128)(2,1)S(1)}) custom-call(f32[2,33]{1,0:T(2,128)S(1)} %copy-done.3, s32[288,256]{1,0:T(8,128)S(1)} %copy-done.1, s32[128,256]{1,0:T(8,128)S(1)} %copy-done.2, f32[288,1]{1,0:T(8,128)S(1)} %broadcast_in_dim.11.inside_ref), custom_call_target="tpu_custom_call" | custom-call | tf_op jit(solution)/shard_map/bands/pallas_call | solution.py:711
  68.5 0.0 copy-start
  68.5 0.9 copy-done
  69.4 0.0 collective-permute-done.5.refs_3_
  69.4 0.0 collective-permute-done.6.refs_4_
  69.4 5.4 %collective-permute-done.7.refs_5_ = f32[288,256]{1,0:T(8,128)S(1)} collective-permute-done((f32[288,256]{1,0:T(8,128)S(1)}, f32[288,256]{1,0:T(8,128)S(1)}, u32[]{:S(2)}, u32[]{:S(2)}) %collective-permute-start.7) | collective-permute-done | bytes 294944 | tf_op jit(solution)/shard_map/ppermute | solution.py:697
  74.9 0.0 collective-permute-done.8.refs_6_
  74.9 0.0 collective-permute-done.9.refs_7_
  74.9 0.7 copy-done.7
  75.6 22.3 %columns.1 = f32[512,8192]{1,0:T(8,128)} custom-call(s32[1,1]{1,0:T(1,128)} %bitcast.row_ref, f32[288,256]{1,0:T(8,128)S(1)} %get-tuple-element.22.refs_0_, f32[288,256]{1,0:T(8,128)S(1)} %collective-permute-done.3.refs_1_, f32[288,256]{1,0:T(8,128)S(1)} %collective-permute-done.4.refs_2_, f32[288,256]{1,0:T(8,128)S(1)} %collective-permute-done.5.refs_3_, ...), custom_call_target="tpu_custom_call" | custom-call | tf_op jit(solution)/shard_map/columns/pallas_call | solution.py:765
  (11 shorter events, 0.0 us)
Async XLA Ops:
  3.6 18.0 %collective-permute-start.2 = (f32[4,8320]{1,0:T(4,128)S(1)}, f32[4,8320]{1,0:T(4,128)S(1)}, u32[]{:S(2)}, u32[]{:S(2)}) collective-permute-start(f32[4,8320]{1,0:T(4,128)S(1)} %maximum_maximum_fusion.packed_ref), channel_id=1, source_target_pairs={{0,3},{1,0},{2,1},{3,2},{4,7},{5,4},{6,5},{7,6},{8,11},{9,8},{10,9... | collective-permute-start | bytes 399368 | tf_op jit(solution)/shard_map/ppermute | solution.py:643
  3.9 17.8 %collective-permute-start.1 = (f32[4,8320]{1,0:T(4,128)S(1)}, f32[4,8320]{1,0:T(4,128)S(1)}, u32[]{:S(2)}, u32[]{:S(2)}) collective-permute-start(f32[4,8320]{1,0:T(4,128)S(1)} %maximum_maximum_fusion.packed_ref), channel_id=1, source_target_pairs={{0,2},{1,3},{2,0},{3,1},{4,6},{5,7},{6,4},{7,5},{8,10},{9,11},{10,... | collective-permute-start | bytes 399368 | tf_op jit(solution)/shard_map/ppermute | solution.py:643
  7.1 11.1 %collective-permute-start = (f32[4,8320]{1,0:T(4,128)S(1)}, f32[4,8320]{1,0:T(4,128)S(1)}, u32[]{:S(2)}, u32[]{:S(2)}) collective-permute-start(f32[4,8320]{1,0:T(4,128)S(1)} %maximum_maximum_fusion.packed_ref), channel_id=1, source_target_pairs={{0,1},{1,2},{2,3},{3,0},{4,5},{5,6},{6,7},{7,4},{8,9},{9,10},{10,1... | collective-permute-start | bytes 399368 | tf_op jit(solution)/shard_map/ppermute | solution.py:643
  8.2 0.7 copy-start.4
  18.1 0.7 copy-start.5
  24.5 0.7 copy-start.6
  44.4 9.3 %collective-permute-start.3 = (f32[288,256]{1,0:T(8,128)}, f32[288,256]{1,0:T(8,128)S(1)}, u32[]{:S(2)}, u32[]{:S(2)}) collective-permute-start(f32[288,256]{1,0:T(8,128)} %get-tuple-element.23), channel_id=1, source_target_pairs={{0,4},{4,8},{8,12},{12,16},{16,20},{20,24},{24,28},{28,0},{1,5},{5... | collective-permute-start | bytes 884744 | tf_op jit(solution)/shard_map/ppermute | solution.py:697
  46.8 13.7 %collective-permute-start.4 = (f32[288,256]{1,0:T(8,128)S(1)}, f32[288,256]{1,0:T(8,128)S(1)}, u32[]{:S(2)}, u32[]{:S(2)}) collective-permute-start(f32[288,256]{1,0:T(8,128)S(1)} %get-tuple-element.24), channel_id=1, source_target_pairs={{0,8},{4,12},{8,16},{12,20},{16,24},{20,28},{24,0},{28,4},{1,9},{5... | collective-permute-start | bytes 884744 | tf_op jit(solution)/shard_map/ppermute | solution.py:697
  48.0 21.4 %collective-permute-start.5 = (f32[288,256]{1,0:T(8,128)S(1)}, f32[288,256]{1,0:T(8,128)S(1)}, u32[]{:S(2)}, u32[]{:S(2)}) collective-permute-start(f32[288,256]{1,0:T(8,128)S(1)} %get-tuple-element.25), channel_id=1, source_target_pairs={{0,12},{4,16},{8,20},{12,24},{16,28},{20,0},{24,4},{28,8},{1,13},{... | collective-permute-start | bytes 884744 | tf_op jit(solution)/shard_map/ppermute | solution.py:697
  48.0 21.4 %collective-permute-start.6 = (f32[288,256]{1,0:T(8,128)S(1)}, f32[288,256]{1,0:T(8,128)S(1)}, u32[]{:S(2)}, u32[]{:S(2)}) collective-permute-start(f32[288,256]{1,0:T(8,128)S(1)} %get-tuple-element.26), channel_id=1, source_target_pairs={{0,16},{4,20},{8,24},{12,28},{16,0},{20,4},{24,8},{28,12},{1,17},{... | collective-permute-start | bytes 884744 | tf_op jit(solution)/shard_map/ppermute | solution.py:697
  48.6 26.2 %collective-permute-start.7 = (f32[288,256]{1,0:T(8,128)S(1)}, f32[288,256]{1,0:T(8,128)S(1)}, u32[]{:S(2)}, u32[]{:S(2)}) collective-permute-start(f32[288,256]{1,0:T(8,128)S(1)} %get-tuple-element.27), channel_id=1, source_target_pairs={{0,20},{4,24},{8,28},{12,0},{16,4},{20,8},{24,12},{28,16},{1,21},{... | collective-permute-start | bytes 884744 | tf_op jit(solution)/shard_map/ppermute | solution.py:697
  53.6 21.2 %collective-permute-start.8 = (f32[288,256]{1,0:T(8,128)S(1)}, f32[288,256]{1,0:T(8,128)}, u32[]{:S(2)}, u32[]{:S(2)}) collective-permute-start(f32[288,256]{1,0:T(8,128)S(1)} %get-tuple-element.28), channel_id=1, source_target_pairs={{0,24},{4,28},{8,0},{12,4},{16,8},{20,12},{24,16},{28,20},{1,25},{... | collective-permute-start | bytes 884744 | tf_op jit(solution)/shard_map/ppermute | solution.py:697
  60.5 14.3 %collective-permute-start.9 = (f32[288,256]{1,0:T(8,128)S(1)}, f32[288,256]{1,0:T(8,128)}, u32[]{:S(2)}, u32[]{:S(2)}) collective-permute-start(f32[288,256]{1,0:T(8,128)S(1)} %get-tuple-element.29), channel_id=1, source_target_pairs={{0,28},{4,0},{8,4},{12,8},{16,12},{20,16},{24,20},{28,24},{1,29},{... | collective-permute-start | bytes 884744 | tf_op jit(solution)/shard_map/ppermute | solution.py:697
  62.9 1.0 copy-start.1
  63.9 0.9 copy-start.2
  64.8 0.7 copy-start.3
  68.5 0.9 copy-start
  74.9 0.7 copy-start.7
